TPU v7x, 32 devices: a whole 2x2x4 slice. The times are simulated.
32 devices in a mesh: dp: 8 (over y, x, core), rows: 4 (over z).
Axes of the slice: x: 2, y: 2, z: 4, core: 2. Of those that a mesh axis runs over, the one named last changes fastest.
Arguments:
- tokens: bfloat16 [16, 5, 32, 32, 512], P('dp', None, 'rows'), may hold values from -6 to 6
- video_flag: int32 [16], P('dp'), may hold values from 0 to 1, as said below
- frame_count: int32 [16], P('dp'), may hold values from 1 to 5, as said below
- norm_gain: float32 [4, 512], replicated, may hold values from 0.5 to 1.5
- norm_bias: float32 [4, 512], replicated, may hold values from -3 to 3
- w_qkv: bfloat16 [2, 512, 1536], replicated, may hold values from -0.25 to 0.25
- w_proj: bfloat16 [2, 512, 512], replicated, may hold values from -0.5 to 0.5
- w_up: bfloat16 [2, 512, 2048], replicated, may hold values from -0.25 to 0.25
- w_down: bfloat16 [2, 2048, 512], replicated, may hold values from -0.125 to 0.125
- out_bias: float32 [4, 512], replicated, may hold values from -3 to 3
- up_bias: float32 [2, 2048], replicated, may hold values from -3 to 3
- cotangent: bfloat16 [16, 5, 32, 32, 512], P('dp', None, 'rows'), may hold values from -6 to 6
Outputs:
- layer_out: bfloat16 [16, 5, 32, 32, 512], P('dp', None, 'rows')
- grad_tokens: bfloat16 [16, 5, 32, 32, 512], P('dp', None, 'rows')
- grad_norm_gain: float32 [4, 512], P(None, 'rows')
- grad_norm_bias: float32 [4, 512], P(None, 'rows')
- grad_qkv: float32 [2, 512, 1536], P(None, 'rows')
- grad_proj: float32 [2, 512, 512], P(None, 'rows')
- grad_up: float32 [2, 512, 2048], P(None, 'rows')
- grad_down: float32 [2, 2048, 512], P(None, 'rows')
- grad_out_bias: float32 [4, 512], P(None, 'rows')
- grad_up_bias: float32 [2, 2048], P(None, 'rows')
Inputs may be any that keep to these rules, and one draw needn't show every extreme that they name: `video_flag`: 1 marks a video, 0 an image; at least one item is a video. `frame_count`: valid frame slots of the item: 1 for every image, 1 to 5 for a video, exactly 5 for at least one video in every draw.
All inputs are finite; a program needn't handle non-finite values.
Results may differ from a plain program's by a relative error of at most 0.02.
Values may be sent and summed in bfloat16 or wider, within the bound.
No kernel may reach another device: no remote copies, remote signals or barrier semaphores. Data moves between devices by JAX's collectives and lax.ppermute only.
A program may use at most 448 MiB of HBM per device.

v0:
```python
import jax
import jax.numpy as jnp
from jax import lax
from jax.sharding import PartitionSpec as P

HEADS = 8
HEAD_DIM = 64
WIN = 8
SHIFT = 4


EPS = 1e-05
NEG = -1e30


def from_behind(block, axis, distance):
    devices = range(lax.axis_size(axis))
    route = [((i - distance) % len(devices), i) for i in devices]
    return lax.ppermute(block, axis, route)


def norm_apply(hidden, gain, bias):
    center = hidden - jnp.mean(hidden, axis=-1, keepdims=True)
    spread = jnp.mean(center * center, axis=-1, keepdims=True)
    return center * lax.rsqrt(spread + EPS) * gain + bias


def gelu_exact(pre_act):
    return jax.nn.gelu(pre_act, approximate=False)


def region_label(index, extent):
    return jnp.where(index < extent - WIN, 0, jnp.where(index < extent - SHIFT, 1, 2))


def tile_mask(grid_cols):
    height = lax.axis_size("rows") * WIN
    row_label = region_label(lax.axis_index("rows") * WIN + jnp.arange(WIN), height)
    col_label = region_label(jnp.arange(grid_cols), grid_cols).reshape(grid_cols // WIN, WIN)
    label = (row_label[None, :, None] * 3 + col_label[:, None, :]).reshape(
        grid_cols // WIN, WIN * WIN
    )
    return label[:, :, None] == label[:, None, :]


def into_shifted(layout):
    upper = from_behind(layout[:, :, :SHIFT], "rows", -1)
    joined = jnp.concatenate([layout[:, :, SHIFT:], upper], axis=2)
    return jnp.roll(joined, -SHIFT, axis=3)


def out_of_shifted(layout):
    rolled = jnp.roll(layout, SHIFT, axis=3)
    lower = from_behind(rolled[:, :, WIN - SHIFT :], "rows", 1)
    return jnp.concatenate([lower, rolled[:, :, : WIN - SHIFT]], axis=2)


def into_tiles(layout):
    count_items, frames, grid_rows, grid_cols, channels = layout.shape
    tile_rows = layout.reshape(count_items * frames, grid_rows, grid_cols // WIN, WIN, channels)
    tile_rows = tile_rows.transpose(0, 2, 1, 3, 4)
    return tile_rows.reshape(count_items * frames, grid_cols // WIN, grid_rows * WIN, channels)


def from_tiles(tile_rows, count_items):
    planes, windows, length, channels = tile_rows.shape
    layout = tile_rows.reshape(planes, windows, WIN, WIN, channels).transpose(0, 2, 1, 3, 4)
    return layout.reshape(count_items, planes // count_items, WIN, windows * WIN, channels)


def flat_rows(array):
    return array.reshape(-1, array.shape[-1])


def outer_sum(left, right):
    return lax.dot_general(
        flat_rows(left),
        flat_rows(right),
        (((0,), (0,)), ((), ())),
        preferred_element_type=jnp.float32,
    )


def back_dot(gradient, weight):
    return lax.dot_general(
        gradient,
        weight,
        (((gradient.ndim - 1,), (1,)), ((), ())),
        preferred_element_type=jnp.float32,
    )


def feed_forward(hidden, gain, bias, weight_up, weight_down, bias_up, bias_down):
    normed, norm_back = jax.vjp(norm_apply, hidden, gain, bias)
    normed_low = normed.astype(jnp.bfloat16)
    pre_act = jnp.dot(normed_low, weight_up, preferred_element_type=jnp.float32) + bias_up
    active, gelu_back = jax.vjp(gelu_exact, pre_act)
    active_low = active.astype(jnp.bfloat16)
    result = (
        hidden + jnp.dot(active_low, weight_down, preferred_element_type=jnp.float32) + bias_down
    )
    return (result, (norm_back, gelu_back, normed_low, active_low))


def feed_back(gradient, saved, weight_up, weight_down):
    norm_back, gelu_back, normed_low, active_low = saved
    grad_low = gradient.astype(jnp.bfloat16)
    grad_down = outer_sum(active_low, grad_low)
    grad_down_bias = jnp.sum(grad_low, axis=(0, 1, 2, 3), dtype=jnp.float32)
    (d_pre,) = gelu_back(back_dot(grad_low, weight_down))
    d_pre_low = d_pre.astype(jnp.bfloat16)
    grad_up = outer_sum(normed_low, d_pre_low)
    grad_up_bias = jnp.sum(d_pre_low, axis=(0, 1, 2, 3), dtype=jnp.float32)
    d_hidden, grad_gain, grad_bias = norm_back(back_dot(d_pre_low, weight_up))
    return (
        gradient + d_hidden,
        (grad_gain, grad_bias, grad_up, grad_down, grad_up_bias, grad_down_bias),
    )


def softmax_rows(scores):
    row_max = jnp.max(scores, axis=-1, keepdims=True)
    exponent = jnp.exp(scores - row_max)
    row_total = jnp.sum(exponent, axis=-1, keepdims=True)
    return (exponent / row_total, row_max + jnp.log(row_total))


def softmax_back(soft_w, d_weights):
    return (soft_w * (d_weights - jnp.sum(soft_w * d_weights, axis=-1, keepdims=True))).astype(
        jnp.bfloat16
    )


def on_device(
    tokens,
    video_flag,
    frame_count,
    norm_gain,
    norm_bias,
    w_qkv,
    w_proj,
    w_up,
    w_down,
    out_bias,
    up_bias,
    cotangent,
):
    count_items, frames, grid_rows, grid_cols, features = tokens.shape
    score_scale = HEAD_DIM ** (-0.5)
    length = WIN * WIN
    windows = grid_cols // WIN
    places = grid_rows * grid_cols
    planes = count_items * frames
    is_video = video_flag.astype(jnp.float32).reshape(count_items, 1, 1, 1, 1)
    is_valid = (
        (jnp.arange(frames)[None, :] < frame_count[:, None])
        .astype(jnp.float32)
        .reshape(count_items, frames, 1, 1, 1)
    )
    allowed = tile_mask(grid_cols)[:, None]
    causal = jnp.arange(frames)[:, None] >= jnp.arange(frames)[None, :]
    inputs = tokens.astype(jnp.float32)
    normed_zero, norm_zero_back = jax.vjp(norm_apply, inputs, norm_gain[0], norm_bias[0])
    normed_zero_low = normed_zero.astype(jnp.bfloat16)
    tile_rows = into_tiles(into_shifted(normed_zero_low))
    packed = jnp.dot(tile_rows, w_qkv[0], preferred_element_type=jnp.float32).astype(jnp.bfloat16)
    packed = packed.reshape(planes, windows, length, 3, HEADS, HEAD_DIM)
    queries, key_rows, values = (packed[:, :, :, 0], packed[:, :, :, 1], packed[:, :, :, 2])
    scores = (
        jnp.einsum("fwqhe,fwkhe->fwhqk", queries, key_rows, preferred_element_type=jnp.float32)
        * score_scale
    )
    soft_w, logsum = softmax_rows(jnp.where(allowed, scores, NEG))
    mixed_heads = jnp.einsum(
        "fwhqk,fwkhe->fwqhe",
        soft_w.astype(jnp.bfloat16),
        values,
        preferred_element_type=jnp.float32,
    )
    mixed_heads = mixed_heads.astype(jnp.bfloat16).reshape(planes, windows, length, features)
    mixed_grid = out_of_shifted(from_tiles(mixed_heads, count_items))
    after_space = (
        inputs + jnp.dot(mixed_grid, w_proj[0], preferred_element_type=jnp.float32) + out_bias[0]
    )
    after_mlp, saved_first = feed_forward(
        after_space, norm_gain[1], norm_bias[1], w_up[0], w_down[0], up_bias[0], out_bias[1]
    )
    normed_two, norm_two_back = jax.vjp(norm_apply, after_mlp, norm_gain[2], norm_bias[2])
    normed_two_low = normed_two.astype(jnp.bfloat16)
    packed_time = jnp.dot(normed_two_low, w_qkv[1], preferred_element_type=jnp.float32).astype(
        jnp.bfloat16
    )
    packed_time = packed_time.reshape(count_items, frames, places, 3, HEADS, HEAD_DIM)
    query_time, key_time, value_time = (
        packed_time[:, :, :, 0],
        packed_time[:, :, :, 1],
        packed_time[:, :, :, 2],
    )
    scores_time = (
        jnp.einsum("itphe,iuphe->iphtu", query_time, key_time, preferred_element_type=jnp.float32)
        * score_scale
    )
    soft_time, logsum_time = softmax_rows(jnp.where(causal, scores_time, NEG))
    soft_time_low = soft_time.astype(jnp.bfloat16)
    mixed_time = jnp.einsum(
        "iphtu,iuphe->itphe", soft_time_low, value_time, preferred_element_type=jnp.float32
    )
    mixed_time = mixed_time.astype(jnp.bfloat16).reshape(
        count_items, frames, grid_rows, grid_cols, features
    )
    after_time = after_mlp + is_video * (
        jnp.dot(mixed_time, w_proj[1], preferred_element_type=jnp.float32) + out_bias[2]
    )
    final_state, saved_second = feed_forward(
        after_time, norm_gain[3], norm_bias[3], w_up[1], w_down[1], up_bias[1], out_bias[3]
    )
    layer_out = (final_state * is_valid).astype(jnp.bfloat16)
    gradient = cotangent.astype(jnp.float32) * is_valid
    gradient, grads_second = feed_back(gradient, saved_second, w_up[1], w_down[1])
    d_attn_time = (is_video * gradient).astype(jnp.bfloat16)
    grad_proj_time = outer_sum(mixed_time, d_attn_time)
    grad_bias_time = jnp.sum(d_attn_time, axis=(0, 1, 2, 3), dtype=jnp.float32)
    d_mixed_time = (
        back_dot(d_attn_time, w_proj[1])
        .astype(jnp.bfloat16)
        .reshape(count_items, frames, places, HEADS, HEAD_DIM)
    )
    d_value_time = jnp.einsum(
        "iphtu,itphe->iuphe", soft_time_low, d_mixed_time, preferred_element_type=jnp.float32
    )
    d_soft_time = jnp.einsum(
        "itphe,iuphe->iphtu", d_mixed_time, value_time, preferred_element_type=jnp.float32
    )
    d_scores_time = softmax_back(soft_time, d_soft_time)
    d_query_time = (
        jnp.einsum(
            "iphtu,iuphe->itphe", d_scores_time, key_time, preferred_element_type=jnp.float32
        )
        * score_scale
    )
    d_key_time = (
        jnp.einsum(
            "iphtu,itphe->iuphe", d_scores_time, query_time, preferred_element_type=jnp.float32
        )
        * score_scale
    )
    d_packed_time = jnp.stack([d_query_time, d_key_time, d_value_time], axis=3).astype(jnp.bfloat16)
    d_packed_time = d_packed_time.reshape(count_items, frames, grid_rows, grid_cols, 3 * features)
    grad_qkv_time = outer_sum(normed_two_low, d_packed_time)
    d_after_mlp, grad_gain_two, grad_bias_two = norm_two_back(back_dot(d_packed_time, w_qkv[1]))
    gradient = gradient + d_after_mlp
    gradient, grads_first = feed_back(gradient, saved_first, w_up[0], w_down[0])
    d_attn = gradient.astype(jnp.bfloat16)
    grad_proj_space = outer_sum(mixed_grid, d_attn)
    grad_bias_space = jnp.sum(d_attn, axis=(0, 1, 2, 3), dtype=jnp.float32)
    d_mixed = back_dot(d_attn, w_proj[0]).astype(jnp.bfloat16)
    d_tiles = into_tiles(into_shifted(d_mixed)).reshape(planes, windows, length, HEADS, HEAD_DIM)
    scores = (
        jnp.einsum("fwqhe,fwkhe->fwhqk", queries, key_rows, preferred_element_type=jnp.float32)
        * score_scale
    )
    soft_w = jnp.exp(jnp.where(allowed, scores, NEG) - logsum)
    d_values = jnp.einsum(
        "fwhqk,fwqhe->fwkhe",
        soft_w.astype(jnp.bfloat16),
        d_tiles,
        preferred_element_type=jnp.float32,
    )
    d_soft = jnp.einsum("fwqhe,fwkhe->fwhqk", d_tiles, values, preferred_element_type=jnp.float32)
    d_scores = softmax_back(soft_w, d_soft)
    d_queries = (
        jnp.einsum("fwhqk,fwkhe->fwqhe", d_scores, key_rows, preferred_element_type=jnp.float32)
        * score_scale
    )
    d_keys = (
        jnp.einsum("fwhqk,fwqhe->fwkhe", d_scores, queries, preferred_element_type=jnp.float32)
        * score_scale
    )
    d_packed = jnp.stack([d_queries, d_keys, d_values], axis=3).astype(jnp.bfloat16)
    d_grid = out_of_shifted(
        from_tiles(d_packed.reshape(planes, windows, length, 3 * features), count_items)
    )
    grad_qkv_space = outer_sum(normed_zero_low, d_grid)
    d_inputs, grad_gain_zero, grad_bias_zero = norm_zero_back(back_dot(d_grid, w_qkv[0]))
    grad_tokens = (gradient + d_inputs).astype(jnp.bfloat16)
    gains = jnp.stack([grad_gain_zero, grads_first[0], grad_gain_two, grads_second[0]])
    biases = jnp.stack([grad_bias_zero, grads_first[1], grad_bias_two, grads_second[1]])
    qkv_all = jnp.stack([grad_qkv_space, grad_qkv_time])
    proj_all = jnp.stack([grad_proj_space, grad_proj_time])
    up_all = jnp.stack([grads_first[2], grads_second[2]])
    down_all = jnp.stack([grads_first[3], grads_second[3]])
    outer_all = jnp.stack([grad_bias_space, grads_first[5], grad_bias_time, grads_second[5]])
    upper_all = jnp.stack([grads_first[4], grads_second[4]])
    shares = (
        lax.psum_scatter(
            gains.astype(jnp.bfloat16), "rows", scatter_dimension=1, tiled=True
        ).astype(jnp.float32),
        lax.psum_scatter(
            biases.astype(jnp.bfloat16), "rows", scatter_dimension=1, tiled=True
        ).astype(jnp.float32),
        lax.psum_scatter(
            qkv_all.astype(jnp.bfloat16), "rows", scatter_dimension=1, tiled=True
        ).astype(jnp.float32),
        lax.psum_scatter(
            proj_all.astype(jnp.bfloat16), "rows", scatter_dimension=1, tiled=True
        ).astype(jnp.float32),
        lax.psum_scatter(
            up_all.astype(jnp.bfloat16), "rows", scatter_dimension=1, tiled=True
        ).astype(jnp.float32),
        lax.psum_scatter(
            down_all.astype(jnp.bfloat16), "rows", scatter_dimension=1, tiled=True
        ).astype(jnp.float32),
        lax.psum_scatter(
            outer_all.astype(jnp.bfloat16), "rows", scatter_dimension=1, tiled=True
        ).astype(jnp.float32),
        lax.psum_scatter(
            upper_all.astype(jnp.bfloat16), "rows", scatter_dimension=1, tiled=True
        ).astype(jnp.float32),
    )
    gain_s, bias_s, qkv_s, proj_s, up_s, down_s, outer_s, upper_s = shares
    totals = lax.psum((gain_s, bias_s, qkv_s, proj_s, up_s, down_s, outer_s, upper_s), "dp")
    return (
        layer_out,
        grad_tokens,
        totals[0],
        totals[1],
        totals[2],
        totals[3],
        totals[4],
        totals[5],
        totals[6],
        totals[7],
    )


def solution(mesh):
    in_specs = (
        P("dp", None, "rows", None, None),
        P("dp"),
        P("dp"),
        P(),
        P(),
        P(),
        P(),
        P(),
        P(),
        P(),
        P(),
        P("dp", None, "rows", None, None),
    )
    out_specs = (
        P("dp", None, "rows", None, None),
        P("dp", None, "rows", None, None),
        P(None, "rows"),
        P(None, "rows"),
        P(None, "rows", None),
        P(None, "rows", None),
        P(None, "rows", None),
        P(None, "rows", None),
        P(None, "rows"),
        P(None, "rows"),
    )
    return jax.shard_map(
        on_device, mesh=mesh, in_specs=in_specs, out_specs=out_specs, check_vma=False
    )
```

profile of v0, /device:TPU:0, one launch (start us, length us, event | category | flops | bytes accessed | tf_op | source)
XLA Modules:
  0.0 1357.9 jit_solution(2997041833732743838)
XLA Ops:
  25.6 28.0 %collective-permute-done = bf16[2,5,4,32,512]{4,3,2,1,0:T(8,128)(2,1)} collective-permute-done((bf16[2,5,4,32,512]{4,3,2,1,0:T(8,128)(2,1)}, bf16[2,5,4,32,512]{4,3,2,1,0:T(8,128)(2,1)}, u32[]{:S(2)}, u32[]{:S(2)}) %collective-permute-start) | collective-permute-done | bytes 1310752 | tf_op jit(solution)/shard_map/ppermute | solution.py:19
  58.0 6.4 convolution_convert_fusion.1
  64.3 19.8 %reshape.317 = bf16[10,4,64,3,8,64]{5,4,3,2,1,0:T(8,128)(2,1)} reshape(bf16[10,4,64,1536]{3,2,1,0:T(8,128)(2,1)} %convolution_convert_fusion.1) | data formatting | bytes 15728640 | tf_op jit(solution)/shard_map/reshape | solution.py:167
  84.1 12.0 fusion.163
  96.2 8.3 copy.179
  104.5 10.9 fusion.62
  115.4 7.2 fusion.14
  122.6 9.1 convert_bitcast_fusion.3
  131.6 8.2 copy.117
  139.8 7.8 reshape_reshape.11
  154.7 28.6 %collective-permute-done.1 = bf16[2,5,4,32,512]{4,3,2,1,0:T(8,128)(2,1)S(1)} collective-permute-done((bf16[2,5,4,32,512]{4,3,2,1,0:T(8,128)(2,1)S(1)}, bf16[2,5,4,32,512]{4,3,2,1,0:T(8,128)(2,1)S(1)}, u32[]{:S(2)}, u32[]{:S(2)}) %collective-permute-start.1) | collective-permute-done | bytes 1310752 | tf_op jit(solution)/shard_map/ppermute | solution.py:19
  190.6 15.4 %fusion.57 = (u8[2,5,32,2048]{3,2,1,0:T(8,128)(4,1)}, u8[2,5,32,2048]{3,2,1,0:T(8,128)(4,1)}, f32[2,5,8,32,2048]{4,3,2,1,0:T(8,128)}) fusion(f32[2048]{0:T(1024)S(1)} %bitcast.349, bf16[2,512,2048]{2,1,0:T(8,128)(2,1)S(1)} %copy-done.94, f32[2,5,8,32,512]{4,3,2,1,0:T(8,128)S(1)} %get-tuple-element.78, f32[512]{0:T(512)S(1)} %bitcast.366, ...), kind=kOutput, calls=%fused_computation.142 | convolution fusion | flops 5447352320 | bytes 29716480 | tf_op jit(solution)/shard_map/dot_general | solution.py:96
  206.0 51.2 %multiply_convert_fusion.1 = (bf16[2,5,8,32,2048]{4,3,2,1,0:T(8,128)(2,1)S(1)}, f32[2,5,8,32,2048]{4,3,2,1,0:T(8,128)}) fusion(f32[2,5,8,32,2048]{4,3,2,1,0:T(8,128)} %get-tuple-element.79, f32[2048]{0:T(1024)S(1)} %bitcast.350, u8[2,5,32,2048]{3,2,1,0:T(8,128)(4,1)} %get-tuple-element.13, u8[2,5,32,2048]{3,2,1,0:T(8,128)(4,1)} %get-tuple-element.12), kind=kLoop, calls=%fused_computation.30 | loop fusion | flops 372244480 | bytes 53747712 | tf_op jit(solution)/shard_map/convert_element_type | solution.py:98
  268.0 6.7 convolution_convert_fusion
  274.6 19.8 %reshape.319 = bf16[2,5,256,3,8,64]{5,4,3,2,1,0:T(8,128)(2,1)} reshape(bf16[2,5,8,32,1536]{4,3,2,1,0:T(8,128)(2,1)} %convolution_convert_fusion) | data formatting | bytes 15728640 | tf_op jit(solution)/shard_map/reshape | solution.py:193
  294.5 8.8 fusion.162
  307.2 12.7 fusion.22
  319.9 25.4 %fusion.172 = (f32[2,256,8,5]{3,2,1,0:T(8,128)S(1)}, f32[2,256,8,5,5]{3,4,2,1,0:T(8,128)}) fusion(f32[2,256,8,5,5]{3,4,2,1,0:T(8,128)} %fusion.22, pred[5,5]{0,1:T(8,128)(4,1)S(1)} %iota_compare_fusion), kind=kOutput, calls=%fused_computation.296 | output fusion | flops 614404 | bytes 901145 | tf_op jit(solution)/shard_map/sub | solution.py:123
  345.3 14.3 %convert_bitcast_fusion.1 = bf16[2,5,256,8,64]{4,1,3,2,0:T(8,128)(2,1)} fusion(bf16[2,5,256,1,8,64]{5,4,3,2,1,0:T(8,128)(2,1)} %get-tuple-element.51, f32[2,256,8,5,5]{3,4,2,1,0:T(8,128)} %get-tuple-element.83, f32[2,256,8,5]{3,2,1,0:T(8,128)S(1)} %get-tuple-element.82), kind=kOutput, calls=%fused_computation.74 | convolution fusion | flops 14622720 | bytes 5734400 | tf_op jit(solution)/shard_map/iphtu,iuphe->itphe/dot_general | solution.py:205
  359.6 12.2 copy.143
  371.8 6.5 copy.123
  378.3 7.1 reshape.320
  394.2 14.5 %fusion.58 = (u8[2,5,32,2048]{3,2,1,0:T(8,128)(4,1)S(1)}, u8[2,5,32,2048]{3,2,1,0:T(8,128)(4,1)S(1)}, f32[2,5,8,32,2048]{4,3,2,1,0:T(8,128)}) fusion(f32[2048]{0:T(1024)S(1)} %bitcast.352, bf16[2,512,2048]{2,1,0:T(8,128)(2,1)S(1)} %copy-done.95, f32[2,5,8,32,512]{4,3,2,1,0:T(8,128)S(1)} %get-tuple-element.85, f32[512]{0:T(512)S(1)} %bitcast.368, ...), kind=kOutput, calls=%fused_computation.143 | convolution fusion | flops 5447352320 | bytes 29716480 | tf_op jit(solution)/shard_map/dot_general | solution.py:96
  408.7 50.9 %multiply_convert_fusion = (bf16[2,5,8,32,2048]{4,3,2,1,0:T(8,128)(2,1)}, f32[2,5,8,32,2048]{4,3,2,1,0:T(8,128)}) fusion(f32[2,5,8,32,2048]{4,3,2,1,0:T(8,128)} %get-tuple-element.86, f32[2048]{0:T(1024)S(1)} %bitcast.353, u8[2,5,32,2048]{3,2,1,0:T(8,128)(4,1)S(1)} %get-tuple-element.11, u8[2,5,32,2048]{3,2,1,0:T(8,128)(4,1)S(1)} %get-tuple-element.10), kind=kLoop, calls=%fused_computation.17 | loop fusion | flops 372244480 | bytes 53747712 | tf_op jit(solution)/shard_map/convert_element_type | solution.py:98
  459.7 21.6 %fusion.174 = (bf16[2048]{0:T(1024)(128)(2,1)S(1)}, bf16[2,5,8,32,2048]{4,3,2,1,0:T(8,128)(2,1)}) fusion(f32[2,5,8,32,2048]{4,3,2,1,0:T(8,128)} %get-tuple-element.47, bf16[2,2048,512]{2,1,0:T(8,128)(2,1)} %param.20, bf16[2,5,8,32,512]{4,3,2,1,0:T(8,128)(2,1)S(1)} %copy-done.20, f32[2,5]{1,0:T(2,128)S(1)} %copy-done.85, ...), kind=kOutput, calls=%fused_computation.298 | convolution fusion | flops 5456525312 | bytes 57159720 | tf_op jit(solution)/shard_map/dot_general | solution.py:85
  481.2 10.4 multiply_reduce_fusion.2
  504.2 13.7 %convert_bitcast_fusion = bf16[2,5,256,1,8,64]{5,1,4,2,0,3:T(8,128)(2,1)} fusion(bf16[2,5,256,8,64]{4,3,2,1,0:T(8,128)(2,1)} %reshape.321, f32[2,256,8,5,5]{3,4,2,1,0:T(8,128)} %get-tuple-element.83, f32[2,256,8,5]{3,2,1,0:T(8,128)} %copy-done.34), kind=kOutput, calls=%fused_computation.73 | convolution fusion | flops 14622720 | bytes 5734400 | tf_op jit(solution)/shard_map/iphtu,itphe->iuphe/dot_general | solution.py:228
  518.0 22.0 %multiply_reduce_fusion = (f32[2,256,8,5]{3,2,1,0:T(8,128)}, f32[2,256,8,5,5]{3,4,2,1,0:T(8,128)}) fusion(f32[2,256,8,5,5]{3,4,2,1,0:T(8,128)} %get-tuple-element.83, f32[2,256,8,5]{3,2,1,0:T(8,128)S(1)} %copy-done.35, bf16[2,5,256,1,8,64]{5,4,3,2,1,0:T(8,128)(2,1)} %get-tuple-element.51, bf16[2,5,256,8,64]{4,3,2,1,0:T(8,128)(2,1)} %reshape.321), kind=kOutput, calls=%fused_computation.46 | convolution fusion | flops 13393920 | bytes 6225920 | tf_op jit(solution)/shard_map/itphe,iuphe->iphtu/dot_general | solution.py:231
  539.9 16.1 %multiply_convert_fusion.4 = bf16[2,256,8,5,5]{3,4,2,1,0:T(8,128)(2,1)} fusion(f32[2,256,8,5,5]{3,4,2,1,0:T(8,128)} %get-tuple-element.89, f32[2,256,8,5]{3,2,1,0:T(8,128)} %get-tuple-element.88, f32[2,256,8,5,5]{3,4,2,1,0:T(8,128)} %get-tuple-element.83, f32[2,256,8,5]{3,2,1,0:T(8,128)S(1)} %copy-done.35), kind=kLoop, calls=%fused_computation.45 | loop fusion | flops 409600 | bytes 1187840 | tf_op jit(solution)/shard_map/convert_element_type | solution.py:129
  556.1 10.9 fusion.20
  567.0 10.8 fusion.19
  577.8 7.0 reshape_reshape.13
  584.9 15.4 %pad_maximum_fusion = bf16[2,5,256,3,8,64]{5,1,4,2,0,3:T(8,128)(2,1)S(1)} fusion(bf16[2,5,256,1,8,64]{5,1,4,2,0,3:T(8,128)(2,1)} %convert_bitcast_fusion, bf16[2,5,256,1,8,64]{5,1,4,2,0,3:T(8,128)(2,1)} %fusion.20, bf16[2,5,256,1,8,64]{5,1,4,2,0,3:T(8,128)(2,1)} %fusion.19), kind=kLoop, calls=%fused_computation.3 | loop fusion | flops 7864320 | bytes 15728640 | tf_op jit(solution)/shard_map/stack | solution.py:247
  600.3 8.3 copy-done.1
  608.6 7.3 copy.127
  615.9 21.1 %convert_element_type.197 = bf16[2,5,8,32,1536]{4,3,2,1,0:T(8,128)(2,1)} reshape(bf16[2,5,256,3,8,64]{5,4,3,2,1,0:T(8,128)(2,1)} %copy.127) | data formatting | bytes 15728640 | tf_op jit(solution)/shard_map/convert_element_type | solution.py:247
  637.1 10.8 fusion.154
  656.4 13.2 fusion.75
  669.6 21.8 %fusion.175 = (bf16[2048]{0:T(1024)(128)(2,1)S(1)}, bf16[2,5,8,32,2048]{4,3,2,1,0:T(8,128)(2,1)}) fusion(f32[2,5,8,32,2048]{4,3,2,1,0:T(8,128)} %get-tuple-element.49, bf16[2,2048,512]{2,1,0:T(8,128)(2,1)} %param.20, f32[2,5,8,32,512]{4,3,2,1,0:T(8,128)S(1)} %get-tuple-element.39, f32[2,5,8,32,2048]{4,3,2,1,0:T(8,128)} %get-tuple-element.79, ...), kind=kOutput, calls=%fused_computation.299 | convolution fusion | flops 5453903872 | bytes 59781120 | tf_op jit(solution)/shard_map/dot_general | solution.py:85
  691.5 10.2 multiply_reduce_fusion.4
  721.5 21.8 %collective-permute-done.2 = bf16[2,5,4,32,512]{4,3,2,1,0:T(8,128)(2,1)} collective-permute-done((bf16[2,5,4,32,512]{4,3,2,1,0:T(8,128)(2,1)}, bf16[2,5,4,32,512]{4,3,2,1,0:T(8,128)(2,1)}, u32[]{:S(2)}, u32[]{:S(2)}) %collective-permute-start.2) | collective-permute-done | bytes 1310752 | tf_op jit(solution)/shard_map/ppermute | solution.py:19
  752.3 8.3 copy.137
  760.6 10.8 convert_bitcast_fusion.2
  771.3 15.1 %multiply_reduce_fusion.1 = (f32[10,4,8,64]{3,2,1,0:T(8,128)S(1)}, f32[10,4,8,64,64]{3,4,2,1,0:T(8,128)}) fusion(f32[10,4,8,64]{3,2,1,0:T(8,128)S(1)} %copy-done.28, f32[10,4,8,64,64]{3,4,2,1,0:T(8,128)} %get-tuple-element.76, pred[4,64,64]{1,2,0:T(8,128)(4,1)S(1)} %copy-done.43, bf16[10,4,64,8,64]{2,4,3,1,0:T(8,128)(2,1)} %copy.137, ...), kind=kOutput, calls=%fused_computation.54 | convolution fusion | flops 174305280 | bytes 15908864 | tf_op jit(solution)/shard_map/fwqhe,fwkhe->fwhqk/dot_general | solution.py:269
  786.4 9.3 multiply_convert_fusion.7
  798.0 6.4 fusion.47
  804.5 8.5 fusion.46
  813.0 8.9 pad_maximum_fusion.1
  821.9 12.4 copy.140
  834.3 20.7 %convert_element_type.204 = bf16[10,4,8,8,1536]{4,3,2,1,0:T(8,128)(2,1)} reshape(bf16[10,4,64,3,8,64]{5,4,3,2,1,0:T(8,128)(2,1)} %copy.140) | data formatting | bytes 15728640 | tf_op jit(solution)/shard_map/convert_element_type | solution.py:279
  863.5 11.8 fusion.76
  875.4 73.9 %collective-permute-done.3 = bf16[2,5,4,32,1536]{4,3,2,1,0:T(8,128)(2,1)} collective-permute-done((bf16[2,5,4,32,1536]{4,3,2,1,0:T(8,128)(2,1)S(1)}, bf16[2,5,4,32,1536]{4,3,2,1,0:T(8,128)(2,1)}, u32[]{:S(2)}, u32[]{:S(2)}) %collective-permute-start.3) | collective-permute-done | bytes 3932192 | tf_op jit(solution)/shard_map/ppermute | solution.py:19
  949.3 7.6 fusion.153
  969.1 11.5 fusion.74
  980.7 11.5 fusion.73
  994.8 33.2 %copy.142 = bf16[2,5,256,3,8,64]{2,1,0,5,4,3:T(8,128)(2,1)} copy(bf16[2,5,256,3,8,64]{5,1,4,2,0,3:T(8,128)(2,1)} %copy-done.1) | data formatting | bytes 15728640 | tf_op jit(solution)/shard_map/stack | solution.py:247
  1028.0 18.2 %convert_element_type.208 = bf16[2560,1536]{0,1:T(8,128)(2,1)} reshape(bf16[2,5,256,3,8,64]{2,1,0,5,4,3:T(8,128)(2,1)} %copy.142) | data formatting | bytes 15728640 | tf_op jit(solution)/shard_map/convert_element_type | solution.py:247
  1046.2 8.5 fusion.72
  1054.7 6.8 fusion.71
  1063.5 10.9 multiply_convert_fusion.9
  1076.4 8.2 add_convert_fusion.2
  1086.2 71.7 %reduce-scatter.21.cloned.1.call-done = bf16[2,128,2048]{2,1,0:T(8,128)(2,1)} async-done(((bf16[2,512,2048]{2,1,0:T(8,128)(2,1)}), bf16[2,128,2048]{2,1,0:T(8,128)(2,1)}) %reduce-scatter.21.cloned.1.call-update) | async-done | bytes 1048592 | tf_op jit(solution)/shard_map/reduce_scatter | solution.py:307
  1157.9 63.1 %reduce-scatter.17.cloned.1.call-done = bf16[2,128,1536]{2,1,0:T(8,128)(2,1)} async-done(((bf16[2,512,1536]{2,1,0:T(8,128)(2,1)}), bf16[2,128,1536]{2,1,0:T(8,128)(2,1)}) %reduce-scatter.17.cloned.1.call-update) | async-done | bytes 786448 | tf_op jit(solution)/shard_map/reduce_scatter | solution.py:301
  1221.0 129.6 %all-reduce.2 = (f32[4,128]{1,0:T(4,128)}, f32[4,128]{1,0:T(4,128)}, f32[2,128,1536]{2,1,0:T(8,128)}, f32[2,128,512]{2,1,0:T(8,128)}, f32[2,128,2048]{2,1,0:T(8,...) all-reduce(bf16[4,128]{1,0:T(4,128)(2,1)S(1)} %copy.172, ...), channel_id=1, replica_groups=mesh['dp'=8,'rows'=4] {'dp'}, use_global_device_ids=true, to_apply=%region_27.28 | all-reduce | flops 1575424 | bytes 9452544 | tf_op jit(solution)/shard_map/psum | solution.py:321
  (344 shorter events, 140.5 us)
Async XLA Ops:
  7.2 8.7 copy-start.4
  7.2 1067.3 %reduce-scatter.29.cloned.1.call-start = ((), (), s32[]{:S(2)}) async-start(), calls=%async_computation.14 | async-start | bytes 163840
  8.7 179.4 %copy-start.78 = (f32[1,512]{1,0:T(1,128)}, f32[1,512]{1,0:T(1,128)S(1)}, u32[]{:S(2)}) copy-start(f32[1,512]{1,0:T(1,128)S(1)} %get-tuple-element.64) | copy-start | bytes 6148
  8.7 256.6 %copy-start.71 = (f32[1,512]{1,0:T(1,128)}, f32[1,512]{1,0:T(1,128)S(1)}, u32[]{:S(2)}) copy-start(f32[1,512]{1,0:T(1,128)S(1)} %get-tuple-element.66) | copy-start | bytes 6148
  10.2 178.0 %copy-start.87 = (f32[1,512]{1,0:T(1,128)}, f32[1,512]{1,0:T(1,128)S(1)}, u32[]{:S(2)}) copy-start(f32[1,512]{1,0:T(1,128)S(1)} %get-tuple-element.68) | copy-start | bytes 6148
  20.2 33.4 %collective-permute-start = (bf16[2,5,4,32,512]{4,3,2,1,0:T(8,128)(2,1)}, bf16[2,5,4,32,512]{4,3,2,1,0:T(8,128)(2,1)}, u32[]{:S(2)}, u32[]{:S(2)}) collective-permute-start(bf16[2,5,4,32,512]{4,3,2,1,0:T(8,128)(2,1)} %get-tuple-element.60), channel_id=1, source_target_pairs={{1,0},{2,1},{3,2},{0,3},{5,4},{6,5},{7,6},{4,7},{9,8},{10,9},{11,1... | collective-permute-start | bytes 3932168 | tf_op jit(solution)/shard_map/ppermute | solution.py:19
  25.5 30.5 %copy-start.19 = (bf16[2,5,4,32,512]{4,3,2,1,0:T(8,128)(2,1)S(1)}, bf16[2,5,4,32,512]{4,3,2,1,0:T(8,128)(2,1)}, u32[]{:S(2)}) copy-start(bf16[2,5,4,32,512]{4,3,2,1,0:T(8,128)(2,1)} %get-tuple-element.59) | copy-start | bytes 3932164
  25.6 96.9 %copy-start.42 = (pred[4,64,64]{1,2,0:T(8,128)(4,1)}, pred[4,64,64]{1,2,0:T(8,128)(4,1)S(1)}, u32[]{:S(2)}) copy-start(pred[4,64,64]{1,2,0:T(8,128)(4,1)S(1)} %broadcast_compare_fusion) | copy-start | bytes 49156
  147.7 36.8 %copy-start.61 = (bf16[2,512,512]{2,1,0:T(8,128)(2,1)S(1)}, bf16[2,512,512]{2,1,0:T(8,128)(2,1)}, u32[]{:S(2)}) copy-start(bf16[2,512,512]{2,1,0:T(8,128)(2,1)} %param.18) | copy-start | bytes 3145732
  149.8 36.7 %copy-start.16 = (bf16[10,8,4,8,512]{4,3,2,1,0:T(8,128)(2,1)}, bf16[10,8,4,8,512]{4,3,2,1,0:T(8,128)(2,1)S(1)}, u32[]{:S(2)}) copy-start(bf16[10,8,4,8,512]{4,3,2,1,0:T(8,128)(2,1)S(1)} %copy.118) | copy-start | bytes 7864324
  150.0 36.5 %copy-start.36 = (bf16[2,5,8,4,512]{4,3,2,1,0:T(4,128)(2,1)}, bf16[2,5,8,4,512]{4,3,2,1,0:T(4,128)(2,1)S(1)}, u32[]{:S(2)}) copy-start(bf16[2,5,8,4,512]{4,3,2,1,0:T(4,128)(2,1)S(1)} %slice.197) | copy-start | bytes 983044
  150.7 32.6 %collective-permute-start.1 = (bf16[2,5,4,32,512]{4,3,2,1,0:T(8,128)(2,1)S(1)}, bf16[2,5,4,32,512]{4,3,2,1,0:T(8,128)(2,1)S(1)}, u32[]{:S(2)}, u32[]{:S(2)}) collective-permute-start(bf16[2,5,4,32,512]{4,3,2,1,0:T(8,128)(2,1)S(1)} %fusion.117), channel_id=1, source_target_pairs={{3,0},{0,1},{1,2},{2,3},{7,4},{4,5},{5,6},{6,7},{11,8},{8,9},{9,10... | collective-permute-start | bytes 3932168 | tf_op jit(solution)/shard_map/ppermute | solution.py:19
  154.0 52.0 %copy-start.73 = (f32[1,2048]{1,0:T(1,128)}, f32[1,2048]{1,0:T(1,128)S(1)}, u32[]{:S(2)}) copy-start(f32[1,2048]{1,0:T(1,128)S(1)} %get-tuple-element.62) | copy-start | bytes 24580
  186.5 70.7 %copy-start.14 = (f32[2,5,8,32,512]{4,3,2,1,0:T(8,128)}, f32[2,5,8,32,512]{4,3,2,1,0:T(8,128)S(1)}, u32[]{:S(2)}) copy-start(f32[2,5,8,32,512]{4,3,2,1,0:T(8,128)S(1)} %get-tuple-element.78) | copy-start | bytes 15728644
  186.5 19.5 %copy-start.52 = (f32[2,5,8,32]{3,2,1,0:T(8,128)}, f32[2,5,8,32]{3,2,1,0:T(8,128)S(1)}, u32[]{:S(2)}) copy-start(f32[2,5,8,32]{3,2,1,0:T(8,128)S(1)} %broadcast_multiply_fusion.2) | copy-start | bytes 30724
  188.1 17.9 %copy-start.64 = (f32[2,5,8,32]{3,2,1,0:T(8,128)}, f32[2,5,8,32]{3,2,1,0:T(8,128)S(1)}, u32[]{:S(2)}) copy-start(f32[2,5,8,32]{3,2,1,0:T(8,128)S(1)} %fusion.135) | copy-start | bytes 30724
  206.0 51.2 %copy-start.96 = (bf16[2,2048,512]{2,1,0:T(8,128)(2,1)S(1)}, bf16[2,2048,512]{2,1,0:T(8,128)(2,1)}, u32[]{:S(2)}) copy-start(bf16[2,2048,512]{2,1,0:T(8,128)(2,1)} %param.20) | copy-start | bytes 12582916
  345.3 14.3 %copy-start.34 = (f32[2,256,8,5]{3,2,1,0:T(8,128)}, f32[2,256,8,5]{3,2,1,0:T(8,128)S(1)}, u32[]{:S(2)}) copy-start(f32[2,256,8,5]{3,2,1,0:T(8,128)S(1)} %get-tuple-element.82) | copy-start | bytes 245764
  390.1 101.6 %copy-start.7 = (f32[2,5,8,32,512]{4,3,2,1,0:T(8,128)}, f32[2,5,8,32,512]{4,3,2,1,0:T(8,128)S(1)}, u32[]{:S(2)}) copy-start(f32[2,5,8,32,512]{4,3,2,1,0:T(8,128)S(1)} %get-tuple-element.85) | copy-start | bytes 15728644
  390.1 101.6 %copy-start.55 = (f32[2,5,8,32]{3,2,1,0:T(8,128)}, f32[2,5,8,32]{3,2,1,0:T(8,128)S(1)}, u32[]{:S(2)}) copy-start(f32[2,5,8,32]{3,2,1,0:T(8,128)S(1)} %broadcast_multiply_fusion) | copy-start | bytes 30724
  391.1 100.6 %copy-start.67 = (f32[2,5,8,32]{3,2,1,0:T(8,128)}, f32[2,5,8,32]{3,2,1,0:T(8,128)S(1)}, u32[]{:S(2)}) copy-start(f32[2,5,8,32]{3,2,1,0:T(8,128)S(1)} %fusion.137) | copy-start | bytes 30724
  408.7 50.9 %copy-start.20 = (bf16[2,5,8,32,512]{4,3,2,1,0:T(8,128)(2,1)S(1)}, bf16[2,5,8,32,512]{4,3,2,1,0:T(8,128)(2,1)}, u32[]{:S(2)}) copy-start(bf16[2,5,8,32,512]{4,3,2,1,0:T(8,128)(2,1)} %param.23) | copy-start | bytes 7864324
  408.7 50.9 %copy-start.85 = (f32[2,5]{1,0:T(2,128)S(1)}, f32[2,5]{1,0:T(2,128)}, u32[]{:S(2)}) copy-start(f32[2,5]{1,0:T(2,128)} %compare_convert_fusion) | copy-start | bytes 124
  504.2 13.8 %copy-start.35 = (f32[2,256,8,5]{3,2,1,0:T(8,128)S(1)}, f32[2,256,8,5]{3,2,1,0:T(8,128)}, u32[]{:S(2)}) copy-start(f32[2,256,8,5]{3,2,1,0:T(8,128)} %copy-done.34) | copy-start | bytes 245764
  518.0 49.0 %slice-start = ((s8[5242880]{0:T(1024)(128)(4,1)}), s8[1048576]{0:T(1024)(128)(4,1)S(1)}, s32[]{:S(2)}) async-start(s8[5242880]{0:T(1024)(128)(4,1)} %bitcast.312), calls=%async_computation.16 | async-start | bytes 2097152
  539.9 27.1 %slice-start.1 = ((s8[5242880]{0:T(1024)(128)(4,1)}), s8[4194304]{0:T(1024)(128)(4,1)S(1)}, s32[]{:S(2)}) async-start(s8[5242880]{0:T(1024)(128)(4,1)} %bitcast.312), calls=%async_computation.17 | async-start | bytes 8388608
  615.9 21.2 %copy-start.41 = (f32[2,5,8,32]{3,2,1,0:T(8,128)S(1)}, f32[2,5,8,32]{3,2,1,0:T(8,128)}, u32[]{:S(2)}) copy-start(f32[2,5,8,32]{3,2,1,0:T(8,128)} %copy-done.40) | copy-start | bytes 30724
  615.9 21.2 %copy-start.72 = (f32[1,512]{1,0:T(1,128)S(1)}, f32[1,512]{1,0:T(1,128)}, u32[]{:S(2)}) copy-start(f32[1,512]{1,0:T(1,128)} %copy-done.71) | copy-start | bytes 6148
  615.9 32.1 %slice-start.2 = ((s8[5242880]{0:T(1024)(128)(4,1)}), s8[1048576]{0:T(1024)(128)(4,1)S(1)}, s32[]{:S(2)}) async-start(s8[5242880]{0:T(1024)(128)(4,1)} %bitcast.314), calls=%async_computation.18 | async-start | bytes 2097152
  637.1 10.8 copy-start.60
  637.1 10.9 slice-start.3
  637.1 10.9 copy-start.47
  650.8 40.6 %slice-start.4 = ((s8[5242880]{0:T(1024)(128)(4,1)}), s8[1048576]{0:T(1024)(128)(4,1)S(1)}, s32[]{:S(2)}) async-start(s8[5242880]{0:T(1024)(128)(4,1)} %bitcast.321), calls=%async_computation.20 | async-start | bytes 2097152
  656.4 47.6 %copy-start.8 = (f32[2,5,8,32,512]{4,3,2,1,0:T(8,128)}, f32[2,5,8,32,512]{4,3,2,1,0:T(8,128)S(1)}, u32[]{:S(2)}) copy-start(f32[2,5,8,32,512]{4,3,2,1,0:T(8,128)S(1)} %get-tuple-element.39) | copy-start | bytes 15728644
  656.4 13.2 copy-start.74
  656.4 35.0 %slice-start.5 = ((s8[5242880]{0:T(1024)(128)(4,1)}), s8[4194304]{0:T(1024)(128)(4,1)S(1)}, s32[]{:S(2)}) async-start(s8[5242880]{0:T(1024)(128)(4,1)} %bitcast.321), calls=%async_computation.21 | async-start | bytes 8388608
  669.6 21.8 %copy-start.53 = (f32[2,5,8,32]{3,2,1,0:T(8,128)S(1)}, f32[2,5,8,32]{3,2,1,0:T(8,128)}, u32[]{:S(2)}) copy-start(f32[2,5,8,32]{3,2,1,0:T(8,128)} %copy-done.52) | copy-start | bytes 30724
  669.6 21.8 %copy-start.65 = (f32[2,5,8,32]{3,2,1,0:T(8,128)S(1)}, f32[2,5,8,32]{3,2,1,0:T(8,128)}, u32[]{:S(2)}) copy-start(f32[2,5,8,32]{3,2,1,0:T(8,128)} %copy-done.64) | copy-start | bytes 30724
  669.6 21.9 %copy-start.79 = (f32[1,512]{1,0:T(1,128)S(1)}, f32[1,512]{1,0:T(1,128)}, u32[]{:S(2)}) copy-start(f32[1,512]{1,0:T(1,128)} %copy-done.78) | copy-start | bytes 6148
  691.5 10.2 copy-start.58
  707.4 367.9 %reduce-scatter.31.cloned.1.call-start = ((), (), s32[]{:S(2)}) async-start(), calls=%async_computation.15 | async-start | bytes 655360
  711.9 31.4 %collective-permute-start.2 = (bf16[2,5,4,32,512]{4,3,2,1,0:T(8,128)(2,1)}, bf16[2,5,4,32,512]{4,3,2,1,0:T(8,128)(2,1)}, u32[]{:S(2)}, u32[]{:S(2)}) collective-permute-start(bf16[2,5,4,32,512]{4,3,2,1,0:T(8,128)(2,1)} %get-tuple-element.58), channel_id=1, source_target_pairs={{1,0},{2,1},{3,2},{0,3},{5,4},{6,5},{7,6},{4,7},{9,8},{10,9},{11,1... | collective-permute-start | bytes 3932168 | tf_op jit(solution)/shard_map/ppermute | solution.py:19
  716.3 360.0 %reduce-scatter.19.cloned.1.call-start = ((), (), s32[]{:S(2)}) async-start(), calls=%async_computation.9 | async-start | bytes 1310720 | tf_op jit(solution)/shard_map/reduce_scatter | solution.py:304
  720.1 25.6 %copy-start.18 = (bf16[2,5,4,32,512]{4,3,2,1,0:T(8,128)(2,1)S(1)}, bf16[2,5,4,32,512]{4,3,2,1,0:T(8,128)(2,1)}, u32[]{:S(2)}) copy-start(bf16[2,5,4,32,512]{4,3,2,1,0:T(8,128)(2,1)} %get-tuple-element.57) | copy-start | bytes 3932164
  721.3 363.3 %reduce-scatter.25.cloned.1.call-start = ((), (), s32[]{:S(2)}) async-start(), calls=%async_computation.12 | async-start | bytes 163840
  859.8 89.5 %copy-start.26 = (bf16[2,5,8,4,1536]{4,3,2,1,0:T(4,128)(2,1)}, bf16[2,5,8,4,1536]{4,3,2,1,0:T(4,128)(2,1)S(1)}, u32[]{:S(2)}) copy-start(bf16[2,5,8,4,1536]{4,3,2,1,0:T(4,128)(2,1)S(1)} %slice.208) | copy-start | bytes 2949124
  862.8 86.5 %collective-permute-start.3 = (bf16[2,5,4,32,1536]{4,3,2,1,0:T(8,128)(2,1)S(1)}, bf16[2,5,4,32,1536]{4,3,2,1,0:T(8,128)(2,1)}, u32[]{:S(2)}, u32[]{:S(2)}) collective-permute-start(bf16[2,5,4,32,1536]{4,3,2,1,0:T(8,128)(2,1)S(1)} %fusion.65), channel_id=1, source_target_pairs={{3,0},{0,1},{1,2},{2,3},{7,4},{4,5},{5,6},{6,7},{11,8},{8,9},{9,10... | collective-permute-start | bytes 11796488 | tf_op jit(solution)/shard_map/ppermute | solution.py:19
  863.5 85.8 %copy-start.5 = (bf16[2,5,8,32,512]{4,3,2,1,0:T(8,128)(2,1)S(1)}, bf16[2,5,8,32,512]{4,3,2,1,0:T(8,128)(2,1)}, u32[]{:S(2)}) copy-start(bf16[2,5,8,32,512]{4,3,2,1,0:T(8,128)(2,1)} %param.12) | copy-start | bytes 7864324
  863.5 85.8 %copy-start.11 = (bf16[10,8,4,8,1536]{4,3,2,1,0:T(8,128)(2,1)S(1)}, bf16[10,8,4,8,1536]{4,3,2,1,0:T(8,128)(2,1)}, u32[]{:S(2)}) copy-start(bf16[10,8,4,8,1536]{4,3,2,1,0:T(8,128)(2,1)} %copy-done.10) | copy-start | bytes 23592964
  863.5 85.8 %copy-start.39 = (f32[2,5,8,32]{3,2,1,0:T(8,128)S(1)}, f32[2,5,8,32]{3,2,1,0:T(8,128)}, u32[]{:S(2)}) copy-start(f32[2,5,8,32]{3,2,1,0:T(8,128)} %copy-done.38) | copy-start | bytes 30724
  863.5 85.8 %copy-start.70 = (f32[1,512]{1,0:T(1,128)S(1)}, f32[1,512]{1,0:T(1,128)}, u32[]{:S(2)}) copy-start(f32[1,512]{1,0:T(1,128)} %copy-done.69) | copy-start | bytes 6148
  863.5 85.8 %copy-start.99 = (bf16[2,512,1536]{2,1,0:T(8,128)(2,1)S(1)}, bf16[2,512,1536]{2,1,0:T(8,128)(2,1)}, u32[]{:S(2)}) copy-start(bf16[2,512,1536]{2,1,0:T(8,128)(2,1)} %param.17) | copy-start | bytes 9437188
  875.4 81.6 %copy-start.51 = (f32[2,5,8,32]{3,2,1,0:T(8,128)S(1)}, f32[2,5,8,32]{3,2,1,0:T(8,128)}, u32[]{:S(2)}) copy-start(f32[2,5,8,32]{3,2,1,0:T(8,128)} %copy-done.50) | copy-start | bytes 30724
  875.4 83.9 %copy-start.45 = (f32[2,5,8,32]{3,2,1,0:T(8,128)S(1)}, f32[2,5,8,32]{3,2,1,0:T(8,128)}, u32[]{:S(2)}) copy-start(f32[2,5,8,32]{3,2,1,0:T(8,128)} %copy-done.44) | copy-start | bytes 30724
  963.0 122.3 %reduce-scatter.27.cloned.1.call-start = ((), (), s32[]{:S(2)}) async-start(), calls=%async_computation.13 | async-start | bytes 163840
  964.0 122.2 %reduce-scatter.23.cloned.1.call-start = ((), (), s32[]{:S(2)}) async-start(), calls=%async_computation.11 | async-start | bytes 5242880 | tf_op jit(solution)/shard_map/reduce_scatter | solution.py:310
  968.8 11.9 copy-start.54
  968.8 11.9 copy-start.66
  968.8 11.9 copy-start.80
  968.8 11.9 copy-start.88
  968.8 189.1 %reduce-scatter.21.cloned.1.call-start = ((), (), s32[]{:S(2)}) async-start(), calls=%async_computation.10 | async-start | bytes 5242880 | tf_op jit(solution)/shard_map/reduce_scatter | solution.py:307
  994.5 226.5 %reduce-scatter.17.cloned.1.call-start = ((), (), s32[]{:S(2)}) async-start(), calls=%async_computation.8 | async-start | bytes 3932160 | tf_op jit(solution)/shard_map/reduce_scatter | solution.py:301
  1063.5 12.8 copy-start.49
  1076.4 144.7 %copy-start.63 = (bf16[2,128,512]{2,1,0:T(8,128)(2,1)S(1)}, bf16[2,128,512]{2,1,0:T(8,128)(2,1)}, u32[]{:S(2)}) copy-start(bf16[2,128,512]{2,1,0:T(8,128)(2,1)} %reduce-scatter.19.cloned.1.call-done) | copy-start | bytes 786436
  (57 other events, 228.0 us)
Sparse Core Ops, SparseCore 0:
  707.5 20.6 reduce-scatter.28
  731.2 38.4 reduce-scatter.30
  772.1 25.4 reduce-scatter.18
  963.2 18.3 reduce-scatter.24
  983.7 17.3 reduce-scatter.26
  1003.3 74.9 reduce-scatter.22
  1080.6 77.2 reduce-scatter.20
  1160.2 60.7 reduce-scatter.16
where the time goes:
time: 1370 us; the launch traced here: 1360 us
  matrix products  367 us (27%)
  local copies, waits for them, and re-layouts  306 us (22%)
  waiting for transfers between devices  287 us (21%)
  other arithmetic  243 us (18%)
  blocking collectives  130 us (9%)
  between operations  16.2 us (1%)
    ppermute x4, waiting for transfers between devices, from_behind(): return lax.ppermute(block, axis, route)  152 us
    psum x1, blocking collectives, on_device(): lax.psum((gain_s, bias_s, qkv_s, proj_s, up_s, down_s, outer_s, upper_s),...  130 us
    convert_element_type x2, other arithmetic, feed_forward(): active_low = active.astype(jnp.bfloat16)  102 us
    dot_general x8, matrix products, back_dot(): lax.dot_general(gradient, weight, (((gradient.ndim - 1,), (1,)), ((), ())...  86.8 us
    reduce_scatter x1, waiting for transfers between devices, on_device(): lax.psum_scatter(up_all.astype(jnp.bfloat16), 'rows', scatter_dimension=1...  71.7 us
    dot_general x8, matrix products, outer_sum(): lax.dot_general(flat_rows(left), flat_rows(right), (((0,), (0,)), ((), ()...  68.6 us
    reduce_scatter x1, waiting for transfers between devices, on_device(): lax.psum_scatter(qkv_all.astype(jnp.bfloat16), 'rows', scatter_dimension=...  63.1 us
    unnamed x227, local copies, waits for them, and re-layouts  51 us
  transfers between devices with their start and end apart: 12, of which 6 were waited for; matrix products, arithmetic and copies ran while one was open for 20% of the time, Pallas kernels for 0%

commit v1 on v0

v1 whole, which is shorter than its diff:
```python
import functools

import jax
import jax.numpy as jnp
from jax import lax
from jax.experimental import pallas as pl
from jax.experimental.pallas import tpu as pltpu
from jax.sharding import PartitionSpec as P

HEADS = 8
HEAD_DIM = 64
WIN = 8
SHIFT = 4
EPS = 1e-05
NEG = -1e30
SCALE = HEAD_DIM ** (-0.5)
BF16 = jnp.bfloat16
F32 = jnp.float32
NN = (((1,), (0,)), ((), ()))
NT = (((1,), (1,)), ((), ()))
CHUNK = 512
MIB = 1 << 20


def mm(left, right, dims=NN):
    return lax.dot_general(left, right, dims, preferred_element_type=F32)


def wide(column, lanes):
    return jnp.concatenate([column] * (lanes // column.shape[1]), axis=1)


def lane_sum(x):
    total = x[:, :128]
    for k in range(1, x.shape[1] // 128):
        total = total + x[:, 128 * k : 128 * (k + 1)]
    return total


def half_mask(shape):
    return lax.rem(lax.broadcasted_iota(jnp.int32, shape, len(shape) - 1), 128) < 64


def load_frame(own_ref, halo_ref):
    grid = jnp.concatenate([own_ref[0, 0], halo_ref[0, 0]], axis=0).astype(F32)
    rows, cols, feats = grid.shape
    blocks = grid.reshape(rows, cols // WIN, WIN, feats)
    after = jnp.concatenate([blocks[:, 1:], blocks[:, :1]], axis=1)
    first = lax.broadcasted_iota(jnp.int32, blocks.shape, 2) < SHIFT
    tiles = jnp.where(first, after, blocks).transpose(1, 0, 2, 3)
    return tiles.reshape(rows * cols, feats).astype(BF16).T.astype(F32)


def store_frame(value, own_ref, halo_ref):
    rows = own_ref.shape[2] + halo_ref.shape[2]
    cols, feats = own_ref.shape[3], own_ref.shape[4]
    flat = value.astype(BF16).T.astype(F32)
    tiles = flat.reshape(cols // WIN, rows, WIN, feats).transpose(1, 0, 2, 3)
    before = jnp.concatenate([tiles[:, -1:], tiles[:, :-1]], axis=1)
    first = lax.broadcasted_iota(jnp.int32, tiles.shape, 2) < SHIFT
    grid = jnp.where(first, before, tiles).reshape(rows, cols, feats).astype(BF16)
    own_ref[0, 0] = grid[: own_ref.shape[2]]
    halo_ref[0, 0] = grid[own_ref.shape[2] :]


def norm(x, gain, bias):
    center = x - jnp.mean(x, axis=0, keepdims=True)
    spread = jnp.mean(center * center, axis=0, keepdims=True)
    rstd = lax.rsqrt(spread + EPS)
    xhat = center * rstd
    return xhat, rstd, (xhat * gain + bias).astype(BF16)


def norm_back(d_norm, xhat, rstd, gain):
    grad_gain = d_norm * xhat
    e_mean = jnp.mean(d_norm * gain, axis=0, keepdims=True)
    x_mean = jnp.mean(grad_gain * gain, axis=0, keepdims=True)
    d_hidden = (d_norm * gain - e_mean - xhat * x_mean) * rstd
    return d_hidden, lane_sum(grad_gain), lane_sum(d_norm)


def gelu_parts(pre):
    upper = 0.5 + 0.5 * lax.erf(pre * (0.5**0.5))
    density = jnp.exp(pre * pre * -0.5) * 0.3989422804014327
    return (pre * upper).astype(BF16), upper + pre * density


def head_sum(x):
    return jnp.sum(x.reshape(HEADS, HEAD_DIM, x.shape[1]), axis=1)


def head_spread(p):
    return jnp.broadcast_to(p[:, None, :], (HEADS, HEAD_DIM, p.shape[1])).reshape(
        HEADS * HEAD_DIM, p.shape[1]
    )


def head_pair(x):
    zero = jnp.zeros_like(x[:HEAD_DIM])
    return jnp.concatenate(
        [
            jnp.concatenate([x[:HEAD_DIM], zero], axis=1),
            jnp.concatenate([zero, x[HEAD_DIM:]], axis=1),
        ],
        axis=0,
    )


def window_blocks(p, left):
    zero = jnp.zeros_like(p)
    return jnp.concatenate([jnp.where(left, p, zero), jnp.where(left, zero, p)], axis=0)


def pack(info, pieces, keep_ref, send_ref):
    me, row = info[0], info[1]
    core, cell = lax.rem(me, 2), lax.div(me, 2)

    def step(i, carry):
        j, z = lax.div(i, 4), lax.rem(i, 4)
        for ref, side in ((keep_ref, core), (send_ref, 1 - core)):
            base = 0
            for acc_ref, depth in pieces:
                first = (z ^ row) * (8 * depth) + (side * 4 + (j ^ cell)) * depth
                part = acc_ref[pl.ds(pl.multiple_of(first, 16), depth), :].astype(BF16)
                for k in range(part.shape[1] // 512):
                    ref[j, z, base : base + depth, :] = part[:, 512 * k : 512 * (k + 1)]
                    base += depth
        return carry

    lax.fori_loop(0, 16, step, 0)


def row_sums(acc):
    return lax.dot_general(
        jnp.ones((8, 128), F32), acc, NT, precision=lax.Precision.HIGHEST, preferred_element_type=F32
    )


GAIN, BIAS, OUTB, UPB = 0, 2048, 4096, 6144

C1, XHAT1, ACT0, SLOPE0, A2, XHAT2, O2, R1_ROWS = 0, 512, 1024, 3072, 5120, 5632, 6144, 6656
A0, XHAT0, O0, QKV0, P0, R2_ROWS = 0, 512, 1024, 1536, 3072, 3584


def forward_kernel(
    info,
    own_ref,
    halo_ref,
    cot_own_ref,
    cot_halo_ref,
    mask_ref,
    vec_ref,
    wqkv_t_ref,
    wproj_t_ref,
    wup_t_ref,
    wdown_t_ref,
    wup_ref,
    wdown_ref,
    out_own_ref,
    out_halo_ref,
    r1_ref,
    r2_ref,
    qkv2_ref,
    p2_ref,
    stat_ref,
    g3_ref,
    keep_ref,
    send_ref,
    sums_ref,
    acc_up,
    acc_down,
    acc_vec,
    kv_ref,
):
    item, frame = pl.program_id(0), pl.program_id(1)
    items, frames = pl.num_programs(0), pl.num_programs(1)
    lanes = r1_ref.shape[2]
    feats = wqkv_t_ref.shape[2]

    def vec(base, index=0, size=512):
        return wide(vec_ref[base + 512 * index : base + 512 * index + size, :], lanes)

    @pl.when((item == 0) & (frame == 0))
    def _():
        acc_up[...] = jnp.zeros_like(acc_up)
        acc_down[...] = jnp.zeros_like(acc_down)
        acc_vec[...] = jnp.zeros_like(acc_vec)
        kv_ref[...] = jnp.zeros_like(kv_ref)

    x0 = load_frame(own_ref, halo_ref)
    xhat0, rstd0, a0 = norm(x0, vec(GAIN, 0), vec(BIAS, 0))
    r2_ref[0, A0 : A0 + 512, :] = a0
    r2_ref[0, XHAT0 : XHAT0 + 512, :] = xhat0.astype(BF16)
    qkv = mm(wqkv_t_ref[0], a0).astype(BF16)
    r2_ref[0, QKV0 : QKV0 + 1536, :] = qkv
    keys = qkv[512:1024].T
    left = half_mask((64, 256))
    left_one = left[:, :128]
    for pair in range(lanes // 128):
        cols = slice(128 * pair, 128 * pair + 128)
        allowed = mask_ref[pair] > 0.5
        for hp in range(HEADS // 2):
            dims = slice(128 * hp, 128 * hp + 128)
            scores = mm(keys[cols, dims], head_pair(qkv[dims, cols]))
            scores = jnp.where(left, scores[:64], scores[64:]) * SCALE
            scores = jnp.where(allowed, scores, NEG)
            exponent = jnp.exp(scores - jnp.max(scores, axis=0, keepdims=True))
            weights = exponent * (1.0 / jnp.sum(exponent, axis=0, keepdims=True))
            weights = weights.astype(BF16)
            r2_ref[0, P0 + 256 * pair + 64 * hp : P0 + 256 * pair + 64 * hp + 64, :] = weights
            for j in range(2):
                blocks = window_blocks(weights[:, 128 * j : 128 * j + 128], left_one)
                first = 128 * hp + 64 * j
                values = qkv[1024 + first : 1024 + first + 64, cols]
                r2_ref[0, O0 + first : O0 + first + 64, cols] = mm(values, blocks).astype(BF16)
    x1 = x0 + mm(wproj_t_ref[0], r2_ref[0, O0 : O0 + 512, :]) + vec(OUTB, 0)

    xhat1, rstd1, c1 = norm(x1, vec(GAIN, 1), vec(BIAS, 1))
    r1_ref[0, C1 : C1 + 512, :] = c1
    r1_ref[0, XHAT1 : XHAT1 + 512, :] = xhat1.astype(BF16)
    x2 = x1 + vec(OUTB, 1)
    for k in range(wup_t_ref.shape[1] // CHUNK):
        part = slice(CHUNK * k, CHUNK * (k + 1))
        pre = mm(wup_t_ref[0, part, :], c1) + vec(UPB, k)
        act, slope = gelu_parts(pre)
        r1_ref[0, ACT0 + CHUNK * k : ACT0 + CHUNK * (k + 1), :] = act
        r1_ref[0, SLOPE0 + CHUNK * k : SLOPE0 + CHUNK * (k + 1), :] = slope.astype(BF16)
        x2 = x2 + mm(wdown_t_ref[0, :, part], act)

    xhat2, rstd2, a2 = norm(x2, vec(GAIN, 2), vec(BIAS, 2))
    r1_ref[0, A2 : A2 + 512, :] = a2
    r1_ref[0, XHAT2 : XHAT2 + 512, :] = xhat2.astype(BF16)
    qkv = mm(wqkv_t_ref[1], a2).astype(BF16)
    qkv2_ref[0] = qkv
    kv_ref[frame] = qkv[512:]
    query = qkv[:512].astype(F32) * SCALE
    scores = []
    for u in range(kv_ref.shape[0]):
        score = head_sum(query * kv_ref[u, :512, :].astype(F32))
        scores.append(jnp.where(u <= frame, score, NEG))
    top = functools.reduce(jnp.maximum, scores)
    exponents = [jnp.exp(s - top) for s in scores]
    scale = 1.0 / sum(exponents)
    mixed = jnp.zeros((feats, lanes), F32)
    for u in range(kv_ref.shape[0]):
        weight = exponents[u] * scale
        p2_ref[0, u] = weight
        weight = weight.astype(BF16).astype(F32)
        mixed = mixed + head_spread(weight) * kv_ref[u, 512:, :].astype(F32)
    o2 = mixed.astype(BF16)
    r1_ref[0, O2 : O2 + 512, :] = o2
    is_video = info[2 + item].astype(F32)
    x3 = x2 + is_video * (mm(wproj_t_ref[1], o2) + vec(OUTB, 2))

    is_valid = jnp.where(frame < info[2 + items + item], 1.0, 0.0)
    g4 = load_frame(cot_own_ref, cot_halo_ref) * is_valid
    grad_low = g4.astype(BF16)
    xhat3, rstd3, c3 = norm(x3, vec(GAIN, 3), vec(BIAS, 3))
    x4 = x3 + vec(OUTB, 3)
    d_norm = jnp.zeros((feats, lanes), F32)
    for k in range(wup_t_ref.shape[1] // CHUNK):
        part = slice(CHUNK * k, CHUNK * (k + 1))
        pre = mm(wup_t_ref[1, part, :], c3) + vec(UPB, 4 + k)
        act, slope = gelu_parts(pre)
        x4 = x4 + mm(wdown_t_ref[1, :, part], act)
        d_pre = (mm(wdown_ref[0, part, :], grad_low) * slope).astype(BF16)
        d_norm = d_norm + mm(wup_ref[0, :, part], d_pre)
        acc_up[:, part] += mm(c3, d_pre, NT)
        acc_down[part, :] += mm(act, grad_low, NT)
        acc_vec[1536 + CHUNK * k : 1536 + CHUNK * (k + 1), :] += lane_sum(d_pre.astype(F32))
    store_frame(x4 * is_valid, out_own_ref, out_halo_ref)
    d_hidden, gain_part, bias_part = norm_back(d_norm, xhat3, rstd3, vec(GAIN, 3))
    acc_vec[0:512, :] += gain_part
    acc_vec[512:1024, :] += bias_part
    acc_vec[1024:1536, :] += lane_sum(g4)
    g3_ref[0] = g4 + d_hidden
    stat_ref[0] = jnp.concatenate([rstd0, rstd1, rstd2, jnp.zeros((5, lanes), F32)], axis=0)

    @pl.when((item == items - 1) & (frame == frames - 1))
    def _():
        pack(info, [(acc_up, 16), (acc_down, 64)], keep_ref, send_ref)
        sums_ref[...] = row_sums(acc_vec[...])


def middle_kernel(
    info,
    g3_ref,
    r1_ref,
    qkv2_ref,
    p2_ref,
    stat_ref,
    vec_ref,
    wqkv_ref,
    wproj_ref,
    wup_ref,
    wdown_ref,
    g1_ref,
    keep_ref,
    send_ref,
    sums_ref,
    acc_up,
    acc_down,
    acc_qkv,
    acc_proj,
    acc_vec,
    dkv_ref,
):
    item, step = pl.program_id(0), pl.program_id(1)
    items, frames = pl.num_programs(0), pl.num_programs(1)
    frame = frames - 1 - step
    lanes = r1_ref.shape[2]
    feats = wqkv_ref.shape[1]

    def vec(base, index=0, size=512):
        return wide(vec_ref[base + 512 * index : base + 512 * index + size, :], lanes)

    @pl.when((item == 0) & (step == 0))
    def _():
        for acc in (acc_up, acc_down, acc_qkv, acc_proj, acc_vec):
            acc[...] = jnp.zeros_like(acc)

    @pl.when(step == 0)
    def _():
        dkv_ref[...] = jnp.zeros_like(dkv_ref)

    g3 = g3_ref[0]
    is_video = info[2 + item].astype(F32)
    d_attn = (g3 * is_video).astype(BF16)
    acc_proj[...] += mm(r1_ref[0, O2 : O2 + 512, :], d_attn, NT)
    acc_vec[0:512, :] += lane_sum(d_attn.astype(F32))
    d_mixed = mm(wproj_ref[0], d_attn).astype(BF16).astype(F32)
    query = qkv2_ref[frame, :512, :].astype(F32) * SCALE
    count = qkv2_ref.shape[0]
    weights = [p2_ref[0, u] for u in range(count)]
    d_weights = []
    for u in range(count):
        d_weights.append(head_sum(d_mixed * qkv2_ref[u, 1024:, :].astype(F32)))
    inner = sum(w * d for w, d in zip(weights, d_weights))
    d_query = jnp.zeros((feats, lanes), F32)
    for u in range(count):
        d_score = (weights[u] * (d_weights[u] - inner)).astype(BF16).astype(F32)
        spread = head_spread(d_score)
        d_query = d_query + spread * qkv2_ref[u, 512:1024, :].astype(F32)
        dkv_ref[u, :512, :] += spread * query
        dkv_ref[u, 512:, :] += head_spread(weights[u].astype(BF16).astype(F32)) * d_mixed
    d_qkv = jnp.concatenate(
        [(d_query * SCALE).astype(BF16), dkv_ref[frame].astype(BF16)], axis=0
    )
    acc_qkv[...] += mm(r1_ref[0, A2 : A2 + 512, :], d_qkv, NT)
    d_norm = mm(wqkv_ref[0], d_qkv)
    xhat = r1_ref[0, XHAT2 : XHAT2 + 512, :].astype(F32)
    d_hidden, gain_part, bias_part = norm_back(d_norm, xhat, stat_ref[0, 2:3, :], vec(GAIN, 2))
    acc_vec[512:1024, :] += gain_part
    acc_vec[1024:1536, :] += bias_part
    g2 = g3 + d_hidden

    grad_low = g2.astype(BF16)
    acc_vec[1536:2048, :] += lane_sum(grad_low.astype(F32))
    c1 = r1_ref[0, C1 : C1 + 512, :]
    d_norm = jnp.zeros((feats, lanes), F32)
    for k in range(wup_ref.shape[2] // CHUNK):
        part = slice(CHUNK * k, CHUNK * (k + 1))
        slope = r1_ref[0, SLOPE0 + CHUNK * k : SLOPE0 + CHUNK * (k + 1), :].astype(F32)
        d_pre = (mm(wdown_ref[0, part, :], grad_low) * slope).astype(BF16)
        d_norm = d_norm + mm(wup_ref[0, :, part], d_pre)
        acc_up[:, part] += mm(c1, d_pre, NT)
        acc_down[part, :] += mm(
            r1_ref[0, ACT0 + CHUNK * k : ACT0 + CHUNK * (k + 1), :], grad_low, NT
        )
        acc_vec[3072 + CHUNK * k : 3072 + CHUNK * (k + 1), :] += lane_sum(d_pre.astype(F32))
    xhat = r1_ref[0, XHAT1 : XHAT1 + 512, :].astype(F32)
    d_hidden, gain_part, bias_part = norm_back(d_norm, xhat, stat_ref[0, 1:2, :], vec(GAIN, 1))
    acc_vec[2048:2560, :] += gain_part
    acc_vec[2560:3072, :] += bias_part
    g1_ref[0] = g2 + d_hidden

    @pl.when((item == items - 1) & (step == frames - 1))
    def _():
        pieces = [(acc_up, 16), (acc_down, 64), (acc_qkv, 16), (acc_proj, 16)]
        pack(info, pieces, keep_ref, send_ref)
        sums_ref[...] = row_sums(acc_vec[...])


def space_kernel(
    info,
    g1_ref,
    r2_ref,
    stat_ref,
    vec_ref,
    wqkv_ref,
    wproj_ref,
    out_own_ref,
    out_halo_ref,
    keep_ref,
    send_ref,
    sums_ref,
    acc_qkv,
    acc_proj,
    acc_vec,
    dqkv_ref,
):
    item, frame = pl.program_id(0), pl.program_id(1)
    items, frames = pl.num_programs(0), pl.num_programs(1)
    lanes = r2_ref.shape[2]

    @pl.when((item == 0) & (frame == 0))
    def _():
        for acc in (acc_qkv, acc_proj, acc_vec):
            acc[...] = jnp.zeros_like(acc)

    g1 = g1_ref[0]
    d_attn = g1.astype(BF16)
    acc_proj[...] += mm(r2_ref[0, O0 : O0 + 512, :], d_attn, NT)
    acc_vec[0:512, :] += lane_sum(d_attn.astype(F32))
    d_mixed = mm(wproj_ref[0], d_attn).astype(BF16)
    values = r2_ref[0, QKV0 + 1024 : QKV0 + 1536, :].T
    left = half_mask((64, 256))
    left_one = left[:, :128]
    for pair in range(lanes // 128):
        cols = slice(128 * pair, 128 * pair + 128)
        for hp in range(HEADS // 2):
            dims = slice(128 * hp, 128 * hp + 128)
            d_weights = mm(values[cols, dims], head_pair(d_mixed[dims, cols]))
            d_weights = jnp.where(left, d_weights[:64], d_weights[64:])
            low = r2_ref[0, P0 + 256 * pair + 64 * hp : P0 + 256 * pair + 64 * hp + 64, :]
            weights = low.astype(F32)
            inner = jnp.sum(weights * d_weights, axis=0, keepdims=True)
            d_scores = (weights * (d_weights - inner)).astype(BF16)
            for j in range(2):
                one = slice(128 * j, 128 * j + 128)
                first = 128 * hp + 64 * j
                soft = window_blocks(low[:, one], left_one)
                slope = window_blocks(d_scores[:, one], left_one)
                query = r2_ref[0, QKV0 + first : QKV0 + first + 64, cols]
                key = r2_ref[0, QKV0 + 512 + first : QKV0 + 512 + first + 64, cols]
                dqkv_ref[first : first + 64, cols] = (mm(key, slope) * SCALE).astype(BF16)
                dqkv_ref[512 + first : 512 + first + 64, cols] = (
                    mm(query, slope, NT) * SCALE
                ).astype(BF16)
                dqkv_ref[1024 + first : 1024 + first + 64, cols] = mm(
                    d_mixed[first : first + 64, cols], soft, NT
                ).astype(BF16)
    d_qkv = dqkv_ref[...]
    acc_qkv[...] += mm(r2_ref[0, A0 : A0 + 512, :], d_qkv, NT)
    d_norm = mm(wqkv_ref[0], d_qkv)
    xhat = r2_ref[0, XHAT0 : XHAT0 + 512, :].astype(F32)
    gain = wide(vec_ref[GAIN : GAIN + 512, :], lanes)
    d_hidden, gain_part, bias_part = norm_back(d_norm, xhat, stat_ref[0, 0:1, :], gain)
    acc_vec[512:1024, :] += gain_part
    acc_vec[1024:1536, :] += bias_part
    store_frame(g1 + d_hidden, out_own_ref, out_halo_ref)

    @pl.when((item == items - 1) & (frame == frames - 1))
    def _():
        pack(info, [(acc_qkv, 16), (acc_proj, 16)], keep_ref, send_ref)
        sums_ref[...] = row_sums(acc_vec[...])


def unpack_kernel(info, ff1_ref, mid_ref, space_ref, qkv_ref, proj_ref, up_ref, down_ref):
    def put(out_ref, slot, source_ref, base, depth, width):
        for k in range(width // 512):
            rows = source_ref[0, base + depth * k : base + depth * (k + 1), :]
            out_ref[slot, :, 512 * k : 512 * (k + 1)] = rows.astype(F32)

    put(up_ref, 1, ff1_ref, 0, 16, 2048)
    put(down_ref, 1, ff1_ref, 64, 64, 512)
    put(up_ref, 0, mid_ref, 0, 16, 2048)
    put(down_ref, 0, mid_ref, 64, 64, 512)
    put(qkv_ref, 1, mid_ref, 128, 16, 1536)
    put(proj_ref, 1, mid_ref, 176, 16, 512)
    put(qkv_ref, 0, space_ref, 0, 16, 1536)
    put(proj_ref, 0, space_ref, 48, 16, 512)


def whole_spec(shape, single=True):
    mode = pl.Buffered(1) if single else None
    return pl.BlockSpec(shape, lambda *_: (0,) * len(shape), pipeline_mode=mode)


def part_spec(shape, index):
    def place(i, t, info):
        return (index,) + (0,) * (len(shape) - 1)

    return pl.BlockSpec((1,) + tuple(shape[1:]), place, pipeline_mode=pl.Buffered(1))


def params(limit=60 * MIB):
    return pltpu.CompilerParams(
        dimension_semantics=("arbitrary",) * 2, vmem_limit_bytes=limit
    )


def sds(shape, dtype):
    return jax.ShapeDtypeStruct(shape, dtype)


def run_forward(info, tokens, halo, cotangent, cot_halo, mask, vecs, weights):
    wqkv_t, wproj_t, wup_t, wdown_t, wup, wdown = weights
    items, frames, grid_rows, cols, feats = tokens.shape
    lanes = grid_rows * cols
    planes = items * frames
    half = (1, 1, SHIFT, cols, feats)
    own_spec = pl.BlockSpec(half, lambda i, t, info: (i, t, 1, 0, 0))
    halo_spec = pl.BlockSpec(half, lambda i, t, info: (i, t, 0, 0, 0))

    def plane_spec(*shape):
        return pl.BlockSpec(
            (1,) + shape, lambda i, t, info: (i * frames + t,) + (0,) * len(shape)
        )

    hidden = wup.shape[2]
    return pl.pallas_call(
        forward_kernel,
        grid_spec=pltpu.PrefetchScalarGridSpec(
            num_scalar_prefetch=1,
            grid=(items, frames),
            in_specs=[
                own_spec,
                halo_spec,
                own_spec,
                halo_spec,
                whole_spec(mask.shape),
                whole_spec(vecs.shape),
                whole_spec(wqkv_t.shape),
                whole_spec(wproj_t.shape),
                whole_spec(wup_t.shape),
                whole_spec(wdown_t.shape),
                part_spec(wup.shape, 1),
                part_spec(wdown.shape, 1),
            ],
            out_specs=[
                own_spec,
                halo_spec,
                plane_spec(R1_ROWS, lanes),
                plane_spec(R2_ROWS, lanes),
                plane_spec(3 * feats, lanes),
                plane_spec(frames, HEADS, lanes),
                plane_spec(8, lanes),
                plane_spec(feats, lanes),
                whole_spec((4, 4, 128, 512)),
                whole_spec((4, 4, 128, 512)),
                whole_spec((8, 3584)),
            ],
            scratch_shapes=[
                pltpu.VMEM((feats, hidden), F32),
                pltpu.VMEM((hidden, feats), F32),
                pltpu.VMEM((3584, 128), F32),
                pltpu.VMEM((frames, 2 * feats, lanes), BF16),
            ],
        ),
        out_shape=[
            sds(tokens.shape, BF16),
            sds(halo.shape, BF16),
            sds((planes, R1_ROWS, lanes), BF16),
            sds((planes, R2_ROWS, lanes), BF16),
            sds((planes, 3 * feats, lanes), BF16),
            sds((planes, frames, HEADS, lanes), F32),
            sds((planes, 8, lanes), F32),
            sds((planes, feats, lanes), F32),
            sds((4, 4, 128, 512), BF16),
            sds((4, 4, 128, 512), BF16),
            sds((8, 3584), F32),
        ],
        compiler_params=params(),
        cost_estimate=pl.CostEstimate(
            flops=55_000_000_000, bytes_accessed=100_000_000, transcendentals=20_000_000
        ),
        name="forward",
    )(info, tokens, halo, cotangent, cot_halo, mask, vecs, wqkv_t, wproj_t, wup_t, wdown_t, wup, wdown)


def run_middle(info, g3, r1, qkv2, p2, stats, vecs, weights, items):
    wqkv, wproj, wup, wdown = weights
    planes, feats, lanes = g3.shape
    frames = planes // items
    hidden = wup.shape[2]

    def plane_spec(*shape):
        return pl.BlockSpec(
            (1,) + shape,
            lambda i, s, info: (i * frames + frames - 1 - s,) + (0,) * len(shape),
        )

    return pl.pallas_call(
        middle_kernel,
        grid_spec=pltpu.PrefetchScalarGridSpec(
            num_scalar_prefetch=1,
            grid=(items, frames),
            in_specs=[
                plane_spec(feats, lanes),
                plane_spec(R1_ROWS, lanes),
                pl.BlockSpec((frames, 3 * feats, lanes), lambda i, s, info: (i, 0, 0)),
                plane_spec(frames, HEADS, lanes),
                plane_spec(8, lanes),
                whole_spec(vecs.shape),
                part_spec(wqkv.shape, 1),
                part_spec(wproj.shape, 1),
                part_spec(wup.shape, 0),
                part_spec(wdown.shape, 0),
            ],
            out_specs=[
                plane_spec(feats, lanes),
                whole_spec((4, 4, 192, 512)),
                whole_spec((4, 4, 192, 512)),
                whole_spec((8, 5120)),
            ],
            scratch_shapes=[
                pltpu.VMEM((feats, hidden), F32),
                pltpu.VMEM((hidden, feats), F32),
                pltpu.VMEM((feats, 3 * feats), F32),
                pltpu.VMEM((feats, feats), F32),
                pltpu.VMEM((5120, 128), F32),
                pltpu.VMEM((frames, 2 * feats, lanes), F32),
            ],
        ),
        out_shape=[
            sds((planes, feats, lanes), F32),
            sds((4, 4, 192, 512), BF16),
            sds((4, 4, 192, 512), BF16),
            sds((8, 5120), F32),
        ],
        compiler_params=params(),
        cost_estimate=pl.CostEstimate(
            flops=33_000_000_000, bytes_accessed=70_000_000, transcendentals=1_000_000
        ),
        name="middle",
    )(info, g3, r1, qkv2, p2, stats, vecs, wqkv, wproj, wup, wdown)


def run_space(info, g1, r2, stats, vecs, weights, shape):
    wqkv, wproj = weights
    items, frames, grid_rows, cols, feats = shape
    planes, _, lanes = g1.shape
    half = (1, 1, SHIFT, cols, feats)

    def plane_spec(*tail):
        return pl.BlockSpec(
            (1,) + tail, lambda i, t, info: (i * frames + t,) + (0,) * len(tail)
        )

    return pl.pallas_call(
        space_kernel,
        grid_spec=pltpu.PrefetchScalarGridSpec(
            num_scalar_prefetch=1,
            grid=(items, frames),
            in_specs=[
                plane_spec(feats, lanes),
                plane_spec(R2_ROWS, lanes),
                plane_spec(8, lanes),
                whole_spec((512, 128)),
                part_spec(wqkv.shape, 0),
                part_spec(wproj.shape, 0),
            ],
            out_specs=[
                pl.BlockSpec(half, lambda i, t, info: (i, t, 1, 0, 0)),
                pl.BlockSpec(half, lambda i, t, info: (i, t, 0, 0, 0)),
                whole_spec((4, 4, 64, 512)),
                whole_spec((4, 4, 64, 512)),
                whole_spec((8, 1536)),
            ],
            scratch_shapes=[
                pltpu.VMEM((feats, 3 * feats), F32),
                pltpu.VMEM((feats, feats), F32),
                pltpu.VMEM((1536, 128), F32),
                pltpu.VMEM((3 * feats, lanes), BF16),
            ],
        ),
        out_shape=[
            sds(shape, BF16),
            sds((items, frames, SHIFT, cols, feats), BF16),
            sds((4, 4, 64, 512), BF16),
            sds((4, 4, 64, 512), BF16),
            sds((8, 1536), F32),
        ],
        compiler_params=params(),
        cost_estimate=pl.CostEstimate(
            flops=14_000_000_000, bytes_accessed=40_000_000, transcendentals=1_000_000
        ),
        name="space",
    )(info, g1, r2, stats, vecs, wqkv, wproj)


def run_unpack(info, ff1, mid, space):
    def piece(array):
        return pl.BlockSpec((1,) + array.shape[1:], lambda q, info: (q ^ info[0], 0, 0))

    def out(depth, width):
        return pl.BlockSpec((2, depth, width), lambda q, info: (0, q, 0))

    return pl.pallas_call(
        unpack_kernel,
        grid_spec=pltpu.PrefetchScalarGridSpec(
            num_scalar_prefetch=1,
            grid=(8,),
            in_specs=[piece(ff1), piece(mid), piece(space)],
            out_specs=[out(16, 1536), out(16, 512), out(16, 2048), out(64, 512)],
        ),
        out_shape=[
            sds((2, 128, 1536), F32),
            sds((2, 128, 512), F32),
            sds((2, 128, 2048), F32),
            sds((2, 512, 512), F32),
        ],
        name="unpack",
    )(info, ff1, mid, space)


def shift(block, axis, distance):
    size = lax.axis_size(axis)
    return lax.ppermute(block, axis, [(i, (i + distance) % size) for i in range(size)])


def swap(block, axis, bits):
    return lax.ppermute(block, axis, [(i, i ^ bits) for i in range(lax.axis_size(axis))])


def add(*terms):
    return functools.reduce(jnp.add, [t.astype(F32) for t in terms])


def upper_bits(total):
    bit = 8
    while bit < lax.axis_size("dp"):
        total = add(total, swap(total, "dp", bit))
        bit *= 2
    return total


def reduce_pieces(keep, send):
    taken = swap(send, "dp", 1)
    parts = [add(keep[j], taken[j]).astype(BF16) for j in range(4)]
    across = [swap(parts[j], "dp", 2 * j) for j in range(1, 4)]
    rows = add(parts[0], *across).astype(BF16)
    along = [swap(rows[z], "rows", z) for z in range(1, 4)]
    return upper_bits(add(rows[0], *along)).astype(BF16)


def gather_pieces(mine):
    chip = jnp.stack([mine] + [swap(mine, "dp", 2 * j) for j in range(1, 4)])
    return jnp.concatenate([chip, swap(chip, "dp", 1)])


def reduce_vector(vector):
    total = add(vector, swap(vector, "dp", 1))
    total = add(total, *[swap(total, "dp", 2 * j) for j in range(1, 4)])
    total = upper_bits(total)
    return add(total, *[swap(total, "rows", z) for z in range(1, 4)])


def region_label(index, extent):
    return jnp.where(index < extent - WIN, 0, jnp.where(index < extent - SHIFT, 1, 2))


def tile_mask(cols):
    height = lax.axis_size("rows") * WIN
    row_label = region_label(lax.axis_index("rows") * WIN + jnp.arange(WIN), height)
    place = (jnp.arange(WIN) + SHIFT) % WIN
    col_label = region_label(jnp.arange(0, cols, WIN)[:, None] + place, cols)
    label = (row_label[None, :, None] * 3 + col_label[:, None, :]).reshape(-1, WIN * WIN)
    same = (label[:, :, None] == label[:, None, :]).astype(F32)
    pairs = same.reshape(-1, 2, WIN * WIN, WIN * WIN).transpose(0, 2, 1, 3)
    pairs = pairs.reshape(-1, WIN * WIN, 2 * WIN * WIN)
    return jnp.concatenate([pairs, pairs], axis=2)


def on_device(
    tokens,
    video_flag,
    frame_count,
    norm_gain,
    norm_bias,
    w_qkv,
    w_proj,
    w_up,
    w_down,
    out_bias,
    up_bias,
    cotangent,
):
    items, frames, grid_rows, cols, feats = tokens.shape
    place = lax.rem(lax.axis_index("dp"), 8)
    row = lax.axis_index("rows")
    info = jnp.concatenate([jnp.stack([place, row]), video_flag, frame_count]).astype(jnp.int32)
    unpack_info = jnp.stack([lax.rem(place, 2) * 4 + lax.div(place, 2)]).astype(jnp.int32)

    halo = shift(tokens[:, :, :SHIFT], "rows", -1)
    cot_halo = shift(cotangent[:, :, :SHIFT], "rows", -1)
    mask = tile_mask(cols)
    vecs = jnp.concatenate([v.reshape(-1) for v in (norm_gain, norm_bias, out_bias, up_bias)])
    vecs = jnp.broadcast_to(vecs[:, None], (vecs.shape[0], 128))
    flipped = [jnp.swapaxes(w, 1, 2) for w in (w_qkv, w_proj, w_up, w_down)]

    (out_own, out_halo, r1, r2, qkv2, p2, stats, g3, keep1, send1, sums1) = run_forward(
        info, tokens, halo, cotangent, cot_halo, mask, vecs, flipped + [w_up, w_down]
    )
    layer_out = lax.dynamic_update_slice(out_own, shift(out_halo, "rows", 1), (0,) * 5)
    g1, keep0, send0, sums0 = run_middle(
        info, g3, r1, qkv2, p2, stats, vecs, (w_qkv, w_proj, w_up, w_down), items
    )
    grad_own, grad_halo, keeps, sends, sumss = run_space(
        info, g1, r2, stats, vecs, (w_qkv, w_proj), tokens.shape
    )
    grad_tokens = lax.dynamic_update_slice(grad_own, shift(grad_halo, "rows", 1), (0,) * 5)

    ff1 = gather_pieces(reduce_pieces(keep1, send1))
    mid = gather_pieces(reduce_pieces(keep0, send0))
    space = gather_pieces(reduce_pieces(keeps, sends))
    grad_qkv, grad_proj, grad_up, grad_down = run_unpack(unpack_info, ff1, mid, space)

    a, b, c = sums1[0], sums0[0], sumss[0]
    gains = jnp.stack([c[512:1024], b[2048:2560], b[512:1024], a[0:512]])
    biases = jnp.stack([c[1024:1536], b[2560:3072], b[1024:1536], a[512:1024]])
    outer = jnp.stack([c[0:512], b[1536:2048], b[0:512], a[1024:1536]])
    upper = jnp.stack([b[3072:5120], a[1536:3584]])
    vector = jnp.concatenate([gains, biases, outer, upper.reshape(8, 512)])
    total = reduce_vector(vector)

    def share(values, width):
        return lax.dynamic_slice_in_dim(values, row * width, width, axis=1)

    narrow = share(total[:12], feats // lax.axis_size("rows"))
    up_sum = share(total[12:].reshape(2, -1), up_bias.shape[1] // lax.axis_size("rows"))
    return (
        layer_out,
        grad_tokens,
        narrow[0:4],
        narrow[4:8],
        grad_qkv,
        grad_proj,
        grad_up,
        grad_down,
        narrow[8:12],
        up_sum,
    )


def solution(mesh):
    split = P("dp", None, "rows", None, None)
    in_specs = (split, P("dp"), P("dp")) + (P(),) * 8 + (split,)
    out_specs = (
        split,
        split,
        P(None, "rows"),
        P(None, "rows"),
        P(None, "rows", None),
        P(None, "rows", None),
        P(None, "rows", None),
        P(None, "rows", None),
        P(None, "rows"),
        P(None, "rows"),
    )
    return jax.shard_map(
        on_device, mesh=mesh, in_specs=in_specs, out_specs=out_specs, check_vma=False
    )
```

time: 1370 us -> 563 us (0.41)
  matrix products: 367 us -> 0 us
  Pallas kernels: 0 us -> 275 us
  local copies, waits for them, and re-layouts: 306 us -> 38.3 us
  other arithmetic: 243 us -> 11.7 us
  blocking collectives: 130 us -> 0 us
  waiting for transfers between devices: 287 us -> 178 us
  starting transfers between devices: 8.71 us -> 56.1 us
  between operations: 16.2 us -> 1.17 us
    dot_general x36 -> x0, matrix products: 367 us -> none  [the longest x8 86.8 us: back_dot(): lax.dot_general(gradient, weight, (((gradient.ndim - 1,), (1,)), ((), ())...]
    pallas_call x0 -> x4, Pallas kernels: none -> 275 us  [the longest x1 136 us: run_forward(): pl.pallas_call(forward_kernel, grid_spec=pltpu.PrefetchScalarGridSpec(num...]
    reduce_scatter x4 -> x0, waiting for transfers between devices: 135 us -> none  [the longest x1 71.7 us: on_device(): lax.psum_scatter(up_all.astype(jnp.bfloat16), 'rows', scatter_dimension=1...]
    convert_element_type x9 -> x6, other arithmetic: 139 us -> 9.04 us  [the longest x3 5.38 us: reduce_pieces(): parts = [add(keep[j], taken[j]).astype(BF16) for j in range(4)]]
    psum x1 -> x0, blocking collectives: 130 us -> none  [on_device(): lax.psum((gain_s, bias_s, qkv_s, proj_s, up_s, down_s, outer_s, upper_s),...]
    convert_element_type x6 -> x0, local copies, waits for them, and re-layouts: 86.9 us -> none  [the longest x2 39.3 us: on_device(): jnp.stack([d_query_time, d_key_time, d_value_time], axis=3)]
    another operation x21 -> x0, local copies, waits for them, and re-layouts: 80.8 us -> none  [the longest x2 40.5 us: on_device(): jnp.stack([d_query_time, d_key_time, d_value_time], axis=3)]
    reshape x5 -> x2, local copies, waits for them, and re-layouts: 51.7 us -> 0.03 us  [the longest x1 0.02 us: on_device(): total[12:].reshape(2, -1)]
  transfers between devices with their start and end apart: 12 -> 44, of which waited for: 6 -> 21; matrix products, arithmetic and copies ran while one was open for 20% -> 7% of each run, Pallas kernels for 0% -> 0%
where the time goes in v1:
time: 563 us; the launch traced here: 560 us
  Pallas kernels  275 us (49%)
  waiting for transfers between devices  178 us (32%)
  starting transfers between devices  56.1 us (10%)
  local copies, waits for them, and re-layouts  38.3 us (7%)
  other arithmetic  11.7 us (2%)
    ppermute x40, waiting for transfers between devices, swap(): lax.ppermute(block, axis, [(i, i ^ bits) for i in range(lax.axis_size(axi...  143 us
    pallas_call x1, Pallas kernels, run_forward(): pl.pallas_call(forward_kernel, grid_spec=pltpu.PrefetchScalarGridSpec(num...  136 us
    pallas_call x1, Pallas kernels, run_middle(): pl.pallas_call(middle_kernel, grid_spec=pltpu.PrefetchScalarGridSpec(num_...  81.4 us
    pallas_call x1, Pallas kernels, run_space(): pl.pallas_call(space_kernel, grid_spec=pltpu.PrefetchScalarGridSpec(num_s...  50.5 us
    ppermute x40, starting transfers between devices, swap(): lax.ppermute(block, axis, [(i, i ^ bits) for i in range(lax.axis_size(axi...  47.2 us
    ppermute x4, waiting for transfers between devices, shift(): lax.ppermute(block, axis, [(i, (i + distance) % size) for i in range(size)])  34.7 us
    unnamed x53, local copies, waits for them, and re-layouts  19.7 us
  transfers between devices with their start and end apart: 44, of which 21 were waited for; matrix products, arithmetic and copies ran while one was open for 7% of the time, Pallas kernels for 0%

profile of v1, /device:TPU:0, one launch (start us, length us, event | category | flops | bytes accessed | tf_op | source)
XLA Modules:
  0.0 559.9 jit_solution(12789908013467977130)
XLA Ops:
  0.7 2.7 slice.202
  3.3 5.1 collective-permute-start
  8.4 1.1 slice.203
  11.1 6.3 %copy.30 = bf16[2,512,2048]{1,2,0:T(8,128)(2,1)} copy(bf16[2,512,2048]{2,1,0:T(8,128)(2,1)} %wup_ref.3) | data formatting | bytes 8388608 | tf_op args[7]
  17.3 6.4 %copy.31 = bf16[2,2048,512]{1,2,0:T(8,128)(2,1)} copy(bf16[2,2048,512]{2,1,0:T(8,128)(2,1)} %wdown_ref.3) | data formatting | bytes 8388608 | tf_op args[8]
  23.8 2.8 copy.28
  26.6 2.3 copy.29
  30.1 7.8 %collective-permute-done.halo_ref = bf16[2,5,4,32,512]{4,3,2,1,0:T(8,128)(2,1)} collective-permute-done((bf16[2,5,4,32,512]{4,3,2,1,0:T(8,128)(2,1)}, bf16[2,5,4,32,512]{4,3,2,1,0:T(8,128)(2,1)}, u32[]{:S(2)}, u32[]{:S(2)}) %collective-permute-start) | collective-permute-done | bytes 1310752 | tf_op jit(solution)/shard_map/ppermute | solution.py:710
  37.9 26.9 %collective-permute-done.1.cot_halo_ref = bf16[2,5,4,32,512]{4,3,2,1,0:T(8,128)(2,1)} collective-permute-done((bf16[2,5,4,32,512]{4,3,2,1,0:T(8,128)(2,1)}, bf16[2,5,4,32,512]{4,3,2,1,0:T(8,128)(2,1)}, u32[]{:S(2)}, u32[]{:S(2)}) %collective-permute-start.1) | collective-permute-done | bytes 1310752 | tf_op jit(solution)/shard_map/ppermute | solution.py:710
  64.9 5.4 broadcast_in_dim.40.vec_ref
  70.3 135.9 %forward.1 = (bf16[2,5,8,32,512]{4,3,2,1,0:T(8,128)(2,1)}, bf16[2,5,4,32,512]{4,3,2,1,0:T(8,128)(2,1)}, bf16[10,6656,256]{2,1,0:T(8,128)(2,1)}, bf16[10,3584,256...) custom-call(s32[6]{0:T(128)} %pad_add_fusion.info, ...), custom_call_target="tpu_custom_call" | custom-call | flops 54999998464 | bytes 100000000 | tf_op jit(solution)/shard_map/forward/pallas_call | solution.py:512
  206.2 81.4 %middle.1 = (f32[10,512,256]{2,1,0:T(8,128)}, bf16[4,4,192,512]{3,2,1,0:T(8,128)(2,1)}, bf16[4,4,192,512]{3,2,1,0:T(8,128)(2,1)}, f32[8,5120]{1,0:T(8,128)}) custom-call(s32[6]{0:T(128)} %pad_add_fusion.info, f32[10,512,256]{2,1,0:T(8,128)} %get-tuple-element.36.g3_ref, bf16[10,6656,256]{2,1,0:T(8,128)(2,1)} %get-tuple-element.37.r1_ref, ...), custom_call_target="tpu_custom_call" | custom-call | flops 32999999488 | bytes 70000000 | tf_op jit(solution)/shard_map/middle/pallas_call | solution.py:584
  287.6 50.5 %space.1 = (bf16[2,5,8,32,512]{4,3,2,1,0:T(8,128)(2,1)}, bf16[2,5,4,32,512]{4,3,2,1,0:T(8,128)(2,1)}, bf16[4,4,64,512]{3,2,1,0:T(8,128)(2,1)}, bf16[4,4,64,512]{3,2,1,0:T(8,128)(2,1)}, f32[8,1536]{1,0:T(8,128)}) custom-call(s32[6]{0:T(128)} %pad_add_fusion.info, f32[10,512,256]{2,1,0:T(8,128)} %get-tuple-element.41.g1_ref, ...), custom_call_target="tpu_custom_call" | custom-call | flops 14000000000 | bytes 40000000 | tf_op jit(solution)/shard_map/space/pallas_call | solution.py:641
  338.7 0.8 slice.216
  343.0 1.2 collective-permute-done.4
  344.2 1.5 collective-permute-start.5
  345.7 1.6 collective-permute-start.6
  348.8 1.0 collective-permute-done.6
  349.8 2.5 collective-permute-done.7
  352.3 4.3 collective-permute-start.10
  357.3 2.1 fusion.21
  359.4 23.5 %collective-permute-done.10 = f32[20,512]{1,0:T(8,128)S(1)} collective-permute-done((f32[20,512]{1,0:T(8,128)S(1)}, f32[20,512]{1,0:T(8,128)S(1)}, u32[]{:S(2)}, u32[]{:S(2)}) %collective-permute-start.10) | collective-permute-done | bytes 40992 | tf_op jit(solution)/shard_map/ppermute | solution.py:714
  382.9 1.6 collective-permute-start.34
  384.5 1.5 collective-permute-start.35
  386.7 3.0 collective-permute-done.34
  389.6 2.8 collective-permute-start.2
  392.4 2.5 collective-permute-start.36
  396.5 3.9 collective-permute-done.36
  400.4 1.4 fusion.16
  401.9 1.3 collective-permute-start.37
  403.2 3.1 collective-permute-start.39
  406.4 2.5 fusion.11
  408.9 14.5 %collective-permute-done.37 = bf16[64,512]{1,0:T(8,128)(2,1)S(1)} collective-permute-done((bf16[64,512]{1,0:T(8,128)(2,1)S(1)}, bf16[64,512]{1,0:T(8,128)(2,1)S(1)}, u32[]{:S(2)}, u32[]{:S(2)}) %collective-permute-start.37) | collective-permute-done | bytes 65568 | tf_op jit(solution)/shard_map/ppermute | solution.py:714
  423.4 0.9 collective-permute-start.12
  424.3 1.5 collective-permute-start.13
  425.8 1.1 collective-permute-start.14
  426.9 1.0 collective-permute-start.40
  428.5 21.4 %collective-permute-done.40 = bf16[64,512]{1,0:T(8,128)(2,1)S(1)} collective-permute-done((bf16[64,512]{1,0:T(8,128)(2,1)S(1)}, bf16[64,512]{1,0:T(8,128)(2,1)S(1)}, u32[]{:S(2)}, u32[]{:S(2)}) %collective-permute-start.40) | collective-permute-done | bytes 65568 | tf_op jit(solution)/shard_map/ppermute | solution.py:714
  450.4 1.4 constant_dynamic-update-slice_fusion.15
  451.9 2.3 collective-permute-done.41
  454.2 1.4 collective-permute-start.42
  455.6 1.4 constant_dynamic-update-slice_fusion.16
  457.0 2.4 collective-permute-done.42
  459.5 1.7 fusion.5
  461.4 4.3 collective-permute-start.17
  465.7 2.6 collective-permute-done.15
  468.4 5.9 %collective-permute-done.16 = bf16[128,512]{1,0:T(8,128)(2,1)S(1)} collective-permute-done((bf16[128,512]{1,0:T(8,128)(2,1)S(1)}, bf16[128,512]{1,0:T(8,128)(2,1)S(1)}, u32[]{:S(2)}, u32[]{:S(2)}) %collective-permute-start.16) | collective-permute-done | bytes 131104 | tf_op jit(solution)/shard_map/ppermute | solution.py:714
  475.7 1.6 collective-permute-start.23
  477.3 0.9 collective-permute-start.24
  478.1 1.1 collective-permute-start.25
  479.3 1.9 collective-permute-start.19
  481.2 1.5 collective-permute-start.20
  482.7 35.2 %collective-permute-done.19 = bf16[128,512]{1,0:T(8,128)(2,1)S(1)} collective-permute-done((bf16[128,512]{1,0:T(8,128)(2,1)S(1)}, bf16[128,512]{1,0:T(8,128)(2,1)S(1)}, u32[]{:S(2)}, u32[]{:S(2)}) %collective-permute-start.19) | collective-permute-done | bytes 131104 | tf_op jit(solution)/shard_map/ppermute | solution.py:714
  518.7 3.4 collective-permute-start.26
  522.1 2.4 collective-permute-start.28
  524.5 6.1 %collective-permute-done.26 = bf16[192,512]{1,0:T(8,128)(2,1)S(1)} collective-permute-done((bf16[192,512]{1,0:T(8,128)(2,1)S(1)}, bf16[192,512]{1,0:T(8,128)(2,1)S(1)}, u32[]{:S(2)}, u32[]{:S(2)}) %collective-permute-start.26) | collective-permute-done | bytes 196640 | tf_op jit(solution)/shard_map/ppermute | solution.py:714
  530.6 8.6 %collective-permute-done.27 = bf16[192,512]{1,0:T(8,128)(2,1)S(1)} collective-permute-done((bf16[192,512]{1,0:T(8,128)(2,1)S(1)}, bf16[192,512]{1,0:T(8,128)(2,1)S(1)}, u32[]{:S(2)}, u32[]{:S(2)}) %collective-permute-start.27) | collective-permute-done | bytes 196640 | tf_op jit(solution)/shard_map/ppermute | solution.py:714
  539.9 1.2 collective-permute-start.30
  541.1 1.7 collective-permute-start.31
  542.9 4.1 collective-permute-done.29
  547.0 2.5 collective-permute-done.30
  549.8 2.1 collective-permute-done.32
  552.0 1.1 copy-done.2
  553.1 6.8 %unpack.1 = (f32[2,128,1536]{2,1,0:T(8,128)}, f32[2,128,512]{2,1,0:T(8,128)}, f32[2,128,2048]{2,1,0:T(8,128)}, f32[2,512,512]{2,1,0:T(8,128)}) custom-call(s32[1]{0:T(128)} %bitcast.7.info, bf16[8,128,512]{2,1,0:T(8,128)(2,1)} %copy-done.3, bf16[8,192,512]{2,1,0:T(8,128)(2,1)} %copy-done.2, bf16[8,64,512]{2,1,0:T(8,128)(2,1)} %copy-done.5), custom_call_target="tpu_custom_call" | custom-call | tf_op jit(solution)/shard_map/unpack/pallas_call | solution.py:690
  (139 shorter events, 15.8 us)
Async XLA Ops:
  0.6 7.8 %copy-start.6 = (bf16[2,5,8,32,512]{4,3,2,1,0:T(8,128)(2,1)S(1)}, bf16[2,5,8,32,512]{4,3,2,1,0:T(8,128)(2,1)}, u32[]{:S(2)}) copy-start(bf16[2,5,8,32,512]{4,3,2,1,0:T(8,128)(2,1)} %cot_own_ref.1) | copy-start | bytes 7864324
  3.3 7.7 %copy-start.8 = (f32[2,2048]{1,0:T(2,128)S(1)}, f32[2,2048]{1,0:T(2,128)}, u32[]{:S(2)}) copy-start(f32[2,2048]{1,0:T(2,128)} %param.22) | copy-start | bytes 49156
  3.3 7.7 %copy-start.9 = (f32[4,512]{1,0:T(4,128)S(1)}, f32[4,512]{1,0:T(4,128)}, u32[]{:S(2)}) copy-start(f32[4,512]{1,0:T(4,128)} %param.15) | copy-start | bytes 24580
  3.3 7.7 %copy-start.10 = (f32[4,512]{1,0:T(4,128)S(1)}, f32[4,512]{1,0:T(4,128)}, u32[]{:S(2)}) copy-start(f32[4,512]{1,0:T(4,128)} %param.16) | copy-start | bytes 24580
  3.3 7.7 %copy-start.11 = (f32[4,512]{1,0:T(4,128)S(1)}, f32[4,512]{1,0:T(4,128)}, u32[]{:S(2)}) copy-start(f32[4,512]{1,0:T(4,128)} %param.21) | copy-start | bytes 24580
  3.3 34.6 %collective-permute-start = (bf16[2,5,4,32,512]{4,3,2,1,0:T(8,128)(2,1)}, bf16[2,5,4,32,512]{4,3,2,1,0:T(8,128)(2,1)}, u32[]{:S(2)}, u32[]{:S(2)}) collective-permute-start(bf16[2,5,4,32,512]{4,3,2,1,0:T(8,128)(2,1)} %slice.202), channel_id=1, source_target_pairs={{0,3},{1,0},{2,1},{3,2},{4,7},{5,4},{6,5},{7,6},{8,11},{9,8},{10,9... | collective-permute-start | bytes 3932168 | tf_op jit(solution)/shard_map/ppermute | solution.py:710
  9.6 55.3 %collective-permute-start.1 = (bf16[2,5,4,32,512]{4,3,2,1,0:T(8,128)(2,1)}, bf16[2,5,4,32,512]{4,3,2,1,0:T(8,128)(2,1)}, u32[]{:S(2)}, u32[]{:S(2)}) collective-permute-start(bf16[2,5,4,32,512]{4,3,2,1,0:T(8,128)(2,1)} %slice.203), channel_id=1, source_target_pairs={{0,3},{1,0},{2,1},{3,2},{4,7},{5,4},{6,5},{7,6},{8,11},{9,8},{10,9... | collective-permute-start | bytes 3932168 | tf_op jit(solution)/shard_map/ppermute | solution.py:710
  17.3 6.4 %copy-start.1 = (bf16[2,512,1536]{2,1,0:T(8,128)(2,1)S(1)}, bf16[2,512,1536]{2,1,0:T(8,128)(2,1)}, u32[]{:S(2)}) copy-start(bf16[2,512,1536]{2,1,0:T(8,128)(2,1)} %wqkv_ref.3) | copy-start | bytes 9437188
  26.6 2.3 copy-start.12
  26.6 2.3 copy-start.13
  338.1 18.5 %collective-permute-start.33 = (bf16[4,4,64,512]{3,2,1,0:T(8,128)(2,1)}, bf16[4,4,64,512]{3,2,1,0:T(8,128)(2,1)S(1)}, u32[]{:S(2)}, u32[]{:S(2)}) collective-permute-start(bf16[4,4,64,512]{3,2,1,0:T(8,128)(2,1)} %get-tuple-element.53), channel_id=1, source_target_pairs={{0,4},{4,0},{8,12},{12,8},{16,20},{20,16},{24,28},{28,24},{1,5},{5... | collective-permute-start | bytes 3145736 | tf_op jit(solution)/shard_map/ppermute | solution.py:714
  338.2 65.1 %collective-permute-start.11 = (bf16[4,4,128,512]{3,2,1,0:T(8,128)(2,1)}, bf16[4,4,128,512]{3,2,1,0:T(8,128)(2,1)}, u32[]{:S(2)}, u32[]{:S(2)}) collective-permute-start(bf16[4,4,128,512]{3,2,1,0:T(8,128)(2,1)} %get-tuple-element.49), channel_id=1, source_target_pairs={{0,4},{4,0},{8,12},{12,8},{16,20},{20,16},{24,28},{28,24},{1,5},{5... | collective-permute-start | bytes 6291464 | tf_op jit(solution)/shard_map/ppermute | solution.py:714
  342.9 1.3 collective-permute-start.4
  344.2 4.2 collective-permute-start.5
  345.7 4.1 collective-permute-start.6
  347.3 5.0 collective-permute-start.7
  348.3 54.9 %collective-permute-start.3 = (bf16[2,5,4,32,512]{4,3,2,1,0:T(8,128)(2,1)}, bf16[2,5,4,32,512]{4,3,2,1,0:T(8,128)(2,1)}, u32[]{:S(2)}, u32[]{:S(2)}) collective-permute-start(bf16[2,5,4,32,512]{4,3,2,1,0:T(8,128)(2,1)} %get-tuple-element.44), channel_id=1, source_target_pairs={{0,1},{1,2},{2,3},{3,0},{4,5},{5,6},{6,7},{7,4},{8,9},{9,10},{10,1... | collective-permute-start | bytes 3932168 | tf_op jit(solution)/shard_map/ppermute | solution.py:710
  352.3 30.7 %collective-permute-start.10 = (f32[20,512]{1,0:T(8,128)S(1)}, f32[20,512]{1,0:T(8,128)S(1)}, u32[]{:S(2)}, u32[]{:S(2)}) collective-permute-start(f32[20,512]{1,0:T(8,128)S(1)} %add_add_fusion.1), channel_id=1, source_target_pairs={{0,3},{1,2},{2,1},{3,0},{4,7},{5,6},{6,5},{7,4},{8,11},{9,10},{10,... | collective-permute-start | bytes 122888 | tf_op jit(solution)/shard_map/ppermute | solution.py:714
  356.6 27.9 %collective-permute-start.8 = (f32[20,512]{1,0:T(8,128)S(1)}, f32[20,512]{1,0:T(8,128)S(1)}, u32[]{:S(2)}, u32[]{:S(2)}) collective-permute-start(f32[20,512]{1,0:T(8,128)S(1)} %add_add_fusion.1), channel_id=1, source_target_pairs={{0,1},{1,0},{2,3},{3,2},{4,5},{5,4},{6,7},{7,6},{8,9},{9,8},{10,11... | collective-permute-start | bytes 122888 | tf_op jit(solution)/shard_map/ppermute | solution.py:714
  356.6 29.4 %copy-start.4 = (bf16[4,4,64,512]{3,2,1,0:T(8,128)(2,1)}, bf16[4,4,64,512]{3,2,1,0:T(8,128)(2,1)S(1)}, u32[]{:S(2)}) copy-start(bf16[4,4,64,512]{3,2,1,0:T(8,128)(2,1)S(1)} %collective-permute-done.33) | copy-start | bytes 3145732
  356.6 29.4 %collective-permute-start.9 = (f32[20,512]{1,0:T(8,128)S(1)}, f32[20,512]{1,0:T(8,128)S(1)}, u32[]{:S(2)}, u32[]{:S(2)}) collective-permute-start(f32[20,512]{1,0:T(8,128)S(1)} %add_add_fusion.1), channel_id=1, source_target_pairs={{0,2},{1,3},{2,0},{3,1},{4,6},{5,7},{6,4},{7,5},{8,10},{9,11},{10,... | collective-permute-start | bytes 122888 | tf_op jit(solution)/shard_map/ppermute | solution.py:714
  382.9 6.7 %collective-permute-start.34 = (bf16[4,64,512]{2,1,0:T(8,128)(2,1)}, bf16[4,64,512]{2,1,0:T(8,128)(2,1)}, u32[]{:S(2)}, u32[]{:S(2)}) collective-permute-start(bf16[4,64,512]{2,1,0:T(8,128)(2,1)} %get-tuple-element.70), channel_id=1, source_target_pairs={{0,8},{4,12},{8,0},{12,4},{16,24},{20,28},{24,16},{28,20},{1,9},{5... | collective-permute-start | bytes 786440 | tf_op jit(solution)/shard_map/ppermute | solution.py:714
  384.5 7.9 %collective-permute-start.35 = (bf16[4,64,512]{2,1,0:T(8,128)(2,1)}, bf16[4,64,512]{2,1,0:T(8,128)(2,1)}, u32[]{:S(2)}, u32[]{:S(2)}) collective-permute-start(bf16[4,64,512]{2,1,0:T(8,128)(2,1)} %get-tuple-element.72), channel_id=1, source_target_pairs={{0,16},{4,20},{8,24},{12,28},{16,0},{20,4},{24,8},{28,12},{1,17},{... | collective-permute-start | bytes 786440 | tf_op jit(solution)/shard_map/ppermute | solution.py:714
  386.0 0.6 copy-start.7
  386.7 88.3 %collective-permute-start.22 = (bf16[4,4,192,512]{3,2,1,0:T(8,128)(2,1)}, bf16[4,4,192,512]{3,2,1,0:T(8,128)(2,1)S(1)}, u32[]{:S(2)}, u32[]{:S(2)}) collective-permute-start(bf16[4,4,192,512]{3,2,1,0:T(8,128)(2,1)} %get-tuple-element.51), channel_id=1, source_target_pairs={{0,4},{4,0},{8,12},{12,8},{16,20},{20,16},{24,28},{28,24},{1,5},{5... | collective-permute-start | bytes 9437192 | tf_op jit(solution)/shard_map/ppermute | solution.py:714
  389.6 37.3 %collective-permute-start.2 = (bf16[2,5,4,32,512]{4,3,2,1,0:T(8,128)(2,1)}, bf16[2,5,4,32,512]{4,3,2,1,0:T(8,128)(2,1)}, u32[]{:S(2)}, u32[]{:S(2)}) collective-permute-start(bf16[2,5,4,32,512]{4,3,2,1,0:T(8,128)(2,1)} %get-tuple-element.35), channel_id=1, source_target_pairs={{0,1},{1,2},{2,3},{3,0},{4,5},{5,6},{6,7},{7,4},{8,9},{9,10},{10,1... | collective-permute-start | bytes 3932168 | tf_op jit(solution)/shard_map/ppermute | solution.py:710
  392.4 8.0 %collective-permute-start.36 = (bf16[4,64,512]{2,1,0:T(8,128)(2,1)S(1)}, bf16[4,64,512]{2,1,0:T(8,128)(2,1)}, u32[]{:S(2)}, u32[]{:S(2)}) collective-permute-start(bf16[4,64,512]{2,1,0:T(8,128)(2,1)S(1)} %get-tuple-element.71), channel_id=1, source_target_pairs={{0,24},{4,28},{8,16},{12,20},{16,8},{20,12},{24,0},{28,4},{1,25},{... | collective-permute-start | bytes 786440 | tf_op jit(solution)/shard_map/ppermute | solution.py:714
  401.9 21.5 %collective-permute-start.37 = (bf16[64,512]{1,0:T(8,128)(2,1)S(1)}, bf16[64,512]{1,0:T(8,128)(2,1)S(1)}, u32[]{:S(2)}, u32[]{:S(2)}) collective-permute-start(bf16[64,512]{1,0:T(8,128)(2,1)S(1)} %get-tuple-element.79), channel_id=1, source_target_pairs={{0,1},{1,0},{2,3},{3,2},{4,5},{5,4},{6,7},{7,6},{8,9},{9,8},{10,11... | collective-permute-start | bytes 196616 | tf_op jit(solution)/shard_map/ppermute | solution.py:714
  403.2 21.1 %collective-permute-start.38 = (bf16[64,512]{1,0:T(8,128)(2,1)S(1)}, bf16[64,512]{1,0:T(8,128)(2,1)S(1)}, u32[]{:S(2)}, u32[]{:S(2)}) collective-permute-start(bf16[64,512]{1,0:T(8,128)(2,1)S(1)} %get-tuple-element.81), channel_id=1, source_target_pairs={{0,2},{1,3},{2,0},{3,1},{4,6},{5,7},{6,4},{7,5},{8,10},{9,11},{10,... | collective-permute-start | bytes 196616 | tf_op jit(solution)/shard_map/ppermute | solution.py:714
  403.2 22.6 %collective-permute-start.39 = (bf16[64,512]{1,0:T(8,128)(2,1)S(1)}, bf16[64,512]{1,0:T(8,128)(2,1)S(1)}, u32[]{:S(2)}, u32[]{:S(2)}) collective-permute-start(bf16[64,512]{1,0:T(8,128)(2,1)S(1)} %get-tuple-element.80), channel_id=1, source_target_pairs={{0,3},{1,2},{2,1},{3,0},{4,7},{5,6},{6,5},{7,4},{8,11},{9,10},{10,... | collective-permute-start | bytes 196616 | tf_op jit(solution)/shard_map/ppermute | solution.py:714
  406.4 44.1 %copy-start.16 = (bf16[2,5,8,32,512]{4,3,2,1,0:T(8,128)(2,1)S(1)}, bf16[2,5,8,32,512]{4,3,2,1,0:T(8,128)(2,1)}, u32[]{:S(2)}) copy-start(bf16[2,5,8,32,512]{4,3,2,1,0:T(8,128)(2,1)} %get-tuple-element.43) | copy-start | bytes 7864324
  408.9 46.7 %copy-start.14 = (bf16[2,5,8,32,512]{4,3,2,1,0:T(8,128)(2,1)S(1)}, bf16[2,5,8,32,512]{4,3,2,1,0:T(8,128)(2,1)}, u32[]{:S(2)}) copy-start(bf16[2,5,8,32,512]{4,3,2,1,0:T(8,128)(2,1)} %get-tuple-element.34) | copy-start | bytes 7864324
  423.4 36.1 %collective-permute-start.12 = (bf16[4,128,512]{2,1,0:T(8,128)(2,1)S(1)}, bf16[4,128,512]{2,1,0:T(8,128)(2,1)S(1)}, u32[]{:S(2)}, u32[]{:S(2)}) collective-permute-start(bf16[4,128,512]{2,1,0:T(8,128)(2,1)S(1)} %get-tuple-element.67), channel_id=1, source_target_pairs={{0,8},{4,12},{8,0},{12,4},{16,24},{20,28},{24,16},{28,20},{1,9},{5... | collective-permute-start | bytes 1572872 | tf_op jit(solution)/shard_map/ppermute | solution.py:714
  424.3 35.2 %collective-permute-start.13 = (bf16[4,128,512]{2,1,0:T(8,128)(2,1)S(1)}, bf16[4,128,512]{2,1,0:T(8,128)(2,1)S(1)}, u32[]{:S(2)}, u32[]{:S(2)}) collective-permute-start(bf16[4,128,512]{2,1,0:T(8,128)(2,1)S(1)} %get-tuple-element.69), channel_id=1, source_target_pairs={{0,16},{4,20},{8,24},{12,28},{16,0},{20,4},{24,8},{28,12},{1,17},{... | collective-permute-start | bytes 1572872 | tf_op jit(solution)/shard_map/ppermute | solution.py:714
  425.8 33.7 %collective-permute-start.14 = (bf16[4,128,512]{2,1,0:T(8,128)(2,1)S(1)}, bf16[4,128,512]{2,1,0:T(8,128)(2,1)S(1)}, u32[]{:S(2)}, u32[]{:S(2)}) collective-permute-start(bf16[4,128,512]{2,1,0:T(8,128)(2,1)S(1)} %get-tuple-element.68), channel_id=1, source_target_pairs={{0,24},{4,28},{8,16},{12,20},{16,8},{20,12},{24,0},{28,4},{1,25},{... | collective-permute-start | bytes 1572872 | tf_op jit(solution)/shard_map/ppermute | solution.py:714
  426.9 23.0 %collective-permute-start.40 = (bf16[64,512]{1,0:T(8,128)(2,1)S(1)}, bf16[64,512]{1,0:T(8,128)(2,1)S(1)}, u32[]{:S(2)}, u32[]{:S(2)}) collective-permute-start(bf16[64,512]{1,0:T(8,128)(2,1)S(1)} %get-tuple-element.59), channel_id=1, source_target_pairs={{0,8},{4,12},{8,0},{12,4},{16,24},{20,28},{24,16},{28,20},{1,9},{5... | collective-permute-start | bytes 196616 | tf_op jit(solution)/shard_map/ppermute | solution.py:714
  449.9 4.3 collective-permute-start.41
  451.9 7.5 %copy-start.17 = (bf16[2,5,8,32,512]{4,3,2,1,0:T(8,128)(2,1)}, bf16[2,5,8,32,512]{4,3,2,1,0:T(8,128)(2,1)S(1)}, u32[]{:S(2)}) copy-start(bf16[2,5,8,32,512]{4,3,2,1,0:T(8,128)(2,1)S(1)} %constant_dynamic-update-slice_fusion.15) | copy-start | bytes 7864324
  454.2 5.2 collective-permute-start.42
  457.0 2.5 copy-start.15
  459.4 19.9 %collective-permute-start.43 = (bf16[4,64,512]{2,1,0:T(8,128)(2,1)S(1)}, bf16[4,64,512]{2,1,0:T(8,128)(2,1)S(1)}, u32[]{:S(2)}, u32[]{:S(2)}) collective-permute-start(bf16[4,64,512]{2,1,0:T(8,128)(2,1)S(1)} %pad_maximum_fusion.2), channel_id=1, source_target_pairs={{0,4},{4,0},{8,12},{12,8},{16,20},{20,16},{24,28},{28,24},{1,5},{5... | collective-permute-start | bytes 786440 | tf_op jit(solution)/shard_map/ppermute | solution.py:714
  459.5 15.4 %copy-start = (bf16[4,4,192,512]{3,2,1,0:T(8,128)(2,1)S(1)}, bf16[4,4,192,512]{3,2,1,0:T(8,128)(2,1)}, u32[]{:S(2)}) copy-start(bf16[4,4,192,512]{3,2,1,0:T(8,128)(2,1)} %get-tuple-element.50) | copy-start | bytes 9437188
  461.3 7.1 %collective-permute-start.15 = (bf16[128,512]{1,0:T(8,128)(2,1)S(1)}, bf16[128,512]{1,0:T(8,128)(2,1)S(1)}, u32[]{:S(2)}, u32[]{:S(2)}) collective-permute-start(bf16[128,512]{1,0:T(8,128)(2,1)S(1)} %get-tuple-element.76), channel_id=1, source_target_pairs={{0,1},{1,0},{2,3},{3,2},{4,5},{5,4},{6,7},{7,6},{8,9},{9,8},{10,11... | collective-permute-start | bytes 393224 | tf_op jit(solution)/shard_map/ppermute | solution.py:714
  461.4 12.9 %collective-permute-start.16 = (bf16[128,512]{1,0:T(8,128)(2,1)S(1)}, bf16[128,512]{1,0:T(8,128)(2,1)S(1)}, u32[]{:S(2)}, u32[]{:S(2)}) collective-permute-start(bf16[128,512]{1,0:T(8,128)(2,1)S(1)} %get-tuple-element.78), channel_id=1, source_target_pairs={{0,2},{1,3},{2,0},{3,1},{4,6},{5,7},{6,4},{7,5},{8,10},{9,11},{10,... | collective-permute-start | bytes 393224 | tf_op jit(solution)/shard_map/ppermute | solution.py:714
  461.4 12.9 %collective-permute-start.17 = (bf16[128,512]{1,0:T(8,128)(2,1)S(1)}, bf16[128,512]{1,0:T(8,128)(2,1)S(1)}, u32[]{:S(2)}, u32[]{:S(2)}) collective-permute-start(bf16[128,512]{1,0:T(8,128)(2,1)S(1)} %get-tuple-element.77), channel_id=1, source_target_pairs={{0,3},{1,2},{2,1},{3,0},{4,7},{5,6},{6,5},{7,4},{8,11},{9,10},{10,... | collective-permute-start | bytes 393224 | tf_op jit(solution)/shard_map/ppermute | solution.py:714
  474.4 6.8 %collective-permute-start.18 = (bf16[128,512]{1,0:T(8,128)(2,1)S(1)}, bf16[128,512]{1,0:T(8,128)(2,1)S(1)}, u32[]{:S(2)}, u32[]{:S(2)}) collective-permute-start(bf16[128,512]{1,0:T(8,128)(2,1)S(1)} %get-tuple-element.63), channel_id=1, source_target_pairs={{0,8},{4,12},{8,0},{12,4},{16,24},{20,28},{24,16},{28,20},{1,9},{5... | collective-permute-start | bytes 393224 | tf_op jit(solution)/shard_map/ppermute | solution.py:714
  475.7 42.3 %collective-permute-start.23 = (bf16[4,192,512]{2,1,0:T(8,128)(2,1)S(1)}, bf16[4,192,512]{2,1,0:T(8,128)(2,1)S(1)}, u32[]{:S(2)}, u32[]{:S(2)}) collective-permute-start(bf16[4,192,512]{2,1,0:T(8,128)(2,1)S(1)} %get-tuple-element.64), channel_id=1, source_target_pairs={{0,8},{4,12},{8,0},{12,4},{16,24},{20,28},{24,16},{28,20},{1,9},{5... | collective-permute-start | bytes 2359304 | tf_op jit(solution)/shard_map/ppermute | solution.py:714
  477.3 40.8 %collective-permute-start.24 = (bf16[4,192,512]{2,1,0:T(8,128)(2,1)S(1)}, bf16[4,192,512]{2,1,0:T(8,128)(2,1)S(1)}, u32[]{:S(2)}, u32[]{:S(2)}) collective-permute-start(bf16[4,192,512]{2,1,0:T(8,128)(2,1)S(1)} %get-tuple-element.66), channel_id=1, source_target_pairs={{0,16},{4,20},{8,24},{12,28},{16,0},{20,4},{24,8},{28,12},{1,17},{... | collective-permute-start | bytes 2359304 | tf_op jit(solution)/shard_map/ppermute | solution.py:714
  478.1 39.9 %collective-permute-start.25 = (bf16[4,192,512]{2,1,0:T(8,128)(2,1)S(1)}, bf16[4,192,512]{2,1,0:T(8,128)(2,1)S(1)}, u32[]{:S(2)}, u32[]{:S(2)}) collective-permute-start(bf16[4,192,512]{2,1,0:T(8,128)(2,1)S(1)} %get-tuple-element.65), channel_id=1, source_target_pairs={{0,24},{4,28},{8,16},{12,20},{16,8},{20,12},{24,0},{28,4},{1,25},{... | collective-permute-start | bytes 2359304 | tf_op jit(solution)/shard_map/ppermute | solution.py:714
  479.3 38.6 %collective-permute-start.19 = (bf16[128,512]{1,0:T(8,128)(2,1)S(1)}, bf16[128,512]{1,0:T(8,128)(2,1)S(1)}, u32[]{:S(2)}, u32[]{:S(2)}) collective-permute-start(bf16[128,512]{1,0:T(8,128)(2,1)S(1)} %get-tuple-element.63), channel_id=1, source_target_pairs={{0,16},{4,20},{8,24},{12,28},{16,0},{20,4},{24,8},{28,12},{1,17},{... | collective-permute-start | bytes 393224 | tf_op jit(solution)/shard_map/ppermute | solution.py:714
  481.2 36.7 %collective-permute-start.20 = (bf16[128,512]{1,0:T(8,128)(2,1)S(1)}, bf16[128,512]{1,0:T(8,128)(2,1)S(1)}, u32[]{:S(2)}, u32[]{:S(2)}) collective-permute-start(bf16[128,512]{1,0:T(8,128)(2,1)S(1)} %get-tuple-element.63), channel_id=1, source_target_pairs={{0,24},{4,28},{8,16},{12,20},{16,8},{20,12},{24,0},{28,4},{1,25},{... | collective-permute-start | bytes 393224 | tf_op jit(solution)/shard_map/ppermute | solution.py:714
  482.7 35.9 %copy-start.5 = (bf16[8,64,512]{2,1,0:T(8,128)(2,1)}, bf16[8,64,512]{2,1,0:T(8,128)(2,1)S(1)}, u32[]{:S(2)}) copy-start(bf16[8,64,512]{2,1,0:T(8,128)(2,1)S(1)} %constant_dynamic-update-slice_fusion.10.space_ref) | copy-start | bytes 1572868
  517.9 31.7 %collective-permute-start.21 = (bf16[4,128,512]{2,1,0:T(8,128)(2,1)S(1)}, bf16[4,128,512]{2,1,0:T(8,128)(2,1)S(1)}, u32[]{:S(2)}, u32[]{:S(2)}) collective-permute-start(bf16[4,128,512]{2,1,0:T(8,128)(2,1)S(1)} %pad_maximum_fusion.1), channel_id=1, source_target_pairs={{0,4},{4,0},{8,12},{12,8},{16,20},{20,16},{24,28},{28,24},{1,5},{5... | collective-permute-start | bytes 1572872 | tf_op jit(solution)/shard_map/ppermute | solution.py:714
  518.7 12.0 %collective-permute-start.26 = (bf16[192,512]{1,0:T(8,128)(2,1)S(1)}, bf16[192,512]{1,0:T(8,128)(2,1)S(1)}, u32[]{:S(2)}, u32[]{:S(2)}) collective-permute-start(bf16[192,512]{1,0:T(8,128)(2,1)S(1)} %get-tuple-element.73), channel_id=1, source_target_pairs={{0,1},{1,0},{2,3},{3,2},{4,5},{5,4},{6,7},{7,6},{8,9},{9,8},{10,11... | collective-permute-start | bytes 589832 | tf_op jit(solution)/shard_map/ppermute | solution.py:714
  522.1 17.1 %collective-permute-start.27 = (bf16[192,512]{1,0:T(8,128)(2,1)S(1)}, bf16[192,512]{1,0:T(8,128)(2,1)S(1)}, u32[]{:S(2)}, u32[]{:S(2)}) collective-permute-start(bf16[192,512]{1,0:T(8,128)(2,1)S(1)} %get-tuple-element.75), channel_id=1, source_target_pairs={{0,2},{1,3},{2,0},{3,1},{4,6},{5,7},{6,4},{7,5},{8,10},{9,11},{10,... | collective-permute-start | bytes 589832 | tf_op jit(solution)/shard_map/ppermute | solution.py:714
  522.1 17.1 %collective-permute-start.28 = (bf16[192,512]{1,0:T(8,128)(2,1)S(1)}, bf16[192,512]{1,0:T(8,128)(2,1)S(1)}, u32[]{:S(2)}, u32[]{:S(2)}) collective-permute-start(bf16[192,512]{1,0:T(8,128)(2,1)S(1)} %get-tuple-element.74), channel_id=1, source_target_pairs={{0,3},{1,2},{2,1},{3,0},{4,7},{5,6},{6,5},{7,4},{8,11},{9,10},{10,... | collective-permute-start | bytes 589832 | tf_op jit(solution)/shard_map/ppermute | solution.py:714
  539.3 7.7 %collective-permute-start.29 = (bf16[192,512]{1,0:T(8,128)(2,1)S(1)}, bf16[192,512]{1,0:T(8,128)(2,1)S(1)}, u32[]{:S(2)}, u32[]{:S(2)}) collective-permute-start(bf16[192,512]{1,0:T(8,128)(2,1)S(1)} %get-tuple-element.61), channel_id=1, source_target_pairs={{0,8},{4,12},{8,0},{12,4},{16,24},{20,28},{24,16},{28,20},{1,9},{5... | collective-permute-start | bytes 589832 | tf_op jit(solution)/shard_map/ppermute | solution.py:714
  539.9 9.5 %collective-permute-start.30 = (bf16[192,512]{1,0:T(8,128)(2,1)S(1)}, bf16[192,512]{1,0:T(8,128)(2,1)S(1)}, u32[]{:S(2)}, u32[]{:S(2)}) collective-permute-start(bf16[192,512]{1,0:T(8,128)(2,1)S(1)} %get-tuple-element.61), channel_id=1, source_target_pairs={{0,16},{4,20},{8,24},{12,28},{16,0},{20,4},{24,8},{28,12},{1,17},{... | collective-permute-start | bytes 589832 | tf_op jit(solution)/shard_map/ppermute | solution.py:714
  541.1 8.3 %collective-permute-start.31 = (bf16[192,512]{1,0:T(8,128)(2,1)S(1)}, bf16[192,512]{1,0:T(8,128)(2,1)S(1)}, u32[]{:S(2)}, u32[]{:S(2)}) collective-permute-start(bf16[192,512]{1,0:T(8,128)(2,1)S(1)} %get-tuple-element.61), channel_id=1, source_target_pairs={{0,24},{4,28},{8,16},{12,20},{16,8},{20,12},{24,0},{28,4},{1,25},{... | collective-permute-start | bytes 589832 | tf_op jit(solution)/shard_map/ppermute | solution.py:714
  549.5 2.4 collective-permute-start.32
  549.7 2.3 copy-start.3
  552.0 1.2 copy-start.2

commit v2 on v1

v2 whole, which is shorter than its diff:
```python
import functools

import jax
import jax.numpy as jnp
from jax import lax
from jax.experimental import pallas as pl
from jax.experimental.pallas import tpu as pltpu
from jax.sharding import PartitionSpec as P

HEADS = 8
HEAD_DIM = 64
WIN = 8
SHIFT = 4
EPS = 1e-05
NEG = -1e30
SCALE = HEAD_DIM ** (-0.5)
BF16 = jnp.bfloat16
F32 = jnp.float32
NN = (((1,), (0,)), ((), ()))
NT = (((1,), (1,)), ((), ()))
CHUNK = 512
MIB = 1 << 20


def mm(left, right, dims=NN):
    return lax.dot_general(left, right, dims, preferred_element_type=F32)


def wide(column, lanes):
    return jnp.concatenate([column] * (lanes // column.shape[1]), axis=1)


def lane_sum(x):
    total = x[:, :128]
    for k in range(1, x.shape[1] // 128):
        total = total + x[:, 128 * k : 128 * (k + 1)]
    return total


def half_mask(shape):
    return lax.rem(lax.broadcasted_iota(jnp.int32, shape, len(shape) - 1), 128) < 64


def load_frame(own, halo):
    grid = jnp.concatenate([own, halo], axis=0).astype(F32)
    rows, cols, feats = grid.shape
    blocks = grid.reshape(rows, cols // WIN, WIN, feats)
    after = jnp.concatenate([blocks[:, 1:], blocks[:, :1]], axis=1)
    first = lax.broadcasted_iota(jnp.int32, blocks.shape, 2) < SHIFT
    tiles = jnp.where(first, after, blocks).transpose(1, 0, 2, 3)
    return tiles.reshape(rows * cols, feats).astype(BF16).T.astype(F32)


def store_frame(value, own_ref, halo_ref):
    rows = own_ref.shape[2] + halo_ref.shape[2]
    cols, feats = own_ref.shape[3], own_ref.shape[4]
    flat = value.astype(BF16).T.astype(F32)
    tiles = flat.reshape(cols // WIN, rows, WIN, feats).transpose(1, 0, 2, 3)
    before = jnp.concatenate([tiles[:, -1:], tiles[:, :-1]], axis=1)
    first = lax.broadcasted_iota(jnp.int32, tiles.shape, 2) < SHIFT
    grid = jnp.where(first, before, tiles).reshape(rows, cols, feats).astype(BF16)
    own_ref[0, 0] = grid[: own_ref.shape[2]]
    halo_ref[0, 0] = grid[own_ref.shape[2] :]


def norm(x, gain, bias):
    center = x - jnp.mean(x, axis=0, keepdims=True)
    spread = jnp.mean(center * center, axis=0, keepdims=True)
    rstd = lax.rsqrt(spread + EPS)
    xhat = center * rstd
    return xhat, rstd, (xhat * gain + bias).astype(BF16)


def norm_back(d_norm, xhat, rstd, gain):
    grad_gain = d_norm * xhat
    e_mean = jnp.mean(d_norm * gain, axis=0, keepdims=True)
    x_mean = jnp.mean(grad_gain * gain, axis=0, keepdims=True)
    d_hidden = (d_norm * gain - e_mean - xhat * x_mean) * rstd
    return d_hidden, lane_sum(grad_gain), lane_sum(d_norm)


def gelu_parts(pre):
    upper = 0.5 + 0.5 * lax.erf(pre * (0.5**0.5))
    density = jnp.exp(pre * pre * -0.5) * 0.3989422804014327
    return (pre * upper).astype(BF16), upper + pre * density


def head_sum(x):
    return jnp.sum(x.reshape(HEADS, HEAD_DIM, x.shape[1]), axis=1)


def head_spread(p):
    return jnp.broadcast_to(p[:, None, :], (HEADS, HEAD_DIM, p.shape[1])).reshape(
        HEADS * HEAD_DIM, p.shape[1]
    )


def blocks_of(x, left, places):
    zero = jnp.zeros((HEAD_DIM, 128), x.dtype)
    halves = (x[:, :128], x[:, 128:])
    rows = []
    for place in places:
        half = halves[place // 2]
        kept = jnp.where(left, zero, half) if place % 2 else jnp.where(left, half, zero)
        rows.append(jnp.concatenate([zero, kept] if place // 2 else [kept, zero], axis=1))
    return jnp.concatenate(rows, axis=0)


BY_LANES = (0, 1, 2, 3)
BY_ROWS = (0, 2, 1, 3)


def unit_lanes(x, pair, hp):
    cols = slice(128 * pair, 128 * pair + 128)
    first = 128 * hp
    return jnp.concatenate([x[first : first + 64, cols], x[first + 64 : first + 128, cols]], axis=1)


def unit_rows(x, pair, hp):
    dims = slice(128 * hp, 128 * hp + 128)
    first = 128 * pair
    return jnp.concatenate([x[first : first + 64, dims], x[first + 64 : first + 128, dims]], axis=1)


def put_unit(ref, base, pair, hp, value):
    cols = slice(128 * pair, 128 * pair + 128)
    first = base + 128 * hp
    ref[first : first + 64, cols] = value[:, :128]
    ref[first + 64 : first + 128, cols] = value[:, 128:]


def spread_vectors(pieces_ref, space, feed, time, last):
    pieces_ref[...] = jnp.zeros_like(pieces_ref)
    starts = (512, 1024, 0)
    sources = [
        (part, first)
        for kind, first in enumerate(starts)
        for part, first in (
            (space, first),
            (feed, first),
            (time, first),
            (last, (0, 512, 1024)[kind]),
        )
    ]
    for z in range(4):
        rows = [part[0:1, first + 128 * z : first + 128 * z + 128] for part, first in sources]
        for part in (feed, last):
            for m in range(4):
                first = 1536 + 512 * z + 128 * m
                rows.append(part[0:1, first : first + 128])
        for r, row in enumerate(rows):
            pieces_ref[8 * z + r // 3, r % 3 : r % 3 + 1, :] = row


def pack(info, pieces, place, vectors=None):
    me, row = info[0], info[1]
    core, cell = lax.rem(me, 2), lax.div(me, 2)

    def step(i, carry):
        c, z = lax.div(i, 4), lax.rem(i, 4)
        for j in range(4):
            base = 0
            for acc_ref, depth in pieces:
                first = (z ^ row) * (8 * depth) + ((core ^ c) * 4 + (cell ^ j)) * depth
                part = acc_ref[pl.ds(pl.multiple_of(first, 16), depth), :].astype(BF16)
                for k in range(part.shape[1] // 512):
                    place(j, c, z, slice(base, base + depth), part[:, 512 * k : 512 * (k + 1)])
                    base += depth
            if vectors is not None:
                part = vectors[(z ^ row) * 8 + (core ^ c) * 4 + (cell ^ j)].astype(BF16)
                part = jnp.concatenate([part, jnp.zeros((16, 384), BF16)], axis=1)
                place(j, c, z, slice(base, base + 16), part)
        return carry

    lax.fori_loop(0, 8, step, 0)


def row_sums(acc):
    return lax.dot_general(
        jnp.ones((8, 128), F32), acc, NT, precision=lax.Precision.HIGHEST, preferred_element_type=F32
    )


A2, XHAT2, O2, R1_ROWS = 0, 512, 1024, 1536
C1, XHAT1, ACT0, SLOPE0, R3_ROWS = 0, 512, 1024, 3072, 5120
A0, XHAT0, O0, QKV0, P0, R2_ROWS = 0, 512, 1024, 1536, 3072, 3584


def state_kernel(
    info,
    own_ref,
    halo_ref,
    mask_ref,
    vec_ref,
    wqkv_t_ref,
    wproj_t_ref,
    wup_t_ref,
    wdown_t_ref,
    *refs,
    item,
):
    r1_ref, r2_ref, r3_ref, qkv2_ref, p2_ref, stat_ref, x3_ref, kv_ref, scores_ref = refs[-9:]
    frame = pl.program_id(0)
    lanes = r1_ref.shape[2]
    feats = wqkv_t_ref.shape[2]

    def vec(index, size=512):
        return wide(vec_ref[512 * index : 512 * index + size, :], lanes)

    @pl.when(frame == 0)
    def _():
        kv_ref[...] = jnp.zeros_like(kv_ref)

    x0 = load_frame(own_ref[0, 0], halo_ref[0, 0])
    xhat0, rstd0, a0 = norm(x0, vec(0), vec(1))
    r2_ref[0, A0 : A0 + 512, :] = a0
    r2_ref[0, XHAT0 : XHAT0 + 512, :] = xhat0.astype(BF16)
    qkv = mm(wqkv_t_ref[0], a0).astype(BF16)
    r2_ref[0, QKV0 : QKV0 + 1536, :] = qkv
    keys = qkv[512:1024].T
    left = half_mask((64, 128))
    units = [(pair, hp) for pair in range(lanes // 128) for hp in range(HEADS // 2)]
    for n, (pair, hp) in enumerate(units):
        query = blocks_of(unit_lanes(qkv[:512], pair, hp), left, BY_ROWS)
        scores = mm(unit_rows(keys, pair, hp), query) * SCALE
        scores_ref[n] = jnp.where(mask_ref[pair] > 0.5, scores, NEG)
    for n, (pair, hp) in enumerate(units):
        scores = scores_ref[n]
        exponent = jnp.exp(scores - jnp.max(scores, axis=0, keepdims=True))
        weights = exponent * (1.0 / jnp.sum(exponent, axis=0, keepdims=True))
        r2_ref[0, P0 + 64 * n : P0 + 64 * n + 64, :] = weights.astype(BF16)
    for n, (pair, hp) in enumerate(units):
        weights = blocks_of(r2_ref[0, P0 + 64 * n : P0 + 64 * n + 64, :], left, BY_LANES)
        mixed = mm(unit_lanes(qkv[1024:], pair, hp), weights).astype(BF16)
        put_unit(r2_ref.at[0], O0, pair, hp, mixed)
    x1 = x0 + mm(wproj_t_ref[0], r2_ref[0, O0 : O0 + 512, :]) + vec(2)

    xhat1, rstd1, c1 = norm(x1, vec(3), vec(4))
    r3_ref[0, C1 : C1 + 512, :] = c1
    r3_ref[0, XHAT1 : XHAT1 + 512, :] = xhat1.astype(BF16)
    x2 = x1 + vec(5)
    for k in range(wup_t_ref.shape[1] // CHUNK):
        part = slice(CHUNK * k, CHUNK * (k + 1))
        pre = mm(wup_t_ref[0, part, :], c1) + vec(9 + k)
        act, slope = gelu_parts(pre)
        r3_ref[0, ACT0 + CHUNK * k : ACT0 + CHUNK * (k + 1), :] = act
        r3_ref[0, SLOPE0 + CHUNK * k : SLOPE0 + CHUNK * (k + 1), :] = slope.astype(BF16)
        x2 = x2 + mm(wdown_t_ref[0, :, part], act)

    xhat2, rstd2, a2 = norm(x2, vec(6), vec(7))
    r1_ref[0, A2 : A2 + 512, :] = a2
    r1_ref[0, XHAT2 : XHAT2 + 512, :] = xhat2.astype(BF16)
    qkv = mm(wqkv_t_ref[1], a2).astype(BF16)
    qkv2_ref[0] = qkv
    kv_ref[frame] = qkv[512:]
    query = qkv[:512].astype(F32) * SCALE
    scores = []
    for u in range(kv_ref.shape[0]):
        score = head_sum(query * kv_ref[u, :512, :].astype(F32))
        scores.append(jnp.where(u <= frame, score, NEG))
    top = functools.reduce(jnp.maximum, scores)
    exponents = [jnp.exp(s - top) for s in scores]
    scale = 1.0 / sum(exponents)
    mixed = jnp.zeros((feats, lanes), F32)
    for u in range(kv_ref.shape[0]):
        weight = exponents[u] * scale
        p2_ref[0, u] = weight
        weight = weight.astype(BF16).astype(F32)
        mixed = mixed + head_spread(weight) * kv_ref[u, 512:, :].astype(F32)
    o2 = mixed.astype(BF16)
    r1_ref[0, O2 : O2 + 512, :] = o2
    is_video = info[2 + item].astype(F32)
    x3_ref[0] = x2 + is_video * (mm(wproj_t_ref[1], o2) + vec(8))
    stat_ref[0] = jnp.concatenate([rstd0, rstd1, rstd2, jnp.zeros((5, lanes), F32)], axis=0)


def last_kernel(info, items, *refs):
    x3_ref, cot_own_ref, *refs = refs
    cot_halo_refs, refs = refs[:items], refs[items:]
    vec_ref, wup_t_ref, wdown_t_ref, wup_ref, wdown_ref, *refs = refs
    out_own_ref, out_halo_ref, g3_ref, *refs = refs
    keep_ref, send_ref, sums_ref, acc_up, acc_down, acc_vec = refs
    item, frame = pl.program_id(0), pl.program_id(1)
    frames = pl.num_programs(1)
    feats, lanes = g3_ref.shape[1:]

    def vec(index, size=512):
        return wide(vec_ref[512 * index : 512 * index + size, :], lanes)

    @pl.when((item == 0) & (frame == 0))
    def _():
        for acc in (acc_up, acc_down, acc_vec):
            acc[...] = jnp.zeros_like(acc)

    is_valid = jnp.where(frame < info[2 + items + item], 1.0, 0.0)
    halo = cot_halo_refs[0][0, 0]
    for i in range(1, items):
        halo = jnp.where(item == i, cot_halo_refs[i][0, 0], halo)
    g4 = load_frame(cot_own_ref[0, 0], halo) * is_valid
    grad_low = g4.astype(BF16)
    x3 = x3_ref[0]
    xhat3, rstd3, c3 = norm(x3, vec(0), vec(1))
    x4 = x3 + vec(2)
    d_norm = jnp.zeros((feats, lanes), F32)
    for k in range(wup_t_ref.shape[1] // CHUNK):
        part = slice(CHUNK * k, CHUNK * (k + 1))
        pre = mm(wup_t_ref[0, part, :], c3) + vec(3 + k)
        act, slope = gelu_parts(pre)
        x4 = x4 + mm(wdown_t_ref[0, :, part], act)
        d_pre = (mm(wdown_ref[0, part, :], grad_low) * slope).astype(BF16)
        d_norm = d_norm + mm(wup_ref[0, :, part], d_pre)
        acc_up[:, part] += mm(c3, d_pre, NT)
        acc_down[part, :] += mm(act, grad_low, NT)
        acc_vec[1536 + CHUNK * k : 1536 + CHUNK * (k + 1), :] += lane_sum(d_pre.astype(F32))
    store_frame(x4 * is_valid, out_own_ref, out_halo_ref)
    d_hidden, gain_part, bias_part = norm_back(d_norm, xhat3, rstd3, vec(0))
    acc_vec[0:512, :] += gain_part
    acc_vec[512:1024, :] += bias_part
    acc_vec[1024:1536, :] += lane_sum(g4)
    g3_ref[0] = g4 + d_hidden

    @pl.when((item == items - 1) & (frame == frames - 1))
    def _():
        pack(info, [(acc_up, 16), (acc_down, 64)], core_first(keep_ref, send_ref))
        sums_ref[...] = row_sums(acc_vec[...])


def core_first(keep_ref, send_ref):
    def place(j, c, z, rows, value):
        @pl.when(c == 0)
        def _():
            keep_ref[j, z, rows, :] = value

        @pl.when(c == 1)
        def _():
            send_ref[j, z, rows, :] = value

    return place


def time_kernel(
    info,
    g3_ref,
    r1_ref,
    qkv2_ref,
    p2_ref,
    stat_ref,
    vec_ref,
    wqkv_ref,
    wproj_ref,
    g2_ref,
    keep_ref,
    send_ref,
    sums_ref,
    acc_qkv,
    acc_proj,
    acc_vec,
    dkv_ref,
):
    item, step = pl.program_id(0), pl.program_id(1)
    items, frames = pl.num_programs(0), pl.num_programs(1)
    frame = frames - 1 - step
    feats, lanes = g2_ref.shape[1:]

    @pl.when((item == 0) & (step == 0))
    def _():
        for acc in (acc_qkv, acc_proj, acc_vec):
            acc[...] = jnp.zeros_like(acc)

    @pl.when(step == 0)
    def _():
        dkv_ref[...] = jnp.zeros_like(dkv_ref)

    g3 = g3_ref[0]
    is_video = info[2 + item].astype(F32)
    d_attn = (g3 * is_video).astype(BF16)
    acc_proj[...] += mm(r1_ref[0, O2 : O2 + 512, :], d_attn, NT)
    acc_vec[0:512, :] += lane_sum(d_attn.astype(F32))
    d_mixed = mm(wproj_ref[0], d_attn).astype(BF16).astype(F32)
    query = qkv2_ref[frame, :512, :].astype(F32) * SCALE
    count = qkv2_ref.shape[0]
    weights = [p2_ref[0, u] for u in range(count)]
    d_weights = []
    for u in range(count):
        d_weights.append(head_sum(d_mixed * qkv2_ref[u, 1024:, :].astype(F32)))
    inner = sum(w * d for w, d in zip(weights, d_weights))
    d_query = jnp.zeros((feats, lanes), F32)
    for u in range(count):
        d_score = (weights[u] * (d_weights[u] - inner)).astype(BF16).astype(F32)
        spread = head_spread(d_score)
        d_query = d_query + spread * qkv2_ref[u, 512:1024, :].astype(F32)
        dkv_ref[u, :512, :] += spread * query
        dkv_ref[u, 512:, :] += head_spread(weights[u].astype(BF16).astype(F32)) * d_mixed
    d_qkv = jnp.concatenate(
        [(d_query * SCALE).astype(BF16), dkv_ref[frame].astype(BF16)], axis=0
    )
    acc_qkv[...] += mm(r1_ref[0, A2 : A2 + 512, :], d_qkv, NT)
    d_norm = mm(wqkv_ref[0], d_qkv)
    xhat = r1_ref[0, XHAT2 : XHAT2 + 512, :].astype(F32)
    gain = wide(vec_ref[...], lanes)
    d_hidden, gain_part, bias_part = norm_back(d_norm, xhat, stat_ref[0, 2:3, :], gain)
    acc_vec[512:1024, :] += gain_part
    acc_vec[1024:1536, :] += bias_part
    g2_ref[0] = g3 + d_hidden

    @pl.when((item == items - 1) & (step == frames - 1))
    def _():
        pack(info, [(acc_qkv, 16), (acc_proj, 16)], core_first(keep_ref, send_ref))
        sums_ref[...] = row_sums(acc_vec[...])


def feed_kernel(info, g2_ref, r3_ref, stat_ref, vec_ref, wup_ref, wdown_ref, *refs, passes):
    g1_ref, keep_ref, send_ref, sums_ref = refs[passes : passes + 4]
    acc_up, acc_down, acc_vec = refs[-3:]
    plane, planes = pl.program_id(0), pl.num_programs(0)
    feats, lanes = g1_ref.shape[1:]

    @pl.when(plane == 0)
    def _():
        for acc in (acc_up, acc_down, acc_vec):
            acc[...] = jnp.zeros_like(acc)

    g2 = g2_ref[0]
    grad_low = g2.astype(BF16)
    acc_vec[0:512, :] += lane_sum(grad_low.astype(F32))
    c1 = r3_ref[0, C1 : C1 + 512, :]
    d_norm = jnp.zeros((feats, lanes), F32)
    for k in range(wup_ref.shape[2] // CHUNK):
        part = slice(CHUNK * k, CHUNK * (k + 1))
        slope = r3_ref[0, SLOPE0 + CHUNK * k : SLOPE0 + CHUNK * (k + 1), :].astype(F32)
        d_pre = (mm(wdown_ref[0, part, :], grad_low) * slope).astype(BF16)
        d_norm = d_norm + mm(wup_ref[0, :, part], d_pre)
        acc_up[:, part] += mm(c1, d_pre, NT)
        acc_down[part, :] += mm(
            r3_ref[0, ACT0 + CHUNK * k : ACT0 + CHUNK * (k + 1), :], grad_low, NT
        )
        acc_vec[1536 + CHUNK * k : 1536 + CHUNK * (k + 1), :] += lane_sum(d_pre.astype(F32))
    xhat = r3_ref[0, XHAT1 : XHAT1 + 512, :].astype(F32)
    gain = wide(vec_ref[...], lanes)
    d_hidden, gain_part, bias_part = norm_back(d_norm, xhat, stat_ref[0, 1:2, :], gain)
    acc_vec[512:1024, :] += gain_part
    acc_vec[1024:1536, :] += bias_part
    g1_ref[0] = g2 + d_hidden

    @pl.when(plane == planes - 1)
    def _():
        pack(info, [(acc_up, 16), (acc_down, 64)], core_first(keep_ref, send_ref))
        sums_ref[...] = row_sums(acc_vec[...])


def core_first(keep_ref, send_ref):
    def place(j, c, z, rows, value):
        @pl.when(c == 0)
        def _():
            keep_ref[j, z, rows, :] = value

        @pl.when(c == 1)
        def _():
            send_ref[j, z, rows, :] = value

    return place


def middle_kernel(
    info,
    g3_ref,
    r1_ref,
    qkv2_ref,
    p2_ref,
    stat_ref,
    vec_ref,
    wqkv_ref,
    wproj_ref,
    wup_ref,
    wdown_ref,
    g1_ref,
    keep_ref,
    send_ref,
    sums_ref,
    acc_up,
    acc_down,
    acc_qkv,
    acc_proj,
    acc_vec,
    dkv_ref,
):
    item, step = pl.program_id(0), pl.program_id(1)
    items, frames = pl.num_programs(0), pl.num_programs(1)
    frame = frames - 1 - step
    lanes = r1_ref.shape[2]
    feats = wqkv_ref.shape[1]

    def vec(index, size=512):
        return wide(vec_ref[512 * index : 512 * index + size, :], lanes)

    @pl.when((item == 0) & (step == 0))
    def _():
        for acc in (acc_up, acc_down, acc_qkv, acc_proj, acc_vec):
            acc[...] = jnp.zeros_like(acc)

    @pl.when(step == 0)
    def _():
        dkv_ref[...] = jnp.zeros_like(dkv_ref)

    g3 = g3_ref[0]
    is_video = info[2 + item].astype(F32)
    d_attn = (g3 * is_video).astype(BF16)
    acc_proj[...] += mm(r1_ref[0, O2 : O2 + 512, :], d_attn, NT)
    acc_vec[0:512, :] += lane_sum(d_attn.astype(F32))
    d_mixed = mm(wproj_ref[0], d_attn).astype(BF16).astype(F32)
    query = qkv2_ref[frame, :512, :].astype(F32) * SCALE
    count = qkv2_ref.shape[0]
    weights = [p2_ref[0, u] for u in range(count)]
    d_weights = []
    for u in range(count):
        d_weights.append(head_sum(d_mixed * qkv2_ref[u, 1024:, :].astype(F32)))
    inner = sum(w * d for w, d in zip(weights, d_weights))
    d_query = jnp.zeros((feats, lanes), F32)
    for u in range(count):
        d_score = (weights[u] * (d_weights[u] - inner)).astype(BF16).astype(F32)
        spread = head_spread(d_score)
        d_query = d_query + spread * qkv2_ref[u, 512:1024, :].astype(F32)
        dkv_ref[u, :512, :] += spread * query
        dkv_ref[u, 512:, :] += head_spread(weights[u].astype(BF16).astype(F32)) * d_mixed
    d_qkv = jnp.concatenate(
        [(d_query * SCALE).astype(BF16), dkv_ref[frame].astype(BF16)], axis=0
    )
    acc_qkv[...] += mm(r1_ref[0, A2 : A2 + 512, :], d_qkv, NT)
    d_norm = mm(wqkv_ref[0], d_qkv)
    xhat = r1_ref[0, XHAT2 : XHAT2 + 512, :].astype(F32)
    d_hidden, gain_part, bias_part = norm_back(d_norm, xhat, stat_ref[0, 2:3, :], vec(1))
    acc_vec[512:1024, :] += gain_part
    acc_vec[1024:1536, :] += bias_part
    g2 = g3 + d_hidden

    grad_low = g2.astype(BF16)
    acc_vec[1536:2048, :] += lane_sum(grad_low.astype(F32))
    c1 = r1_ref[0, C1 : C1 + 512, :]
    d_norm = jnp.zeros((feats, lanes), F32)
    for k in range(wup_ref.shape[2] // CHUNK):
        part = slice(CHUNK * k, CHUNK * (k + 1))
        slope = r1_ref[0, SLOPE0 + CHUNK * k : SLOPE0 + CHUNK * (k + 1), :].astype(F32)
        d_pre = (mm(wdown_ref[0, part, :], grad_low) * slope).astype(BF16)
        d_norm = d_norm + mm(wup_ref[0, :, part], d_pre)
        acc_up[:, part] += mm(c1, d_pre, NT)
        acc_down[part, :] += mm(
            r1_ref[0, ACT0 + CHUNK * k : ACT0 + CHUNK * (k + 1), :], grad_low, NT
        )
        acc_vec[3072 + CHUNK * k : 3072 + CHUNK * (k + 1), :] += lane_sum(d_pre.astype(F32))
    xhat = r1_ref[0, XHAT1 : XHAT1 + 512, :].astype(F32)
    d_hidden, gain_part, bias_part = norm_back(d_norm, xhat, stat_ref[0, 1:2, :], vec(0))
    acc_vec[2048:2560, :] += gain_part
    acc_vec[2560:3072, :] += bias_part
    g1_ref[0] = g2 + d_hidden

    @pl.when((item == items - 1) & (step == frames - 1))
    def _():
        pieces = [(acc_up, 16), (acc_down, 64), (acc_qkv, 16), (acc_proj, 16)]
        pack(info, pieces, core_first(keep_ref, send_ref))
        sums_ref[...] = row_sums(acc_vec[...])


def space_kernel(info, g1_ref, r2_ref, stat_ref, vec_ref, wqkv_ref, wproj_ref, *refs, first, last, passes):
    dqkv_ref, refs = refs[-1], refs[:-1]
    if not first:
        (qkv_in, proj_in, vec_in, _), refs = refs[:4], refs[4:]
    if last:
        (last_sums, time_sums, feed_sums), refs = refs[:3], refs[3:]
    out_own_ref, out_halo_ref, *refs = refs[passes:]
    if last:
        keep_ref, send_ref, *refs = refs
        *refs, vec_pieces = refs[passes:]
    acc_qkv, acc_proj, acc_vec = refs[:3]
    frame = pl.program_id(0)
    frames = pl.num_programs(0)
    lanes = r2_ref.shape[2]

    @pl.when(frame == 0)
    def _():
        for k, acc in enumerate((acc_qkv, acc_proj, acc_vec)):
            acc[...] = jnp.zeros_like(acc) if first else (qkv_in, proj_in, vec_in)[k][...]

    g1 = g1_ref[0]
    d_attn = g1.astype(BF16)
    acc_proj[...] += mm(r2_ref[0, O0 : O0 + 512, :], d_attn, NT)
    acc_vec[0:512, :] += lane_sum(d_attn.astype(F32))
    d_mixed = mm(wproj_ref[0], d_attn).astype(BF16)
    values = r2_ref[0, QKV0 + 1024 : QKV0 + 1536, :].T
    left = half_mask((64, 128))
    units = [(pair, hp) for pair in range(lanes // 128) for hp in range(HEADS // 2)]
    for n, (pair, hp) in enumerate(units):
        grad = unit_lanes(d_mixed, pair, hp)
        d_weights = mm(unit_rows(values, pair, hp), blocks_of(grad, left, BY_ROWS))
        low = r2_ref[0, P0 + 64 * n : P0 + 64 * n + 64, :]
        weights = low.astype(F32)
        inner = jnp.sum(weights * d_weights, axis=0, keepdims=True)
        d_scores = (weights * (d_weights - inner)).astype(BF16)
        slope = blocks_of(d_scores, left, BY_LANES)
        soft = blocks_of(low, left, BY_LANES)
        query = unit_lanes(r2_ref[0, QKV0 : QKV0 + 512, :], pair, hp)
        key = unit_lanes(r2_ref[0, QKV0 + 512 : QKV0 + 1024, :], pair, hp)
        put_unit(dqkv_ref, 0, pair, hp, (mm(key, slope) * SCALE).astype(BF16))
        put_unit(dqkv_ref, 512, pair, hp, (mm(query, slope, NT) * SCALE).astype(BF16))
        put_unit(dqkv_ref, 1024, pair, hp, mm(grad, soft, NT).astype(BF16))
    d_qkv = dqkv_ref[...]
    acc_qkv[...] += mm(r2_ref[0, A0 : A0 + 512, :], d_qkv, NT)
    d_norm = mm(wqkv_ref[0], d_qkv)
    xhat = r2_ref[0, XHAT0 : XHAT0 + 512, :].astype(F32)
    gain = wide(vec_ref[...], lanes)
    d_hidden, gain_part, bias_part = norm_back(d_norm, xhat, stat_ref[0, 0:1, :], gain)
    acc_vec[512:1024, :] += gain_part
    acc_vec[1024:1536, :] += bias_part
    store_frame(g1 + d_hidden, out_own_ref, out_halo_ref)

    if last:

        @pl.when(frame == frames - 1)
        def _():
            spread_vectors(
                vec_pieces, row_sums(acc_vec[...]), feed_sums[...], time_sums[...], last_sums[...]
            )
            place = core_first(keep_ref, send_ref)
            pack(info, [(acc_qkv, 16), (acc_proj, 16)], place, vec_pieces)


def put_rows(out_ref, slot, pieces, base, depth):
    for k in range(out_ref.shape[2] // 512):
        rows = pieces[base + depth * k : base + depth * (k + 1), :]
        out_ref[slot, :, 512 * k : 512 * (k + 1)] = rows.astype(F32)


EARLY_ROWS, LATE_ROWS = 192, 208


def unpack_early_kernel(info, mine_ref, other_ref, up_ref, down_ref, qkv_ref, proj_ref):
    pieces = jnp.where(pl.program_id(0) // 4 == info[0], mine_ref[0], other_ref[0])
    put_rows(up_ref, 0, pieces, 0, 16)
    put_rows(down_ref, 0, pieces, 64, 64)
    put_rows(qkv_ref, 0, pieces, 128, 16)
    put_rows(proj_ref, 0, pieces, 176, 16)


def unpack_late_kernel(info, mine_ref, other_ref, *refs):
    up_ref, down_ref, qkv_ref, proj_ref, gain_ref, bias_ref, outb_ref, upb_ref, vec_ref = refs[-9:]
    place = pl.program_id(0)
    pieces = jnp.where(place // 4 == info[0], mine_ref[0], other_ref[0])
    put_rows(up_ref, 0, pieces, 0, 16)
    put_rows(down_ref, 0, pieces, 64, 64)
    put_rows(qkv_ref, 0, pieces, 128, 16)
    put_rows(proj_ref, 0, pieces, 176, 16)
    vec_ref[place] = pieces[192:208, :128].astype(F32)

    @pl.when(place == 7)
    def _():
        for k, ref in enumerate((gain_ref, bias_ref, outb_ref)):
            for n in range(4):
                r = 4 * k + n
                ref[n : n + 1, :] = vec_ref[r // 3, r % 3 : r % 3 + 1, :]
        for k in range(2):
            for m in range(4):
                r = 12 + 4 * k + m
                upb_ref[k : k + 1, 128 * m : 128 * m + 128] = vec_ref[r // 3, r % 3 : r % 3 + 1, :]


def split_sum_kernel(groups, *refs):
    counts = [(len(g), g[0].shape[0]) for g in groups]
    ins, outs = refs[: sum(c for c, _ in counts)], refs[sum(c for c, _ in counts) :]
    for count, pieces in counts:
        for k in range(pieces):
            total = ins[0][k].astype(F32)
            for ref in ins[1:count]:
                total = total + ref[k].astype(F32)
            outs[k][...] = total.astype(BF16)
        ins, outs = ins[count:], outs[pieces:]


def join_sum_kernel(counts, *refs):
    base = 0
    for count in counts:
        total = refs[0][...].astype(F32)
        for ref in refs[1:count]:
            total = total + ref[...].astype(F32)
        refs[-1][base : base + total.shape[0], :] = total.astype(BF16)
        base += total.shape[0]
        refs = refs[count:]


def stack_kernel(*refs):
    for k, ref in enumerate(refs[:-1]):
        refs[-1][k] = ref[...]


def whole_spec(shape, single=True):
    mode = pl.Buffered(1) if single else None
    return pl.BlockSpec(shape, lambda *_: (0,) * len(shape), pipeline_mode=mode)


def part_spec(shape, index):
    def place(*_):
        return (index,) + (0,) * (len(shape) - 1)

    return pl.BlockSpec((1,) + tuple(shape[1:]), place, pipeline_mode=pl.Buffered(1))


def params(axes, limit=56 * MIB):
    return pltpu.CompilerParams(
        dimension_semantics=("arbitrary",) * axes, vmem_limit_bytes=limit
    )


def cost(flops, moved):
    return pl.CostEstimate(flops=int(flops), bytes_accessed=int(moved), transcendentals=0)


def sds(shape, dtype):
    return jax.ShapeDtypeStruct(shape, dtype)


ANY = pl.BlockSpec(memory_space=pl.ANY)


def run_state(info, item, tokens, halo, mask, vecs, weights, before):
    wqkv_t, wproj_t, wup_t, wdown_t = weights
    items, frames, grid_rows, cols, feats = tokens.shape
    lanes = grid_rows * cols
    planes = items * frames
    half = (1, 1, SHIFT, cols, feats)

    def plane_spec(*shape):
        return pl.BlockSpec(
            (1,) + shape, lambda t, info: (item * frames + t,) + (0,) * len(shape)
        )

    shapes = [
        (R1_ROWS, lanes, BF16),
        (R2_ROWS, lanes, BF16),
        (R3_ROWS, lanes, BF16),
        (3 * feats, lanes, BF16),
        (frames, HEADS, lanes, F32),
        (8, lanes, F32),
        (feats, lanes, F32),
    ]
    operands = [info, tokens, halo, mask, vecs, wqkv_t, wproj_t, wup_t, wdown_t]
    start = len(operands)
    return pl.pallas_call(
        functools.partial(state_kernel, item=item),
        grid_spec=pltpu.PrefetchScalarGridSpec(
            num_scalar_prefetch=1,
            grid=(frames,),
            in_specs=[
                pl.BlockSpec(half, lambda t, info: (item, t, 1, 0, 0)),
                pl.BlockSpec(half, lambda t, info: (0, t, 0, 0, 0)),
                whole_spec(mask.shape),
                whole_spec(vecs.shape),
                whole_spec(wqkv_t.shape),
                whole_spec(wproj_t.shape),
                part_spec(wup_t.shape, 0),
                part_spec(wdown_t.shape, 0),
            ]
            + [ANY] * len(before),
            out_specs=[plane_spec(*s[:-1]) for s in shapes],
            scratch_shapes=[
                pltpu.VMEM((frames, 2 * feats, lanes), BF16),
                pltpu.VMEM((lanes // 128 * (HEADS // 2), 64, 256), F32),
            ],
        ),
        out_shape=[sds((planes,) + s[:-1], s[-1]) for s in shapes],
        input_output_aliases={start + k: k for k in range(len(before))},
        compiler_params=params(1, 40 * MIB),
        cost_estimate=cost(11e9 * 2, 50e6),
        name="state",
    )(*operands, *before)


def run_last(info, x3, cotangent, cot_halos, vecs, weights):
    wup_t, wdown_t, wup, wdown = weights
    items, frames, grid_rows, cols, feats = cotangent.shape
    planes, _, lanes = x3.shape
    hidden = wup.shape[2]
    half = (1, 1, SHIFT, cols, feats)
    own_spec = pl.BlockSpec(half, lambda i, t, info: (i, t, 1, 0, 0))
    halo_spec = pl.BlockSpec(half, lambda i, t, info: (i, t, 0, 0, 0))

    def item_halo(k):
        def place(i, t, info):
            return (0, jnp.where(i == k, t, jnp.where(i < k, 0, frames - 1)), 0, 0, 0)

        return pl.BlockSpec(half, place)

    plane = pl.BlockSpec((1, feats, lanes), lambda i, t, info: (i * frames + t, 0, 0))
    return pl.pallas_call(
        lambda info, *refs: last_kernel(info, items, *refs),
        grid_spec=pltpu.PrefetchScalarGridSpec(
            num_scalar_prefetch=1,
            grid=(items, frames),
            in_specs=[plane, own_spec]
            + [item_halo(k) for k in range(items)]
            + [
                whole_spec(vecs.shape),
                part_spec(wup_t.shape, 1),
                part_spec(wdown_t.shape, 1),
                part_spec(wup.shape, 1),
                part_spec(wdown.shape, 1),
            ],
            out_specs=[own_spec, halo_spec, plane]
            + [whole_spec((4, 4, 128, 512))] * 2
            + [whole_spec((8, 3584))],
            scratch_shapes=[
                pltpu.VMEM((feats, hidden), F32),
                pltpu.VMEM((hidden, feats), F32),
                pltpu.VMEM((3584, 128), F32),
            ],
        ),
        out_shape=[
            sds(cotangent.shape, BF16),
            sds((items, frames, SHIFT, cols, feats), BF16),
            sds((planes, feats, lanes), F32),
        ]
        + [sds((4, 4, 128, 512), BF16)] * 2
        + [sds((8, 3584), F32)],
        compiler_params=params(2, 44 * MIB),
        cost_estimate=cost(32e9 * 1.2, 40e6),
        name="last",
    )(info, x3, cotangent, *cot_halos, vecs, wup_t, wdown_t, wup, wdown)


def run_time(info, g3, r1, qkv2, p2, stats, vecs, weights, items):
    wqkv, wproj = weights
    planes, feats, lanes = g3.shape
    frames = planes // items

    def plane_spec(*shape):
        return pl.BlockSpec(
            (1,) + shape,
            lambda i, s, info: (i * frames + frames - 1 - s,) + (0,) * len(shape),
        )

    return pl.pallas_call(
        time_kernel,
        grid_spec=pltpu.PrefetchScalarGridSpec(
            num_scalar_prefetch=1,
            grid=(items, frames),
            in_specs=[
                plane_spec(feats, lanes),
                plane_spec(R1_ROWS, lanes),
                pl.BlockSpec((frames, 3 * feats, lanes), lambda i, s, info: (i, 0, 0)),
                plane_spec(frames, HEADS, lanes),
                plane_spec(8, lanes),
                whole_spec(vecs.shape),
                part_spec(wqkv.shape, 1),
                part_spec(wproj.shape, 1),
            ],
            out_specs=[
                plane_spec(feats, lanes),
                whole_spec((4, 4, 64, 512)),
                whole_spec((4, 4, 64, 512)),
                whole_spec((8, 1536)),
            ],
            scratch_shapes=[
                pltpu.VMEM((feats, 3 * feats), F32),
                pltpu.VMEM((feats, feats), F32),
                pltpu.VMEM((1536, 128), F32),
                pltpu.VMEM((frames, 2 * feats, lanes), F32),
            ],
        ),
        out_shape=[
            sds((planes, feats, lanes), F32),
            sds((4, 4, 64, 512), BF16),
            sds((4, 4, 64, 512), BF16),
            sds((8, 1536), F32),
        ],
        compiler_params=params(2, 40 * MIB),
        cost_estimate=cost(30e9, 40e6),
        name="time",
    )(info, g3, r1, qkv2, p2, stats, vecs, wqkv, wproj)


def run_feed(info, g2, r3, stats, vecs, weights, passes):
    wup, wdown = weights
    planes, feats, lanes = g2.shape
    hidden = wup.shape[2]

    def plane_spec(*shape):
        return pl.BlockSpec((1,) + shape, lambda n, info: (n,) + (0,) * len(shape))

    return pl.pallas_call(
        functools.partial(feed_kernel, passes=len(passes)),
        grid_spec=pltpu.PrefetchScalarGridSpec(
            num_scalar_prefetch=1,
            grid=(planes,),
            in_specs=[
                plane_spec(feats, lanes),
                plane_spec(R3_ROWS, lanes),
                plane_spec(8, lanes),
                whole_spec(vecs.shape),
                part_spec(wup.shape, 0),
                part_spec(wdown.shape, 0),
            ]
            + [ANY] * len(passes),
            out_specs=[
                plane_spec(feats, lanes),
                whole_spec((4, 4, 128, 512)),
                whole_spec((4, 4, 128, 512)),
                whole_spec((8, 3584)),
            ]
            + [ANY] * len(passes),
            scratch_shapes=[
                pltpu.VMEM((feats, hidden), F32),
                pltpu.VMEM((hidden, feats), F32),
                pltpu.VMEM((3584, 128), F32),
            ],
        ),
        out_shape=[
            sds((planes, feats, lanes), F32),
            sds((4, 4, 128, 512), BF16),
            sds((4, 4, 128, 512), BF16),
            sds((8, 3584), F32),
        ]
        + [sds(p.shape, p.dtype) for p in passes],
        input_output_aliases={7 + k: 4 + k for k in range(len(passes))},
        compiler_params=params(1, 44 * MIB),
        cost_estimate=cost(30e9, 40e6),
        name="feed",
    )(info, g2, r3, stats, vecs, wup, wdown, *passes)


def run_space(info, item, g1, r2, stats, vecs, weights, shape, before, sums, passes):
    wqkv, wproj = weights
    items, frames, grid_rows, cols, feats = shape
    planes, _, lanes = g1.shape
    half = (1, 1, SHIFT, cols, feats)
    first, last = item == 0, item == items - 1

    def plane_spec(*tail):
        return pl.BlockSpec(
            (1,) + tail, lambda t, info: (item * frames + t,) + (0,) * len(tail)
        )

    accs = [(feats, 3 * feats), (feats, feats), (1536, 128)]
    halves = [(4, 4, 80, 512), (4, 4, 80, 512)]
    in_specs = [
        plane_spec(feats, lanes),
        plane_spec(R2_ROWS, lanes),
        plane_spec(8, lanes),
        whole_spec(vecs.shape),
        part_spec(wqkv.shape, 0),
        part_spec(wproj.shape, 0),
    ]
    operands = [info, g1, r2, stats, vecs, wqkv, wproj]
    aliases = {}
    if not first:
        in_specs += [whole_spec(a) for a in accs] + [ANY]
        aliases = {len(operands) + 3: 0}
    in_specs += [whole_spec(v.shape) for v in sums]
    start = len(in_specs) + 1
    in_specs += [ANY] * len(passes)
    out_specs = [
        pl.BlockSpec(half, lambda t, info: (item, t, 1, 0, 0)),
        pl.BlockSpec(half, lambda t, info: (0, t, 0, 0, 0)),
    ]
    out_shape = [sds(shape, BF16), sds((1, frames, SHIFT, cols, feats), BF16)]
    scratch = []
    if last:
        out_specs += [whole_spec(h) for h in halves]
        out_shape += [sds(h, BF16) for h in halves]
        scratch += [pltpu.VMEM(a, F32) for a in accs] + [pltpu.VMEM((32, 16, 128), F32)]
    else:
        out_specs += [whole_spec(a) for a in accs]
        out_shape += [sds(a, F32) for a in accs]
    aliases.update({start + k: len(out_specs) + k for k in range(len(passes))})
    out_specs += [ANY] * len(passes)
    out_shape += [sds(p.shape, p.dtype) for p in passes]
    return pl.pallas_call(
        functools.partial(space_kernel, first=first, last=last, passes=len(passes)),
        grid_spec=pltpu.PrefetchScalarGridSpec(
            num_scalar_prefetch=1,
            grid=(frames,),
            in_specs=in_specs,
            out_specs=out_specs,
            scratch_shapes=scratch + [pltpu.VMEM((3 * feats, lanes), BF16)],
        ),
        out_shape=out_shape,
        input_output_aliases=aliases,
        compiler_params=params(1, 32 * MIB),
        cost_estimate=cost(7e9 * 2, 30e6),
        name="space",
    )(*operands, *before, *sums, *passes)


def run_unpack(info, chip, other, outs):
    rows = chip.shape[1]
    slot = 0 if outs else 1

    def out(depth, width):
        return pl.BlockSpec((1, depth, width), lambda q, info: (slot, q, 0))

    def piece(q, info):
        return (lax.rem(q, 4) ^ info[1], 0, 0)

    shapes = [(2, 128, 2048), (2, 512, 512), (2, 128, 1536), (2, 128, 512)]
    specs = [out(16, 2048), out(64, 512), out(16, 1536), out(16, 512)]
    small = [(4, 128), (4, 128), (4, 128), (2, 512)] if outs else []
    return pl.pallas_call(
        unpack_late_kernel if outs else unpack_early_kernel,
        grid_spec=pltpu.PrefetchScalarGridSpec(
            num_scalar_prefetch=1,
            grid=(8,),
            in_specs=[pl.BlockSpec((1, rows, 512), piece)] * 2 + [ANY] * len(outs),
            out_specs=specs + [whole_spec(a) for a in small],
            scratch_shapes=[pltpu.VMEM((8, 16, 128), F32)] if outs else [],
        ),
        out_shape=[sds(a, F32) for a in shapes + small],
        input_output_aliases={3 + k: k for k in range(len(outs))},
        compiler_params=params(1, 16 * MIB),
        cost_estimate=cost(0, 6e6),
        name="unpack",
    )(info, chip, other, *outs)


def split_sum(*groups):
    size = sum(a.size for g in groups for a in g)
    depths = [g[0].shape[-2] for g in groups]
    steps = next(n for n in (5, 4, 1) if all(d % (16 * n) == 0 for d in depths))

    def spec(shape):
        block = shape[:-2] + (shape[-2] // steps, shape[-1])
        return pl.BlockSpec(block, lambda i: (0,) * (len(shape) - 2) + (i, 0))

    ins = [a for g in groups for a in g]
    outs = [g[0].shape[1:] for g in groups for _ in range(g[0].shape[0])]
    flat = pl.pallas_call(
        functools.partial(split_sum_kernel, groups),
        grid=(steps,),
        in_specs=[spec(a.shape) for a in ins],
        out_specs=[spec(o) for o in outs],
        out_shape=[sds(o, BF16) for o in outs],
        compiler_params=params(1, 24 * MIB),
        cost_estimate=cost(size, 3 * size),
        name="split_sum",
    )(*ins)
    result = []
    for g in groups:
        result.append(flat[: g[0].shape[0]])
        flat = flat[g[0].shape[0] :]
    return result


def join_sum(*groups):
    ins = [a for g in groups for a in g]
    rows = sum(g[0].shape[0] for g in groups)
    return pl.pallas_call(
        functools.partial(join_sum_kernel, [len(g) for g in groups]),
        out_shape=sds((rows, 512), BF16),
        compiler_params=params(0, 16 * MIB),
        name="join_sum",
    )(*ins)


def run_stack(*arrays):
    shape = (len(arrays),) + arrays[0].shape
    return pl.pallas_call(
        stack_kernel, out_shape=sds(shape, BF16), compiler_params=params(0, 16 * MIB), name="stack"
    )(*arrays)


def after(values, *others):
    count = len(values)
    return pl.pallas_call(
        lambda *refs: None,
        in_specs=[ANY] * (count + len(others)),
        out_specs=[ANY] * count,
        out_shape=[sds(v.shape, v.dtype) for v in values],
        input_output_aliases={k: k for k in range(count)},
        compiler_params=params(0, 1 * MIB),
        name="after",
    )(*values, *others)


def shift(block, axis, distance):
    size = lax.axis_size(axis)
    return lax.ppermute(block, axis, [(i, (i + distance) % size) for i in range(size)])


def swap(block, axis, bits):
    return lax.ppermute(block, axis, [(i, i ^ bits) for i in range(lax.axis_size(axis))])


def upper_bits(total):
    bit = 8
    while bit < lax.axis_size("dp"):
        total = (total.astype(F32) + swap(total, "dp", bit).astype(F32)).astype(BF16)
        bit *= 2
    return total


def region_label(index, extent):
    return jnp.where(index < extent - WIN, 0, jnp.where(index < extent - SHIFT, 1, 2))


def tile_mask(cols):
    height = lax.axis_size("rows") * WIN
    row_label = region_label(lax.axis_index("rows") * WIN + jnp.arange(WIN), height)
    place = (jnp.arange(WIN) + SHIFT) % WIN
    col_label = region_label(jnp.arange(0, cols, WIN)[:, None] + place, cols)
    label = (row_label[None, :, None] * 3 + col_label[:, None, :]).reshape(-1, WIN * WIN)
    same = (label[:, :, None] == label[:, None, :]).astype(F32)
    pairs = same.reshape(-1, 2, WIN * WIN, WIN * WIN).transpose(0, 2, 1, 3)
    pairs = pairs.reshape(-1, WIN * WIN, 2 * WIN * WIN)
    return jnp.concatenate([pairs, pairs], axis=2)


def gather(mine):
    chip = run_stack(mine, *[swap(mine, "dp", 2 * j) for j in range(1, 4)])
    return chip, swap(chip, "dp", 1)


def on_device(
    tokens,
    video_flag,
    frame_count,
    norm_gain,
    norm_bias,
    w_qkv,
    w_proj,
    w_up,
    w_down,
    out_bias,
    up_bias,
    cotangent,
):
    items, frames, grid_rows, cols, feats = tokens.shape
    place = lax.rem(lax.axis_index("dp"), 8)
    row = lax.axis_index("rows")
    info = jnp.concatenate([jnp.stack([place, row]), video_flag, frame_count]).astype(jnp.int32)
    unpack_info = jnp.stack([lax.rem(place, 2), lax.div(place, 2)]).astype(jnp.int32)

    def column(*parts):
        flat = jnp.concatenate([p.reshape(-1) for p in parts])
        return jnp.broadcast_to(flat[:, None], (flat.shape[0], 128))

    halos = [shift(tokens[:1, :, :SHIFT], "rows", -1)]
    cot_halos = []
    mask = tile_mask(cols)
    state_vecs = column(
        *[v[n] for n in range(3) for v in (norm_gain, norm_bias, out_bias)], up_bias[0]
    )
    last_vecs = column(norm_gain[3], norm_bias[3], out_bias[3], up_bias[1])
    time_vecs = column(norm_gain[2])
    feed_vecs = column(norm_gain[1])
    space_vecs = column(norm_gain[0])
    wqkv_t, wproj_t, wup_t, wdown_t = [jnp.swapaxes(w, 1, 2) for w in (w_qkv, w_proj, w_up, w_down)]
    kept = ()
    for i in range(items):
        ahead = [cotangent[i : i + 1, :, :SHIFT]]
        if i + 1 < items:
            ahead.append(tokens[i + 1 : i + 2, :, :SHIFT])
        ahead = after(ahead, halos[i])
        cot_halos.append(shift(ahead[0], "rows", -1))
        if i + 1 < items:
            halos.append(shift(ahead[1], "rows", -1))
        kept = run_state(
            info, i, tokens, halos[i], mask, state_vecs, (wqkv_t, wproj_t, wup_t, wdown_t), kept
        )
    r1, r2, r3, qkv2, p2, stats, x3 = kept
    out_own, out_halo, g3, keep1, send1, sums1 = run_last(
        info, x3, cotangent, cot_halos, last_vecs, (wup_t, wdown_t, w_up, w_down)
    )

    def cells(array, *taken):
        return split_sum([array, *taken])[0]

    def halves(array):
        return array.reshape((2, 2) + array.shape[1:])

    out_back = shift(out_halo, "rows", 1)
    core1 = swap(send1, "dp", 1)
    g2, keept, sendt, sumst = run_time(
        info, g3, r1, qkv2, p2, stats, time_vecs, (w_qkv, w_proj), items
    )
    cells1 = cells(keep1, core1)
    layer_out = lax.dynamic_update_slice(out_own, out_back, (0,) * 5)
    (sendt,) = after([sendt], cells1[0], layer_out)

    across1 = [swap(cells1[j], "dp", 2 * j) for j in range(1, 4)]
    coret = swap(sendt, "dp", 1)
    g1, keep0, send0, sums0, mine1, layer_out = run_feed(
        info, g2, r3, stats, feed_vecs, (w_up, w_down), [cells1[0], layer_out]
    )
    rows1, cellst = split_sum([halves(mine1), *[halves(a) for a in across1]], [keept, coret])
    (send0,) = after([send0], rows1[0], cellst[0])

    along1 = swap(rows1[1], "rows", 2)
    acrosst = [swap(cellst[j], "dp", 2 * j) for j in range(1, 4)]
    core0 = swap(send0, "dp", 1)
    grad_own, back0, *accs, mine1, minet = run_space(
        info, 0, g1, r2, stats, space_vecs, (w_qkv, w_proj), tokens.shape, (), (),
        [rows1[0], cellst[0]],
    )
    rows1, rowst, cells0 = split_sum(
        [mine1, along1], [halves(minet), *[halves(a) for a in acrosst]], [keep0, core0]
    )
    (back0,) = after([back0], rows1[0], rowst[0], cells0[0])

    alongt = swap(rowst[1], "rows", 2)
    across0 = [swap(cells0[j], "dp", 2 * j) for j in range(1, 4)]
    backs = [shift(back0, "rows", 1)]
    grad_own, back1, keeps, sends, mine1, minet, mine0 = run_space(
        info, 1, g1, r2, stats, space_vecs, (w_qkv, w_proj), tokens.shape,
        accs + [grad_own], (sums1, sumst, sums0), [rows1[0], rowst[0], cells0[0]],
    )
    rowst, rows0 = split_sum([minet, alongt], [mine0, *across0])
    sends, back1, near1 = after([sends, back1, rows1[1]], rowst[0], rows0[0])

    cores = swap(sends, "dp", 1)
    along0 = [swap(rows0[z], "rows", z) for z in range(1, 4)]
    near1 = swap(near1, "rows", 1)
    neart = swap(rowst[1], "rows", 1)
    cellss = cells(keeps, cores)
    acrosss = [swap(cellss[j], "dp", 2 * j) for j in range(1, 4)]
    early = upper_bits(join_sum([mine1, near1], [rowst[0], neart]))
    early_chip, early_other = gather(early)
    rowss = cells(cellss[0], *acrosss)
    backs.append(shift(back1, "rows", 1))
    alongs = [swap(rowss[z], "rows", z) for z in range(1, 4)]
    outs = run_unpack(unpack_info, early_chip, early_other, ())
    grad_tokens = grad_own
    for i in range(items):
        grad_tokens = lax.dynamic_update_slice(grad_tokens, backs[i], (i, 0, 0, 0, 0))
    late = join_sum([rows0[0], *along0], [rowss[0], *alongs])
    late_chip, late_other = gather(upper_bits(late))
    up, down, qkv, proj, gain, bias, outb, upb = run_unpack(
        unpack_info, late_chip, late_other, outs
    )
    return layer_out, grad_tokens, gain, bias, qkv, proj, up, down, outb, upb


def solution(mesh):
    split = P("dp", None, "rows", None, None)
    in_specs = (split, P("dp"), P("dp")) + (P(),) * 8 + (split,)
    out_specs = (
        split,
        split,
        P(None, "rows"),
        P(None, "rows"),
        P(None, "rows", None),
        P(None, "rows", None),
        P(None, "rows", None),
        P(None, "rows", None),
        P(None, "rows"),
        P(None, "rows"),
    )
    return jax.shard_map(
        on_device, mesh=mesh, in_specs=in_specs, out_specs=out_specs, check_vma=False
    )
```

time: 563 us -> 402 us (0.71)
  waiting for transfers between devices: 178 us -> 46.3 us
  other arithmetic: 11.7 us -> 0.29 us
  starting transfers between devices: 56.1 us -> 46.9 us
  Pallas kernels: 275 us -> 266 us
    ppermute x40 -> x34, waiting for transfers between devices: 143 us -> 28.4 us  [swap(): lax.ppermute(block, axis, [(i, i ^ bits) for i in range(lax.axis_size(axi...]
    ppermute x4 -> x7, waiting for transfers between devices: 34.7 us -> 17.9 us  [shift(): lax.ppermute(block, axis, [(i, (i + distance) % size) for i in range(size)])]
    ppermute x40 -> x34, starting transfers between devices: 47.2 us -> 36.5 us  [swap(): lax.ppermute(block, axis, [(i, i ^ bits) for i in range(lax.axis_size(axi...]
    convert_element_type x6 -> x0, other arithmetic: 9.04 us -> none  [the longest x3 5.38 us: reduce_pieces(): parts = [add(keep[j], taken[j]).astype(BF16) for j in range(4)]]
    pallas_call x4 -> x25, Pallas kernels: 275 us -> 266 us  [the longest x2 71.4 us: run_state(): pl.pallas_call(functools.partial(state_kernel, item=item), grid_spec=pltp...]
    unnamed x53 -> x51, local copies, waits for them, and re-layouts: 19.7 us -> 22.7 us
  transfers between devices with their start and end apart: 44 -> 41, of which waited for: 21 -> 10; matrix products, arithmetic and copies ran while one was open for 7% -> 7% of each run, Pallas kernels for 0% -> 52%
where the time goes in v2:
time: 402 us; the launch traced here: 395 us
  Pallas kernels  266 us (66%)
  starting transfers between devices  46.9 us (12%)
  waiting for transfers between devices  46.3 us (12%)
  local copies, waits for them, and re-layouts  33.6 us (8%)
    pallas_call x2, Pallas kernels, run_state(): pl.pallas_call(functools.partial(state_kernel, item=item), grid_spec=pltp...  71.4 us
    pallas_call x1, Pallas kernels, run_last(): pl.pallas_call(lambda info, *refs: last_kernel(info, items, *refs), grid_...  52.9 us
    pallas_call x2, Pallas kernels, run_space(): pl.pallas_call(functools.partial(space_kernel, first=first, last=last, pa...  51 us
    pallas_call x1, Pallas kernels, run_time(): pl.pallas_call(time_kernel, grid_spec=pltpu.PrefetchScalarGridSpec(num_sc...  39.4 us
    pallas_call x1, Pallas kernels, run_feed(): pl.pallas_call(functools.partial(feed_kernel, passes=len(passes)), grid_s...  38.7 us
    ppermute x34, starting transfers between devices, swap(): lax.ppermute(block, axis, [(i, i ^ bits) for i in range(lax.axis_size(axi...  36.5 us
    ppermute x34, waiting for transfers between devices, swap(): lax.ppermute(block, axis, [(i, i ^ bits) for i in range(lax.axis_size(axi...  28.4 us
    unnamed x51, local copies, waits for them, and re-layouts  22.7 us
  transfers between devices with their start and end apart: 41, of which 10 were waited for; matrix products, arithmetic and copies ran while one was open for 7% of the time, Pallas kernels for 52%

profile of v2, /device:TPU:0, one launch (start us, length us, event | category | flops | bytes accessed | tf_op | source)
XLA Modules:
  0.0 395.0 jit_solution(3656493713057986640)
XLA Ops:
  0.7 2.5 fusion.3
  3.2 5.0 %collective-permute-start = (bf16[1,5,4,32,512]{4,3,2,1,0:T(8,128)(2,1)}, bf16[1,5,4,32,512]{4,3,2,1,0:T(8,128)(2,1)}, u32[]{:S(2)}, u32[]{:S(2)}) collective-permute-start(bf16[1,5,4,32,512]{4,3,2,1,0:T(8,128)(2,1)} %get-tuple-element.198), channel_id=1, source_target_pairs={{0,3},{1,0},{2,1},{3,2},{4,7},{5,4},{6,5},{7,6},{8,11},{9,8},{10,9... | collective-permute-start | bytes 1966088 | tf_op jit(solution)/shard_map/ppermute | solution.py:1081
  9.6 6.3 %copy.58 = bf16[2,512,2048]{1,2,0:T(8,128)(2,1)} copy(bf16[2,512,2048]{2,1,0:T(8,128)(2,1)} %wup_ref.1) | data formatting | bytes 8388608 | tf_op args[7]
  15.9 6.3 %copy.59 = bf16[2,2048,512]{1,2,0:T(8,128)(2,1)} copy(bf16[2,2048,512]{2,1,0:T(8,128)(2,1)} %wdown_ref.1) | data formatting | bytes 8388608 | tf_op args[8]
  22.1 3.2 copy.56
  25.3 2.3 copy.57
  27.7 1.5 fusion.2
  30.2 0.9 broadcast_in_dim.61.vec_ref
  31.2 35.8 %state.2 = (bf16[10,1536,256]{2,1,0:T(8,128)(2,1)}, bf16[10,3584,256]{2,1,0:T(8,128)(2,1)}, bf16[10,5120,256]{2,1,0:T(8,128)(2,1)}, bf16[10,1536,256]{2,1,0:T(8,...) custom-call(s32[6]{0:T(128)S(1)} %pad_add_fusion.info, ...), custom_call_target="tpu_custom_call" | custom-call | flops 22000001024 | bytes 50000000 | tf_op jit(solution)/shard_map/state/pallas_call | solution.py:745
  67.0 0.7 collective-permute-start.3
  67.7 35.6 %state.3 = (bf16[10,1536,256]{2,1,0:T(8,128)(2,1)}, bf16[10,3584,256]{2,1,0:T(8,128)(2,1)}, bf16[10,5120,256]{2,1,0:T(8,128)(2,1)}, bf16[10,1536,256]{2,1,0:T(8,...) custom-call(s32[6]{0:T(128)S(1)} %pad_add_fusion.info, ...), custom_call_target="tpu_custom_call", output_to_operand_aliasing={{0}: (9, {}), {1}: (10, {}), {2}: (11, {}), {3}: (12, {}), ... | custom-call | flops 22000001024 | bytes 50000000 | tf_op jit(solution)/shard_map/state/pallas_call | solution.py:745
  103.9 52.9 %last.1 = (bf16[2,5,8,32,512]{4,3,2,1,0:T(8,128)(2,1)}, bf16[2,5,4,32,512]{4,3,2,1,0:T(8,128)(2,1)S(1)}, f32[10,512,256]{2,1,0:T(8,128)}, bf16[4,4,128,512]{3,2,...) custom-call(s32[6]{0:T(128)S(1)} %pad_add_fusion.info, ...), custom_call_target="tpu_custom_call" | custom-call | flops 38400000000 | bytes 40000000 | tf_op jit(solution)/shard_map/last/pallas_call | solution.py:791
  156.8 1.8 collective-permute-start.5
  158.7 39.4 %time.1 = (f32[10,512,256]{2,1,0:T(8,128)S(1)}, bf16[4,4,64,512]{3,2,1,0:T(8,128)(2,1)S(1)}, bf16[4,4,64,512]{3,2,1,0:T(8,128)(2,1)S(1)}, f32[8,1536]{1,0:T(8,128)S(1)}) custom-call(s32[6]{0:T(128)S(1)} %pad_add_fusion.info, f32[10,512,256]{2,1,0:T(8,128)} %get-tuple-element.113.g3_ref, bf16[10,1536,256]{2,1,0:T(8,128)(2,1)} %get-tuple-element.114.r1_ref, ...), custom_call_target="tpu_custom_call" | custom-call | flops 30000001024 | bytes 40000000 | tf_op jit(solution)/shard_map/time/pallas_call | solution.py:838
  198.3 1.0 split_sum.6
  199.3 1.1 copy-done.10
  200.4 0.9 copy-done.5
  201.9 1.5 collective-permute-start.6
  203.4 1.5 collective-permute-start.7
  205.5 38.7 %feed.1 = (f32[10,512,256]{2,1,0:T(8,128)}, bf16[4,4,128,512]{3,2,1,0:T(8,128)(2,1)S(1)}, bf16[4,4,128,512]{3,2,1,0:T(8,128)(2,1)S(1)}, f32[8,3584]{1,0:T(8,128)...) custom-call(s32[6]{0:T(128)S(1)} %pad_add_fusion.info, ...), custom_call_target="tpu_custom_call", output_to_operand_aliasing={{4}: (7, {}), {5}: (8, {})} | custom-call | flops 30000001024 | bytes 40000000 | tf_op jit(solution)/shard_map/feed/pallas_call | solution.py:886
  244.2 1.0 split_sum.7
  245.4 1.6 collective-permute-start.11
  246.9 1.5 collective-permute-start.12
  248.9 2.5 collective-permute-start.10
  251.6 24.5 %space.2 = (bf16[2,5,8,32,512]{4,3,2,1,0:T(8,128)(2,1)}, bf16[1,5,4,32,512]{4,3,2,1,0:T(8,128)(2,1)}, f32[512,1536]{1,0:T(8,128)S(1)}, f32[512,512]{1,0:T(8,128)...) custom-call(s32[6]{0:T(128)S(1)} %pad_add_fusion.info, ...), custom_call_target="tpu_custom_call", output_to_operand_aliasing={{5}: (7, {}), {6}: (8, {})} | custom-call | flops 14000000000 | bytes 30000000 | tf_op jit(solution)/shard_map/space/pallas_call | solution.py:973
  276.1 1.4 split_sum.8
  277.5 1.6 collective-permute-start.17
  279.1 1.5 collective-permute-start.18
  281.5 2.5 copy-done.9
  283.9 26.5 %space.3 = (bf16[2,5,8,32,512]{4,3,2,1,0:T(8,128)(2,1)}, bf16[1,5,4,32,512]{4,3,2,1,0:T(8,128)(2,1)}, bf16[4,4,80,512]{3,2,1,0:T(8,128)(2,1)S(1)}, bf16[4,4,80,5...) custom-call(s32[6]{0:T(128)S(1)} %pad_add_fusion.info, ...), custom_call_target="tpu_custom_call", output_to_operand_aliasing={{0}: (10, {}), {4}: (14, {}), {5}: (15, {}), {6}: (16, {})} | custom-call | flops 14000000000 | bytes 30000000 | tf_op jit(solution)/shard_map/space/pallas_call | solution.py:973
  310.4 0.6 split_sum.9
  311.1 3.0 collective-permute-done.24.refs_1_
  314.1 0.7 split_sum.10
  314.8 1.6 collective-permute-start.25
  316.4 1.5 collective-permute-start.26
  318.4 1.5 collective-permute-start.21
  319.9 1.3 collective-permute-start.22
  321.2 4.3 %collective-permute-done.25.refs_1_ = bf16[4,80,512]{2,1,0:T(8,128)(2,1)S(1)} collective-permute-done((bf16[4,80,512]{2,1,0:T(8,128)(2,1)S(1)}, bf16[4,80,512]{2,1,0:T(8,128)(2,1)S(1)}, u32[]{:S(2)}, u32[]{:S(2)}) %collective-permute-start.25) | collective-permute-done | bytes 327712 | tf_op jit(solution)/shard_map/ppermute | solution.py:1085
  325.4 2.2 collective-permute-start.23
  327.7 5.2 %collective-permute-done.26.refs_2_ = bf16[4,80,512]{2,1,0:T(8,128)(2,1)S(1)} collective-permute-done((bf16[4,80,512]{2,1,0:T(8,128)(2,1)S(1)}, bf16[4,80,512]{2,1,0:T(8,128)(2,1)S(1)}, u32[]{:S(2)}, u32[]{:S(2)}) %collective-permute-start.26) | collective-permute-done | bytes 327712 | tf_op jit(solution)/shard_map/ppermute | solution.py:1085
  333.3 1.6 collective-permute-start.28
  334.9 1.3 collective-permute-start.29
  336.1 1.6 collective-permute-start.30
  337.7 0.9 collective-permute-done.28.refs_5_
  338.6 4.7 %collective-permute-done.29.refs_6_ = bf16[80,512]{1,0:T(8,128)(2,1)S(1)} collective-permute-done((bf16[80,512]{1,0:T(8,128)(2,1)S(1)}, bf16[80,512]{1,0:T(8,128)(2,1)S(1)}, u32[]{:S(2)}, u32[]{:S(2)}) %collective-permute-start.29) | collective-permute-done | bytes 81952 | tf_op jit(solution)/shard_map/ppermute | solution.py:1085
  343.4 1.5 collective-permute-start.31
  345.0 0.6 collective-permute-start.32
  345.5 1.4 collective-permute-start.35
  346.9 1.5 collective-permute-start.33
  348.4 0.6 collective-permute-start.36
  349.0 3.7 collective-permute-done.36.refs_3_
  352.7 1.5 collective-permute-start.37
  354.3 0.6 collective-permute-start.38
  354.8 1.5 collective-permute-start.39
  356.3 0.6 collective-permute-start.15
  357.0 3.2 collective-permute-done.37.refs_1_
  360.3 3.3 collective-permute-done.38.refs_2_
  363.7 1.4 collective-permute-start.20
  365.2 7.8 %collective-permute-done.15 = bf16[1,5,4,32,512]{4,3,2,1,0:T(8,128)(2,1)} collective-permute-done((bf16[1,5,4,32,512]{4,3,2,1,0:T(8,128)(2,1)}, bf16[1,5,4,32,512]{4,3,2,1,0:T(8,128)(2,1)}, u32[]{:S(2)}, u32[]{:S(2)}) %collective-permute-start.15) | collective-permute-done | bytes 655392 | tf_op jit(solution)/shard_map/ppermute | solution.py:1081
  373.1 2.0 constant_dynamic-update-slice_fusion.11
  375.1 10.0 %collective-permute-done.20 = bf16[1,5,4,32,512]{4,3,2,1,0:T(8,128)(2,1)} collective-permute-done((bf16[1,5,4,32,512]{4,3,2,1,0:T(8,128)(2,1)}, bf16[1,5,4,32,512]{4,3,2,1,0:T(8,128)(2,1)}, u32[]{:S(2)}, u32[]{:S(2)}) %collective-permute-start.20) | collective-permute-done | bytes 655392 | tf_op jit(solution)/shard_map/ppermute | solution.py:1081
  385.1 2.0 constant_dynamic-update-slice_fusion.10
  387.1 3.7 unpack.2
  390.8 3.8 unpack.3
  (130 shorter events, 7.2 us)
Async XLA Ops:
  0.6 7.9 %copy-start.14 = (f32[4,512]{1,0:T(4,128)S(1)}, f32[4,512]{1,0:T(4,128)}, u32[]{:S(2)}) copy-start(f32[4,512]{1,0:T(4,128)} %param.15) | copy-start | bytes 24580
  0.7 7.9 %copy-start.15 = (f32[4,512]{1,0:T(4,128)S(1)}, f32[4,512]{1,0:T(4,128)}, u32[]{:S(2)}) copy-start(f32[4,512]{1,0:T(4,128)} %param.16) | copy-start | bytes 24580
  0.7 7.9 %copy-start.16 = (f32[4,512]{1,0:T(4,128)S(1)}, f32[4,512]{1,0:T(4,128)}, u32[]{:S(2)}) copy-start(f32[4,512]{1,0:T(4,128)} %param.21) | copy-start | bytes 24580
  0.7 8.0 %copy-start.13 = (f32[2,2048]{1,0:T(2,128)S(1)}, f32[2,2048]{1,0:T(2,128)}, u32[]{:S(2)}) copy-start(f32[2,2048]{1,0:T(2,128)} %param.22) | copy-start | bytes 49156
  0.7 8.4 %copy-start.18 = (s32[2]{0:T(128)S(1)}, s32[2]{0:T(128)}, u32[]{:S(2)}) copy-start(s32[2]{0:T(128)} %param.13) | copy-start | bytes 28
  0.7 8.4 %copy-start.17 = (s32[2]{0:T(128)S(1)}, s32[2]{0:T(128)}, u32[]{:S(2)}) copy-start(s32[2]{0:T(128)} %param.14) | copy-start | bytes 28
  3.2 25.9 %collective-permute-start = (bf16[1,5,4,32,512]{4,3,2,1,0:T(8,128)(2,1)}, bf16[1,5,4,32,512]{4,3,2,1,0:T(8,128)(2,1)}, u32[]{:S(2)}, u32[]{:S(2)}) collective-permute-start(bf16[1,5,4,32,512]{4,3,2,1,0:T(8,128)(2,1)} %get-tuple-element.198), channel_id=1, source_target_pairs={{0,3},{1,0},{2,1},{3,2},{4,7},{5,4},{6,5},{7,6},{8,11},{9,8},{10,9... | collective-permute-start | bytes 1966088 | tf_op jit(solution)/shard_map/ppermute | solution.py:1081
  8.6 0.6 copy-start.11
  27.6 1.5 copy-start.6
  29.2 1.9 copy-start
  29.2 2.0 copy-start.1
  29.2 37.8 %collective-permute-start.1 = (bf16[1,5,4,32,512]{4,3,2,1,0:T(8,128)(2,1)S(1)}, bf16[1,5,4,32,512]{4,3,2,1,0:T(8,128)(2,1)S(1)}, u32[]{:S(2)}, u32[]{:S(2)}) collective-permute-start(bf16[1,5,4,32,512]{4,3,2,1,0:T(8,128)(2,1)S(1)} %get-tuple-element.103), channel_id=1, source_target_pairs={{0,3},{1,0},{2,1},{3,2},{4,7},{5,4},{6,5},{7,6},{8,11},{9,8},{10,9... | collective-permute-start | bytes 1966088 | tf_op jit(solution)/shard_map/ppermute | solution.py:1081
  29.7 73.6 %collective-permute-start.2 = (bf16[1,5,4,32,512]{4,3,2,1,0:T(8,128)(2,1)S(1)}, bf16[1,5,4,32,512]{4,3,2,1,0:T(8,128)(2,1)S(1)}, u32[]{:S(2)}, u32[]{:S(2)}) collective-permute-start(bf16[1,5,4,32,512]{4,3,2,1,0:T(8,128)(2,1)S(1)} %get-tuple-element.112), channel_id=1, source_target_pairs={{0,3},{1,0},{2,1},{3,2},{4,7},{5,4},{6,5},{7,6},{8,11},{9,8},{10,9... | collective-permute-start | bytes 1966088 | tf_op jit(solution)/shard_map/ppermute | solution.py:1081
  67.0 36.3 %collective-permute-start.3 = (bf16[1,5,4,32,512]{4,3,2,1,0:T(8,128)(2,1)S(1)}, bf16[1,5,4,32,512]{4,3,2,1,0:T(8,128)(2,1)S(1)}, u32[]{:S(2)}, u32[]{:S(2)}) collective-permute-start(bf16[1,5,4,32,512]{4,3,2,1,0:T(8,128)(2,1)S(1)} %after.7), channel_id=1, source_target_pairs={{0,3},{1,0},{2,1},{3,2},{4,7},{5,4},{6,5},{7,6},{8,11},{9,8},{10,9... | collective-permute-start | bytes 1966088 | tf_op jit(solution)/shard_map/ppermute | solution.py:1081
  103.8 54.8 %copy-start.3 = (bf16[2,512,1536]{2,1,0:T(8,128)(2,1)S(1)}, bf16[2,512,1536]{2,1,0:T(8,128)(2,1)}, u32[]{:S(2)}) copy-start(bf16[2,512,1536]{2,1,0:T(8,128)(2,1)} %wqkv_ref.5) | copy-start | bytes 9437188
  103.8 54.8 %copy-start.7 = (bf16[2,512,512]{2,1,0:T(8,128)(2,1)S(1)}, bf16[2,512,512]{2,1,0:T(8,128)(2,1)}, u32[]{:S(2)}) copy-start(bf16[2,512,512]{2,1,0:T(8,128)(2,1)} %wproj_ref.5) | copy-start | bytes 3145732
  156.8 41.4 %collective-permute-start.5 = (bf16[2,5,4,32,512]{4,3,2,1,0:T(8,128)(2,1)S(1)}, bf16[2,5,4,32,512]{4,3,2,1,0:T(8,128)(2,1)S(1)}, u32[]{:S(2)}, u32[]{:S(2)}) collective-permute-start(bf16[2,5,4,32,512]{4,3,2,1,0:T(8,128)(2,1)S(1)} %get-tuple-element.124), channel_id=1, source_target_pairs={{0,1},{1,2},{2,3},{3,0},{4,5},{5,6},{6,7},{7,4},{8,9},{9,10},{10,1... | collective-permute-start | bytes 3932168 | tf_op jit(solution)/shard_map/ppermute | solution.py:1081
  158.5 39.8 %collective-permute-start.4 = (bf16[4,4,128,512]{3,2,1,0:T(8,128)(2,1)S(1)}, bf16[4,4,128,512]{3,2,1,0:T(8,128)(2,1)S(1)}, u32[]{:S(2)}, u32[]{:S(2)}) collective-permute-start(bf16[4,4,128,512]{3,2,1,0:T(8,128)(2,1)S(1)} %get-tuple-element.121), channel_id=1, source_target_pairs={{0,4},{4,0},{8,12},{12,8},{16,20},{20,16},{24,28},{28,24},{1,5},{5... | collective-permute-start | bytes 6291464 | tf_op jit(solution)/shard_map/ppermute | solution.py:1085
  158.7 39.5 %copy-start.4 = (bf16[2,5,8,32,512]{4,3,2,1,0:T(8,128)(2,1)S(1)}, bf16[2,5,8,32,512]{4,3,2,1,0:T(8,128)(2,1)}, u32[]{:S(2)}) copy-start(bf16[2,5,8,32,512]{4,3,2,1,0:T(8,128)(2,1)} %get-tuple-element.123) | copy-start | bytes 7864324
  198.1 2.3 copy-start.10
  198.3 3.1 copy-start.5
  200.4 5.1 %copy-start.2 = (bf16[2,512,2048]{2,1,0:T(8,128)(2,1)S(1)}, bf16[2,512,2048]{2,1,0:T(8,128)(2,1)}, u32[]{:S(2)}) copy-start(bf16[2,512,2048]{2,1,0:T(8,128)(2,1)} %wup_ref.1) | copy-start | bytes 12582916
  201.4 42.8 %collective-permute-start.9 = (bf16[4,4,64,512]{3,2,1,0:T(8,128)(2,1)S(1)}, bf16[4,4,64,512]{3,2,1,0:T(8,128)(2,1)S(1)}, u32[]{:S(2)}, u32[]{:S(2)}) collective-permute-start(bf16[4,4,64,512]{3,2,1,0:T(8,128)(2,1)S(1)} %after.8), channel_id=1, source_target_pairs={{0,4},{4,0},{8,12},{12,8},{16,20},{20,16},{24,28},{28,24},{1,5},{5... | collective-permute-start | bytes 3145736 | tf_op jit(solution)/shard_map/ppermute | solution.py:1085
  201.9 42.3 %collective-permute-start.6 = (bf16[4,128,512]{2,1,0:T(8,128)(2,1)S(1)}, bf16[4,128,512]{2,1,0:T(8,128)(2,1)S(1)}, u32[]{:S(2)}, u32[]{:S(2)}) collective-permute-start(bf16[4,128,512]{2,1,0:T(8,128)(2,1)S(1)} %get-tuple-element.129), channel_id=1, source_target_pairs={{0,8},{4,12},{8,0},{12,4},{16,24},{20,28},{24,16},{28,20},{1,9},{5... | collective-permute-start | bytes 1572872 | tf_op jit(solution)/shard_map/ppermute | solution.py:1085
  203.4 40.8 %collective-permute-start.7 = (bf16[4,128,512]{2,1,0:T(8,128)(2,1)S(1)}, bf16[4,128,512]{2,1,0:T(8,128)(2,1)S(1)}, u32[]{:S(2)}, u32[]{:S(2)}) collective-permute-start(bf16[4,128,512]{2,1,0:T(8,128)(2,1)S(1)} %get-tuple-element.130), channel_id=1, source_target_pairs={{0,16},{4,20},{8,24},{12,28},{16,0},{20,4},{24,8},{28,12},{1,17},{... | collective-permute-start | bytes 1572872 | tf_op jit(solution)/shard_map/ppermute | solution.py:1085
  204.9 39.3 %collective-permute-start.8 = (bf16[4,128,512]{2,1,0:T(8,128)(2,1)S(1)}, bf16[4,128,512]{2,1,0:T(8,128)(2,1)S(1)}, u32[]{:S(2)}, u32[]{:S(2)}) collective-permute-start(bf16[4,128,512]{2,1,0:T(8,128)(2,1)S(1)} %get-tuple-element.131), channel_id=1, source_target_pairs={{0,24},{4,28},{8,16},{12,20},{16,8},{20,12},{24,0},{28,4},{1,25},{... | collective-permute-start | bytes 1572872 | tf_op jit(solution)/shard_map/ppermute | solution.py:1085
  244.2 7.4 %copy-start.8 = (f32[10,512,256]{2,1,0:T(8,128)S(1)}, f32[10,512,256]{2,1,0:T(8,128)}, u32[]{:S(2)}) copy-start(f32[10,512,256]{2,1,0:T(8,128)} %get-tuple-element.126.g1_ref) | copy-start | bytes 15728644
  245.3 6.2 %copy-start.12 = (f32[1,512]{1,0:T(1,128)S(1)}, f32[1,512]{1,0:T(1,128)}, u32[]{:S(2)}) copy-start(f32[1,512]{1,0:T(1,128)} %copy-done.11) | copy-start | bytes 6148
  245.3 30.9 %collective-permute-start.14 = (bf16[4,4,128,512]{3,2,1,0:T(8,128)(2,1)S(1)}, bf16[4,4,128,512]{3,2,1,0:T(8,128)(2,1)S(1)}, u32[]{:S(2)}, u32[]{:S(2)}) collective-permute-start(bf16[4,4,128,512]{3,2,1,0:T(8,128)(2,1)S(1)} %after.9), channel_id=1, source_target_pairs={{0,4},{4,0},{8,12},{12,8},{16,20},{20,16},{24,28},{28,24},{1,5},{5... | collective-permute-start | bytes 6291464 | tf_op jit(solution)/shard_map/ppermute | solution.py:1085
  245.4 30.7 %collective-permute-start.11 = (bf16[4,64,512]{2,1,0:T(8,128)(2,1)S(1)}, bf16[4,64,512]{2,1,0:T(8,128)(2,1)S(1)}, u32[]{:S(2)}, u32[]{:S(2)}) collective-permute-start(bf16[4,64,512]{2,1,0:T(8,128)(2,1)S(1)} %get-tuple-element.146), channel_id=1, source_target_pairs={{0,8},{4,12},{8,0},{12,4},{16,24},{20,28},{24,16},{28,20},{1,9},{5... | collective-permute-start | bytes 786440 | tf_op jit(solution)/shard_map/ppermute | solution.py:1085
  246.9 29.2 %collective-permute-start.12 = (bf16[4,64,512]{2,1,0:T(8,128)(2,1)S(1)}, bf16[4,64,512]{2,1,0:T(8,128)(2,1)S(1)}, u32[]{:S(2)}, u32[]{:S(2)}) collective-permute-start(bf16[4,64,512]{2,1,0:T(8,128)(2,1)S(1)} %get-tuple-element.147), channel_id=1, source_target_pairs={{0,16},{4,20},{8,24},{12,28},{16,0},{20,4},{24,8},{28,12},{1,17},{... | collective-permute-start | bytes 786440 | tf_op jit(solution)/shard_map/ppermute | solution.py:1085
  248.4 27.7 %collective-permute-start.13 = (bf16[4,64,512]{2,1,0:T(8,128)(2,1)S(1)}, bf16[4,64,512]{2,1,0:T(8,128)(2,1)S(1)}, u32[]{:S(2)}, u32[]{:S(2)}) collective-permute-start(bf16[4,64,512]{2,1,0:T(8,128)(2,1)S(1)} %get-tuple-element.148), channel_id=1, source_target_pairs={{0,24},{4,28},{8,16},{12,20},{16,8},{20,12},{24,0},{28,4},{1,25},{... | collective-permute-start | bytes 786440 | tf_op jit(solution)/shard_map/ppermute | solution.py:1085
  248.9 27.2 %collective-permute-start.10 = (bf16[2,128,512]{2,1,0:T(8,128)(2,1)S(1)}, bf16[2,128,512]{2,1,0:T(8,128)(2,1)S(1)}, u32[]{:S(2)}, u32[]{:S(2)}) collective-permute-start(bf16[2,128,512]{2,1,0:T(8,128)(2,1)S(1)} %get-tuple-element.144), channel_id=1, source_target_pairs={{0,2},{1,3},{2,0},{3,1},{4,6},{5,7},{6,4},{7,5},{8,10},{9,11},{10,... | collective-permute-start | bytes 786440 | tf_op jit(solution)/shard_map/ppermute | solution.py:1085
  277.5 32.9 %collective-permute-start.17 = (bf16[4,128,512]{2,1,0:T(8,128)(2,1)S(1)}, bf16[4,128,512]{2,1,0:T(8,128)(2,1)S(1)}, u32[]{:S(2)}, u32[]{:S(2)}) collective-permute-start(bf16[4,128,512]{2,1,0:T(8,128)(2,1)S(1)} %get-tuple-element.162), channel_id=1, source_target_pairs={{0,8},{4,12},{8,0},{12,4},{16,24},{20,28},{24,16},{28,20},{1,9},{5... | collective-permute-start | bytes 1572872 | tf_op jit(solution)/shard_map/ppermute | solution.py:1085
  279.1 31.3 %collective-permute-start.18 = (bf16[4,128,512]{2,1,0:T(8,128)(2,1)S(1)}, bf16[4,128,512]{2,1,0:T(8,128)(2,1)S(1)}, u32[]{:S(2)}, u32[]{:S(2)}) collective-permute-start(bf16[4,128,512]{2,1,0:T(8,128)(2,1)S(1)} %get-tuple-element.163), channel_id=1, source_target_pairs={{0,16},{4,20},{8,24},{12,28},{16,0},{20,4},{24,8},{28,12},{1,17},{... | collective-permute-start | bytes 1572872 | tf_op jit(solution)/shard_map/ppermute | solution.py:1085
  280.6 29.8 %collective-permute-start.19 = (bf16[4,128,512]{2,1,0:T(8,128)(2,1)S(1)}, bf16[4,128,512]{2,1,0:T(8,128)(2,1)S(1)}, u32[]{:S(2)}, u32[]{:S(2)}) collective-permute-start(bf16[4,128,512]{2,1,0:T(8,128)(2,1)S(1)} %get-tuple-element.164), channel_id=1, source_target_pairs={{0,24},{4,28},{8,16},{12,20},{16,8},{20,12},{24,0},{28,4},{1,25},{... | collective-permute-start | bytes 1572872 | tf_op jit(solution)/shard_map/ppermute | solution.py:1085
  281.1 29.3 %collective-permute-start.16 = (bf16[2,64,512]{2,1,0:T(8,128)(2,1)S(1)}, bf16[2,64,512]{2,1,0:T(8,128)(2,1)S(1)}, u32[]{:S(2)}, u32[]{:S(2)}) collective-permute-start(bf16[2,64,512]{2,1,0:T(8,128)(2,1)S(1)} %get-tuple-element.160), channel_id=1, source_target_pairs={{0,2},{1,3},{2,0},{3,1},{4,6},{5,7},{6,4},{7,5},{8,10},{9,11},{10,... | collective-permute-start | bytes 393224 | tf_op jit(solution)/shard_map/ppermute | solution.py:1085
  281.5 2.5 copy-start.9
  311.0 3.1 collective-permute-start.24
  314.8 10.6 %collective-permute-start.25 = (bf16[4,80,512]{2,1,0:T(8,128)(2,1)S(1)}, bf16[4,80,512]{2,1,0:T(8,128)(2,1)S(1)}, u32[]{:S(2)}, u32[]{:S(2)}) collective-permute-start(bf16[4,80,512]{2,1,0:T(8,128)(2,1)S(1)} %get-tuple-element.174), channel_id=1, source_target_pairs={{0,8},{4,12},{8,0},{12,4},{16,24},{20,28},{24,16},{28,20},{1,9},{5... | collective-permute-start | bytes 983048 | tf_op jit(solution)/shard_map/ppermute | solution.py:1085
  316.4 16.5 %collective-permute-start.26 = (bf16[4,80,512]{2,1,0:T(8,128)(2,1)S(1)}, bf16[4,80,512]{2,1,0:T(8,128)(2,1)S(1)}, u32[]{:S(2)}, u32[]{:S(2)}) collective-permute-start(bf16[4,80,512]{2,1,0:T(8,128)(2,1)S(1)} %get-tuple-element.175), channel_id=1, source_target_pairs={{0,16},{4,20},{8,24},{12,28},{16,0},{20,4},{24,8},{28,12},{1,17},{... | collective-permute-start | bytes 983048 | tf_op jit(solution)/shard_map/ppermute | solution.py:1085
  317.9 15.0 %collective-permute-start.27 = (bf16[4,80,512]{2,1,0:T(8,128)(2,1)S(1)}, bf16[4,80,512]{2,1,0:T(8,128)(2,1)S(1)}, u32[]{:S(2)}, u32[]{:S(2)}) collective-permute-start(bf16[4,80,512]{2,1,0:T(8,128)(2,1)S(1)} %get-tuple-element.176), channel_id=1, source_target_pairs={{0,24},{4,28},{8,16},{12,20},{16,8},{20,12},{24,0},{28,4},{1,25},{... | collective-permute-start | bytes 983048 | tf_op jit(solution)/shard_map/ppermute | solution.py:1085
  318.4 17.8 %collective-permute-start.21 = (bf16[128,512]{1,0:T(8,128)(2,1)S(1)}, bf16[128,512]{1,0:T(8,128)(2,1)S(1)}, u32[]{:S(2)}, u32[]{:S(2)}) collective-permute-start(bf16[128,512]{1,0:T(8,128)(2,1)S(1)} %get-tuple-element.168), channel_id=1, source_target_pairs={{0,1},{1,0},{2,3},{3,2},{4,5},{5,4},{6,7},{7,6},{8,9},{9,8},{10,11... | collective-permute-start | bytes 393224 | tf_op jit(solution)/shard_map/ppermute | solution.py:1085
  319.9 17.8 %collective-permute-start.22 = (bf16[128,512]{1,0:T(8,128)(2,1)S(1)}, bf16[128,512]{1,0:T(8,128)(2,1)S(1)}, u32[]{:S(2)}, u32[]{:S(2)}) collective-permute-start(bf16[128,512]{1,0:T(8,128)(2,1)S(1)} %get-tuple-element.169), channel_id=1, source_target_pairs={{0,2},{1,3},{2,0},{3,1},{4,6},{5,7},{6,4},{7,5},{8,10},{9,11},{10,... | collective-permute-start | bytes 393224 | tf_op jit(solution)/shard_map/ppermute | solution.py:1085
  325.4 12.3 %collective-permute-start.23 = (bf16[128,512]{1,0:T(8,128)(2,1)S(1)}, bf16[128,512]{1,0:T(8,128)(2,1)S(1)}, u32[]{:S(2)}, u32[]{:S(2)}) collective-permute-start(bf16[128,512]{1,0:T(8,128)(2,1)S(1)} %get-tuple-element.170), channel_id=1, source_target_pairs={{0,3},{1,2},{2,1},{3,0},{4,7},{5,6},{6,5},{7,4},{8,11},{9,10},{10,... | collective-permute-start | bytes 393224 | tf_op jit(solution)/shard_map/ppermute | solution.py:1085
  333.3 5.3 %collective-permute-start.28 = (bf16[80,512]{1,0:T(8,128)(2,1)S(1)}, bf16[80,512]{1,0:T(8,128)(2,1)S(1)}, u32[]{:S(2)}, u32[]{:S(2)}) collective-permute-start(bf16[80,512]{1,0:T(8,128)(2,1)S(1)} %get-tuple-element.178), channel_id=1, source_target_pairs={{0,1},{1,0},{2,3},{3,2},{4,5},{5,4},{6,7},{7,6},{8,9},{9,8},{10,11... | collective-permute-start | bytes 245768 | tf_op jit(solution)/shard_map/ppermute | solution.py:1085
  334.9 8.4 %collective-permute-start.29 = (bf16[80,512]{1,0:T(8,128)(2,1)S(1)}, bf16[80,512]{1,0:T(8,128)(2,1)S(1)}, u32[]{:S(2)}, u32[]{:S(2)}) collective-permute-start(bf16[80,512]{1,0:T(8,128)(2,1)S(1)} %get-tuple-element.179), channel_id=1, source_target_pairs={{0,2},{1,3},{2,0},{3,1},{4,6},{5,7},{6,4},{7,5},{8,10},{9,11},{10,... | collective-permute-start | bytes 245768 | tf_op jit(solution)/shard_map/ppermute | solution.py:1085
  336.1 7.2 %collective-permute-start.30 = (bf16[80,512]{1,0:T(8,128)(2,1)S(1)}, bf16[80,512]{1,0:T(8,128)(2,1)S(1)}, u32[]{:S(2)}, u32[]{:S(2)}) collective-permute-start(bf16[80,512]{1,0:T(8,128)(2,1)S(1)} %get-tuple-element.180), channel_id=1, source_target_pairs={{0,3},{1,2},{2,1},{3,0},{4,7},{5,6},{6,5},{7,4},{8,11},{9,10},{10,... | collective-permute-start | bytes 245768 | tf_op jit(solution)/shard_map/ppermute | solution.py:1085
  343.4 11.4 %collective-permute-start.31 = (bf16[208,512]{1,0:T(8,128)(2,1)S(1)}, bf16[208,512]{1,0:T(8,128)(2,1)S(1)}, u32[]{:S(2)}, u32[]{:S(2)}) collective-permute-start(bf16[208,512]{1,0:T(8,128)(2,1)S(1)} %join_sum.2.refs_0_), channel_id=1, source_target_pairs={{0,8},{4,12},{8,0},{12,4},{16,24},{20,28},{24,16},{28,20},{1,9},{5... | collective-permute-start | bytes 638984 | tf_op jit(solution)/shard_map/ppermute | solution.py:1085
  345.0 11.3 %collective-permute-start.32 = (bf16[208,512]{1,0:T(8,128)(2,1)S(1)}, bf16[208,512]{1,0:T(8,128)(2,1)S(1)}, u32[]{:S(2)}, u32[]{:S(2)}) collective-permute-start(bf16[208,512]{1,0:T(8,128)(2,1)S(1)} %join_sum.2.refs_0_), channel_id=1, source_target_pairs={{0,16},{4,20},{8,24},{12,28},{16,0},{20,4},{24,8},{28,12},{1,17},{... | collective-permute-start | bytes 638984 | tf_op jit(solution)/shard_map/ppermute | solution.py:1085
  345.5 7.2 %collective-permute-start.35 = (bf16[128,512]{1,0:T(8,128)(2,1)S(1)}, bf16[128,512]{1,0:T(8,128)(2,1)S(1)}, u32[]{:S(2)}, u32[]{:S(2)}) collective-permute-start(bf16[128,512]{1,0:T(8,128)(2,1)S(1)} %get-tuple-element.182), channel_id=1, source_target_pairs={{0,1},{1,0},{2,3},{3,2},{4,5},{5,4},{6,7},{7,6},{8,9},{9,8},{10,11... | collective-permute-start | bytes 393224 | tf_op jit(solution)/shard_map/ppermute | solution.py:1085
  346.9 10.0 %collective-permute-start.33 = (bf16[208,512]{1,0:T(8,128)(2,1)S(1)}, bf16[208,512]{1,0:T(8,128)(2,1)S(1)}, u32[]{:S(2)}, u32[]{:S(2)}) collective-permute-start(bf16[208,512]{1,0:T(8,128)(2,1)S(1)} %join_sum.2.refs_0_), channel_id=1, source_target_pairs={{0,24},{4,28},{8,16},{12,20},{16,8},{20,12},{24,0},{28,4},{1,25},{... | collective-permute-start | bytes 638984 | tf_op jit(solution)/shard_map/ppermute | solution.py:1085
  348.4 4.3 %collective-permute-start.36 = (bf16[64,512]{1,0:T(8,128)(2,1)S(1)}, bf16[64,512]{1,0:T(8,128)(2,1)S(1)}, u32[]{:S(2)}, u32[]{:S(2)}) collective-permute-start(bf16[64,512]{1,0:T(8,128)(2,1)S(1)} %get-tuple-element.183), channel_id=1, source_target_pairs={{0,1},{1,0},{2,3},{3,2},{4,5},{5,4},{6,7},{7,6},{8,9},{9,8},{10,11... | collective-permute-start | bytes 196616 | tf_op jit(solution)/shard_map/ppermute | solution.py:1085
  352.7 7.5 %collective-permute-start.37 = (bf16[192,512]{1,0:T(8,128)(2,1)S(1)}, bf16[192,512]{1,0:T(8,128)(2,1)S(1)}, u32[]{:S(2)}, u32[]{:S(2)}) collective-permute-start(bf16[192,512]{1,0:T(8,128)(2,1)S(1)} %join_sum.3.refs_0_), channel_id=1, source_target_pairs={{0,8},{4,12},{8,0},{12,4},{16,24},{20,28},{24,16},{28,20},{1,9},{5... | collective-permute-start | bytes 589832 | tf_op jit(solution)/shard_map/ppermute | solution.py:1085
  354.3 9.3 %collective-permute-start.38 = (bf16[192,512]{1,0:T(8,128)(2,1)S(1)}, bf16[192,512]{1,0:T(8,128)(2,1)S(1)}, u32[]{:S(2)}, u32[]{:S(2)}) collective-permute-start(bf16[192,512]{1,0:T(8,128)(2,1)S(1)} %join_sum.3.refs_0_), channel_id=1, source_target_pairs={{0,16},{4,20},{8,24},{12,28},{16,0},{20,4},{24,8},{28,12},{1,17},{... | collective-permute-start | bytes 589832 | tf_op jit(solution)/shard_map/ppermute | solution.py:1085
  354.8 8.8 %collective-permute-start.39 = (bf16[192,512]{1,0:T(8,128)(2,1)S(1)}, bf16[192,512]{1,0:T(8,128)(2,1)S(1)}, u32[]{:S(2)}, u32[]{:S(2)}) collective-permute-start(bf16[192,512]{1,0:T(8,128)(2,1)S(1)} %join_sum.3.refs_0_), channel_id=1, source_target_pairs={{0,24},{4,28},{8,16},{12,20},{16,8},{20,12},{24,0},{28,4},{1,25},{... | collective-permute-start | bytes 589832 | tf_op jit(solution)/shard_map/ppermute | solution.py:1085
  356.3 16.8 %collective-permute-start.15 = (bf16[1,5,4,32,512]{4,3,2,1,0:T(8,128)(2,1)}, bf16[1,5,4,32,512]{4,3,2,1,0:T(8,128)(2,1)}, u32[]{:S(2)}, u32[]{:S(2)}) collective-permute-start(bf16[1,5,4,32,512]{4,3,2,1,0:T(8,128)(2,1)} %after.10), channel_id=1, source_target_pairs={{0,1},{1,2},{2,3},{3,0},{4,5},{5,6},{6,7},{7,4},{8,9},{9,10},{10,1... | collective-permute-start | bytes 1966088 | tf_op jit(solution)/shard_map/ppermute | solution.py:1081
  357.0 33.8 %collective-permute-start.34 = (bf16[4,208,512]{2,1,0:T(8,128)(2,1)S(1)}, bf16[4,208,512]{2,1,0:T(8,128)(2,1)S(1)}, u32[]{:S(2)}, u32[]{:S(2)}) collective-permute-start(bf16[4,208,512]{2,1,0:T(8,128)(2,1)S(1)} %stack.22.mine_ref), channel_id=1, source_target_pairs={{0,4},{4,0},{8,12},{12,8},{16,20},{20,16},{24,28},{28,24},{1,5},{5... | collective-permute-start | bytes 2555912 | tf_op jit(solution)/shard_map/ppermute | solution.py:1085
  363.7 23.4 %collective-permute-start.40 = (bf16[4,192,512]{2,1,0:T(8,128)(2,1)S(1)}, bf16[4,192,512]{2,1,0:T(8,128)(2,1)S(1)}, u32[]{:S(2)}, u32[]{:S(2)}) collective-permute-start(bf16[4,192,512]{2,1,0:T(8,128)(2,1)S(1)} %stack.23.mine_ref), channel_id=1, source_target_pairs={{0,4},{4,0},{8,12},{12,8},{16,20},{20,16},{24,28},{28,24},{1,5},{5... | collective-permute-start | bytes 2359304 | tf_op jit(solution)/shard_map/ppermute | solution.py:1085
  363.7 21.3 %collective-permute-start.20 = (bf16[1,5,4,32,512]{4,3,2,1,0:T(8,128)(2,1)}, bf16[1,5,4,32,512]{4,3,2,1,0:T(8,128)(2,1)}, u32[]{:S(2)}, u32[]{:S(2)}) collective-permute-start(bf16[1,5,4,32,512]{4,3,2,1,0:T(8,128)(2,1)} %get-tuple-element.167), channel_id=1, source_target_pairs={{0,1},{1,2},{2,3},{3,0},{4,5},{5,6},{6,7},{7,4},{8,9},{9,10},{10,1... | collective-permute-start | bytes 1966088 | tf_op jit(solution)/shard_map/ppermute | solution.py:1081
